TPU v7x, 32 devices: a whole 2x2x4 slice. The times are simulated.
32 devices in a mesh: fsdp: 4 (over y, core), dp: 8 (over z, x).
Axes of the slice: x: 2, y: 2, z: 4, core: 2. Of those that a mesh axis runs over, the one named last changes fastest.
Arguments:
- inputs: bfloat16 [64, 128, 1024], P(('fsdp', 'dp')), may hold values from -12 to 12
- memory: bfloat16 [64, 2048, 1024], P(('fsdp', 'dp')), may hold values from -12 to 12
- lengths: int32 [64], P(('fsdp', 'dp')), may hold values from 64 to 128, as said below
- cotangent: bfloat16 [64, 128, 1024], P(('fsdp', 'dp')), may hold values from -6 to 6
- causal_query: bfloat16 [1024, 1024], P(('fsdp', 'dp')), may hold values from -0.046875 to 0.046875
- causal_key: bfloat16 [1024, 512], P(('fsdp', 'dp')), may hold values from -0.1875 to 0.1875
- causal_value: bfloat16 [1024, 512], P(('fsdp', 'dp')), may hold values from -0.1875 to 0.1875
- causal_out: bfloat16 [1024, 1024], P(('fsdp', 'dp')), may hold values from -0.75 to 0.75
- cross_query: bfloat16 [1024, 1024], P(('fsdp', 'dp')), may hold values from -0.046875 to 0.046875
- cross_key: bfloat16 [1024, 512], P(('fsdp', 'dp')), may hold values from -0.1875 to 0.1875
- cross_value: bfloat16 [1024, 512], P(('fsdp', 'dp')), may hold values from -0.1875 to 0.1875
- cross_out: bfloat16 [1024, 1024], P(('fsdp', 'dp')), may hold values from -1.5 to 1.5
- feed_gate: bfloat16 [1024, 2816], P(('fsdp', 'dp')), may hold values from -0.1875 to 0.1875
- feed_up: bfloat16 [1024, 2816], P(('fsdp', 'dp')), may hold values from -0.1875 to 0.1875
- feed_down: bfloat16 [2816, 1024], P(('fsdp', 'dp')), may hold values from -0.109375 to 0.109375
- gain_causal: bfloat16 [1024], P(('fsdp', 'dp')), may hold values from 0.099609375 to 1.8984375
- gain_cross: bfloat16 [1024], P(('fsdp', 'dp')), may hold values from 0.099609375 to 1.8984375
- gain_feed: bfloat16 [1024], P(('fsdp', 'dp')), may hold values from 0.099609375 to 1.8984375
- bias_table: bfloat16 [512], P(('fsdp', 'dp')), may hold values from -4 to 4
Outputs:
- layer_out: bfloat16 [64, 128, 1024], P(('fsdp', 'dp'))
- input_grad: bfloat16 [64, 128, 1024], P(('fsdp', 'dp'))
- memory_grad: bfloat16 [64, 2048, 1024], P(('fsdp', 'dp'))
- grad_causal_query: float32 [1024, 1024], P(('fsdp', 'dp'))
- grad_causal_key: float32 [1024, 512], P(('fsdp', 'dp'))
- grad_causal_value: float32 [1024, 512], P(('fsdp', 'dp'))
- grad_causal_out: float32 [1024, 1024], P(('fsdp', 'dp'))
- grad_cross_query: float32 [1024, 1024], P(('fsdp', 'dp'))
- grad_cross_key: float32 [1024, 512], P(('fsdp', 'dp'))
- grad_cross_value: float32 [1024, 512], P(('fsdp', 'dp'))
- grad_cross_out: float32 [1024, 1024], P(('fsdp', 'dp'))
- grad_feed_gate: float32 [1024, 2816], P(('fsdp', 'dp'))
- grad_feed_up: float32 [1024, 2816], P(('fsdp', 'dp'))
- grad_feed_down: float32 [2816, 1024], P(('fsdp', 'dp'))
- grad_gain_causal: float32 [1024], P(('fsdp', 'dp'))
- grad_gain_cross: float32 [1024], P(('fsdp', 'dp'))
- grad_gain_feed: float32 [1024], P(('fsdp', 'dp'))
- grad_bias_table: float32 [512], P(('fsdp', 'dp'))
Inputs may be any that keep to these rules, and one draw needn't show every extreme that they name: lengths[b] is how many leading target tokens of summary b may serve as keys; some summary has 128 and some 128 // 2.
All inputs are finite; a program needn't handle non-finite values.
Results may differ from a plain program's by a relative error of at most 0.025.
The roundings to bfloat16 on the way count: a program that leaves them out, or rounds other values in their place, can miss the bound.
Values may be sent and summed in bfloat16 or wider, within the bound.
No kernel may reach another device: no remote copies, remote signals or barrier semaphores. Data moves between devices by JAX's collectives and lax.ppermute only.
A program may use at most 192 MiB of HBM per device.

v0:
```python
import jax
import jax.numpy as jnp
import numpy as np
from jax import lax
from jax.sharding import PartitionSpec as P

HEADS = 16
HD = 64
BUCKETS = 32
KVH = 8


norm_eps = 1e-06
masked_score = -1000000000.0
bucket_reach = 128
highest = lax.Precision.HIGHEST


def bucket_onehot(length):
    query_pos = np.arange(length)[:, None]
    key_pos = np.arange(length)[None, :]
    distance = np.maximum(query_pos - key_pos, 0)
    exact_count = BUCKETS // 2
    spread = (
        np.log(np.maximum(distance, 1) / exact_count)
        / np.log(bucket_reach / exact_count)
        * (BUCKETS - exact_count)
    )
    far_bucket = np.minimum(exact_count + np.floor(spread).astype(np.int64), BUCKETS - 1)
    bucket_id = np.where(distance < exact_count, distance, far_bucket)
    return jnp.asarray(bucket_id[None] == np.arange(BUCKETS)[:, None, None]).astype(jnp.float32)


def norm_scale(stream):
    return lax.rsqrt(jnp.mean(stream * stream, axis=-1, keepdims=True) + norm_eps)


def norm_apply(stream, scale, gain):
    return (stream * scale * gain.astype(jnp.float32)).astype(jnp.bfloat16)


def norm_back(grad_normed, stream, scale, gain):
    scaled = grad_normed * gain.astype(jnp.float32)
    inner_mean = jnp.mean(scaled * stream, axis=-1, keepdims=True)
    grad_stream = scale * scaled - stream * (scale * scale * scale) * inner_mean
    grad_gain = jnp.sum(grad_normed * stream * scale, axis=(0, 1))
    return (grad_stream, grad_gain)


def block_scores(queries, keyval, added, key_valid):
    seq_count, row_count, packed = queries.shape
    queries = queries.reshape(seq_count, row_count, packed // HD, HD)
    scores = jnp.einsum(
        "blre,bse->blrs", queries, keyval[:, :, :HD], preferred_element_type=jnp.float32
    )
    if added is not None:
        scores = scores + added[None]
    if key_valid is not None:
        scores = jnp.where(key_valid[:, :, None, :], scores, masked_score)
    return scores


def block_forward(queries, keyval, added, key_valid):
    seq_count, row_count, packed = queries.shape
    scores = block_scores(queries, keyval, added, key_valid)
    row_max = jnp.max(scores, axis=-1, keepdims=True)
    logsum = row_max + jnp.log(jnp.sum(jnp.exp(scores - row_max), axis=-1, keepdims=True))
    softmax_out = jnp.exp(scores - logsum).astype(jnp.bfloat16)
    mixed_all = jnp.einsum(
        "blrs,bse->blre", softmax_out, keyval[:, :, HD:], preferred_element_type=jnp.float32
    )
    return (mixed_all.reshape(seq_count, row_count, packed).astype(jnp.bfloat16), logsum[..., 0])


def block_backward(queries, keyval, added, key_valid, grad_mixed, logsum):
    seq_count, row_count, packed = queries.shape
    group_ratio = packed // HD
    scores = block_scores(queries, keyval, added, key_valid)
    softmax_out = jnp.exp(scores - logsum[..., None])
    grad_heads = grad_mixed.reshape(seq_count, row_count, group_ratio, HD)
    grad_soft = jnp.einsum(
        "blre,bse->blrs", grad_heads, keyval[:, :, HD:], preferred_element_type=jnp.float32
    )
    grad_scores = (
        softmax_out * (grad_soft - jnp.sum(softmax_out * grad_soft, axis=-1, keepdims=True))
    ).astype(jnp.bfloat16)
    grad_query = jnp.einsum(
        "blrs,bse->blre", grad_scores, keyval[:, :, :HD], preferred_element_type=jnp.float32
    )
    grad_keys = jnp.einsum(
        "blrs,blre->bse",
        grad_scores,
        queries.reshape(seq_count, row_count, group_ratio, HD),
        preferred_element_type=jnp.float32,
    )
    grad_values = jnp.einsum(
        "blrs,blre->bse",
        softmax_out.astype(jnp.bfloat16),
        grad_heads,
        preferred_element_type=jnp.float32,
    )
    grad_keyval = jnp.concatenate([grad_keys, grad_values], axis=-1).astype(jnp.bfloat16)
    grad_added = jnp.sum(grad_scores.astype(jnp.float32), axis=0)
    return (
        grad_query.reshape(seq_count, row_count, packed).astype(jnp.bfloat16),
        grad_keyval,
        grad_added,
    )


def project_heads(normed, source, w_query, w_key, w_value):
    model_width = normed.shape[-1]
    packed = HEADS // KVH * HD
    query_all = jnp.einsum(
        "bld,dgk->gblk",
        normed,
        w_query.reshape(model_width, KVH, packed),
        preferred_element_type=jnp.float32,
    ).astype(jnp.bfloat16)
    w_keyval = jnp.concatenate(
        [w_key.reshape(model_width, KVH, HD), w_value.reshape(model_width, KVH, HD)], axis=2
    )
    keyval_all = jnp.einsum(
        "bsd,dgk->gbsk", source, w_keyval, preferred_element_type=jnp.float32
    ).astype(jnp.bfloat16)
    return (query_all, keyval_all)


def attention_forward(query_all, keyval_all, added_all, key_valid):
    if added_all is None:
        return lax.map(
            lambda block_items: block_forward(block_items[0], block_items[1], None, None),
            (query_all, keyval_all),
        )
    return lax.map(
        lambda block_items: block_forward(
            block_items[0], block_items[1], block_items[2], key_valid
        ),
        (query_all, keyval_all, added_all),
    )


def out_project(mixed_all, w_out):
    model_width = w_out.shape[1]
    return jnp.einsum(
        "gblk,gkd->bld",
        mixed_all,
        w_out.reshape(KVH, HEADS // KVH * HD, model_width),
        preferred_element_type=jnp.float32,
    )


def attention_backward(
    grad_stream,
    normed,
    source,
    mixed_all,
    logsum_all,
    query_all,
    keyval_all,
    added_all,
    key_valid,
    w_query,
    w_key,
    w_value,
    w_out,
):
    model_width = normed.shape[-1]
    packed = HEADS // KVH * HD
    grad_branch = grad_stream.astype(jnp.bfloat16)
    grad_out_w = jnp.einsum(
        "gblk,bld->gkd", mixed_all, grad_branch, preferred_element_type=jnp.float32
    ).reshape(KVH * packed, model_width)
    grad_mixed = jnp.einsum(
        "bld,gkd->gblk",
        grad_branch,
        w_out.reshape(KVH, packed, model_width),
        preferred_element_type=jnp.float32,
    ).astype(jnp.bfloat16)
    if added_all is None:
        grad_query, grad_keyval, grad_added = lax.map(
            lambda block_items: block_backward(
                block_items[0], block_items[1], None, None, block_items[2], block_items[3]
            ),
            (query_all, keyval_all, grad_mixed, logsum_all),
        )
    else:
        grad_query, grad_keyval, grad_added = lax.map(
            lambda block_items: block_backward(
                block_items[0],
                block_items[1],
                block_items[2],
                key_valid,
                block_items[3],
                block_items[4],
            ),
            (query_all, keyval_all, added_all, grad_mixed, logsum_all),
        )
    w_keyval = jnp.concatenate(
        [w_key.reshape(model_width, KVH, HD), w_value.reshape(model_width, KVH, HD)], axis=2
    )
    grad_query_w = jnp.einsum(
        "bld,gblk->dgk", normed, grad_query, preferred_element_type=jnp.float32
    ).reshape(model_width, KVH * packed)
    grad_keyval_w = jnp.einsum(
        "bsd,gbsk->dgk", source, grad_keyval, preferred_element_type=jnp.float32
    )
    grad_key_w = grad_keyval_w[:, :, :HD].reshape(model_width, KVH * HD)
    grad_value_w = grad_keyval_w[:, :, HD:].reshape(model_width, KVH * HD)
    grad_normed = jnp.einsum(
        "gblk,dgk->bld",
        grad_query,
        w_query.reshape(model_width, KVH, packed),
        preferred_element_type=jnp.float32,
    )
    grad_source = jnp.einsum(
        "gbsk,dgk->bsd", grad_keyval, w_keyval, preferred_element_type=jnp.float32
    )
    return (
        grad_normed,
        grad_source,
        grad_query_w,
        grad_key_w,
        grad_value_w,
        grad_out_w,
        grad_added,
    )


def local(
    inputs,
    memory,
    lengths,
    cotangent,
    causal_query,
    causal_key,
    causal_value,
    causal_out,
    cross_query,
    cross_key,
    cross_value,
    cross_out,
    feed_gate,
    feed_up,
    feed_down,
    gain_causal,
    gain_cross,
    gain_feed,
    bias_table,
):
    seq_count, length, model_width = inputs.shape
    group_ratio = HEADS // KVH
    stream = inputs.astype(jnp.float32)
    onehot = bucket_onehot(length)
    positions = jnp.arange(length, dtype=jnp.int32)
    key_valid = (positions[None, None, :] <= positions[None, :, None]) & (
        positions[None, None, :] < lengths[:, None, None]
    )
    q_one, k_one, v_one, o_one, gain_one, bias_rows = (
        lax.all_gather(causal_query, ("fsdp", "dp"), axis=0, tiled=True),
        lax.all_gather(causal_key, ("fsdp", "dp"), axis=0, tiled=True),
        lax.all_gather(causal_value, ("fsdp", "dp"), axis=0, tiled=True),
        lax.all_gather(causal_out, ("fsdp", "dp"), axis=0, tiled=True),
        lax.all_gather(gain_causal, ("fsdp", "dp"), axis=0, tiled=True),
        lax.all_gather(bias_table, ("fsdp", "dp"), axis=0, tiled=True),
    )
    bias_full = jnp.einsum(
        "hc,cij->hij",
        bias_rows.astype(jnp.float32).reshape(HEADS, BUCKETS),
        onehot,
        precision=highest,
    )
    added_all = bias_full.reshape(KVH, group_ratio, length, length).transpose(0, 2, 1, 3)
    scale_one = norm_scale(stream)
    normed_one = norm_apply(stream, scale_one, gain_one)
    query_one, keyval_one = project_heads(normed_one, normed_one, q_one, k_one, v_one)
    mixed_one, logsum_one = attention_forward(query_one, keyval_one, added_all, key_valid)
    after_causal = stream + out_project(mixed_one, o_one)
    q_two, k_two, v_two, o_two, gain_two = (
        lax.all_gather(cross_query, ("fsdp", "dp"), axis=0, tiled=True),
        lax.all_gather(cross_key, ("fsdp", "dp"), axis=0, tiled=True),
        lax.all_gather(cross_value, ("fsdp", "dp"), axis=0, tiled=True),
        lax.all_gather(cross_out, ("fsdp", "dp"), axis=0, tiled=True),
        lax.all_gather(gain_cross, ("fsdp", "dp"), axis=0, tiled=True),
    )
    scale_two = norm_scale(after_causal)
    normed_two = norm_apply(after_causal, scale_two, gain_two)
    query_two, keyval_two = project_heads(normed_two, memory, q_two, k_two, v_two)
    mixed_two, logsum_two = attention_forward(query_two, keyval_two, None, None)
    after_cross = after_causal + out_project(mixed_two, o_two)
    w_gate, w_up, w_down, gain_three = (
        lax.all_gather(feed_gate, ("fsdp", "dp"), axis=0, tiled=True),
        lax.all_gather(feed_up, ("fsdp", "dp"), axis=0, tiled=True),
        lax.all_gather(feed_down, ("fsdp", "dp"), axis=0, tiled=True),
        lax.all_gather(gain_feed, ("fsdp", "dp"), axis=0, tiled=True),
    )
    scale_three = norm_scale(after_cross)
    normed_three = norm_apply(after_cross, scale_three, gain_three)
    gate_pre = jnp.einsum("bld,df->blf", normed_three, w_gate, preferred_element_type=jnp.float32)
    up_pre = jnp.einsum("bld,df->blf", normed_three, w_up, preferred_element_type=jnp.float32)
    gelu_value, gelu_pull = jax.vjp(
        lambda pre_act: jax.nn.gelu(pre_act, approximate=True), gate_pre
    )
    hidden = (gelu_value * up_pre).astype(jnp.bfloat16)
    layer_out = (
        after_cross + jnp.einsum("blf,fd->bld", hidden, w_down, preferred_element_type=jnp.float32)
    ).astype(jnp.bfloat16)
    w_gate, w_up, w_down, gain_three = (
        lax.all_gather(feed_gate, ("fsdp", "dp"), axis=0, tiled=True),
        lax.all_gather(feed_up, ("fsdp", "dp"), axis=0, tiled=True),
        lax.all_gather(feed_down, ("fsdp", "dp"), axis=0, tiled=True),
        lax.all_gather(gain_feed, ("fsdp", "dp"), axis=0, tiled=True),
    )
    grad_down_w = jnp.einsum("blf,bld->fd", hidden, cotangent, preferred_element_type=jnp.float32)
    grad_hidden = jnp.einsum("bld,fd->blf", cotangent, w_down, preferred_element_type=jnp.float32)
    grad_gate = gelu_pull(grad_hidden * up_pre)[0].astype(jnp.bfloat16)
    grad_up = (grad_hidden * gelu_value).astype(jnp.bfloat16)
    grad_gate_w = jnp.einsum(
        "bld,blf->df", normed_three, grad_gate, preferred_element_type=jnp.float32
    )
    grad_up_w = jnp.einsum("bld,blf->df", normed_three, grad_up, preferred_element_type=jnp.float32)
    grad_normed = jnp.einsum(
        "blf,df->bld", grad_gate, w_gate, preferred_element_type=jnp.float32
    ) + jnp.einsum("blf,df->bld", grad_up, w_up, preferred_element_type=jnp.float32)
    grad_rows, grad_gain_three = norm_back(grad_normed, after_cross, scale_three, gain_three)
    grad_after_cross = cotangent.astype(jnp.float32) + grad_rows
    feed_sums = (
        lax.psum_scatter(grad_gate_w, ("fsdp", "dp"), scatter_dimension=0, tiled=True),
        lax.psum_scatter(grad_up_w, ("fsdp", "dp"), scatter_dimension=0, tiled=True),
        lax.psum_scatter(grad_down_w, ("fsdp", "dp"), scatter_dimension=0, tiled=True),
        lax.psum_scatter(grad_gain_three, ("fsdp", "dp"), scatter_dimension=0, tiled=True),
    )
    q_two, k_two, v_two, o_two, gain_two = (
        lax.all_gather(cross_query, ("fsdp", "dp"), axis=0, tiled=True),
        lax.all_gather(cross_key, ("fsdp", "dp"), axis=0, tiled=True),
        lax.all_gather(cross_value, ("fsdp", "dp"), axis=0, tiled=True),
        lax.all_gather(cross_out, ("fsdp", "dp"), axis=0, tiled=True),
        lax.all_gather(gain_cross, ("fsdp", "dp"), axis=0, tiled=True),
    )
    (
        grad_normed,
        memory_term,
        grad_query_two,
        grad_key_two,
        grad_value_two,
        grad_out_two,
        unused_added,
    ) = attention_backward(
        grad_after_cross,
        normed_two,
        memory,
        mixed_two,
        logsum_two,
        query_two,
        keyval_two,
        None,
        None,
        q_two,
        k_two,
        v_two,
        o_two,
    )
    memory_grad = memory_term.astype(jnp.bfloat16)
    grad_rows, grad_gain_two = norm_back(grad_normed, after_causal, scale_two, gain_two)
    grad_after_causal = grad_after_cross + grad_rows
    cross_sums = (
        lax.psum_scatter(grad_query_two, ("fsdp", "dp"), scatter_dimension=0, tiled=True),
        lax.psum_scatter(grad_key_two, ("fsdp", "dp"), scatter_dimension=0, tiled=True),
        lax.psum_scatter(grad_value_two, ("fsdp", "dp"), scatter_dimension=0, tiled=True),
        lax.psum_scatter(grad_out_two, ("fsdp", "dp"), scatter_dimension=0, tiled=True),
        lax.psum_scatter(grad_gain_two, ("fsdp", "dp"), scatter_dimension=0, tiled=True),
    )
    q_one, k_one, v_one, o_one, gain_one = (
        lax.all_gather(causal_query, ("fsdp", "dp"), axis=0, tiled=True),
        lax.all_gather(causal_key, ("fsdp", "dp"), axis=0, tiled=True),
        lax.all_gather(causal_value, ("fsdp", "dp"), axis=0, tiled=True),
        lax.all_gather(causal_out, ("fsdp", "dp"), axis=0, tiled=True),
        lax.all_gather(gain_causal, ("fsdp", "dp"), axis=0, tiled=True),
    )
    (
        grad_normed,
        source_term,
        grad_query_one,
        grad_key_one,
        grad_value_one,
        grad_out_one,
        grad_added,
    ) = attention_backward(
        grad_after_causal,
        normed_one,
        normed_one,
        mixed_one,
        logsum_one,
        query_one,
        keyval_one,
        added_all,
        key_valid,
        q_one,
        k_one,
        v_one,
        o_one,
    )
    grad_rows, grad_gain_one = norm_back(grad_normed + source_term, stream, scale_one, gain_one)
    input_grad = (grad_after_causal + grad_rows).astype(jnp.bfloat16)
    grad_bias_full = grad_added.transpose(0, 2, 1, 3).reshape(HEADS, length, length)
    grad_bias_rows = jnp.einsum("hij,cij->hc", grad_bias_full, onehot, precision=highest).reshape(
        HEADS * BUCKETS
    )
    causal_sums = (
        lax.psum_scatter(grad_query_one, ("fsdp", "dp"), scatter_dimension=0, tiled=True),
        lax.psum_scatter(grad_key_one, ("fsdp", "dp"), scatter_dimension=0, tiled=True),
        lax.psum_scatter(grad_value_one, ("fsdp", "dp"), scatter_dimension=0, tiled=True),
        lax.psum_scatter(grad_out_one, ("fsdp", "dp"), scatter_dimension=0, tiled=True),
        lax.psum_scatter(grad_gain_one, ("fsdp", "dp"), scatter_dimension=0, tiled=True),
        lax.psum_scatter(grad_bias_rows, ("fsdp", "dp"), scatter_dimension=0, tiled=True),
    )
    sum_query_one, sum_key_one, sum_value_one, sum_out_one, sum_gain_one, sum_bias_rows = (
        causal_sums
    )
    sum_query_two, sum_key_two, sum_value_two, sum_out_two, sum_gain_two = cross_sums
    sum_gate_w, sum_up_w, sum_down_w, sum_gain_three = feed_sums
    return (
        layer_out,
        input_grad,
        memory_grad,
        sum_query_one,
        sum_key_one,
        sum_value_one,
        sum_out_one,
        sum_query_two,
        sum_key_two,
        sum_value_two,
        sum_out_two,
        sum_gate_w,
        sum_up_w,
        sum_down_w,
        sum_gain_one,
        sum_gain_two,
        sum_gain_three,
        sum_bias_rows,
    )


def solution(mesh):
    in_specs = (
        P(("fsdp", "dp"), None, None),
        P(("fsdp", "dp"), None, None),
        P(("fsdp", "dp")),
        P(("fsdp", "dp"), None, None),
        P(("fsdp", "dp"), None),
        P(("fsdp", "dp"), None),
        P(("fsdp", "dp"), None),
        P(("fsdp", "dp"), None),
        P(("fsdp", "dp"), None),
        P(("fsdp", "dp"), None),
        P(("fsdp", "dp"), None),
        P(("fsdp", "dp"), None),
        P(("fsdp", "dp"), None),
        P(("fsdp", "dp"), None),
        P(("fsdp", "dp"), None),
        P(("fsdp", "dp")),
        P(("fsdp", "dp")),
        P(("fsdp", "dp")),
        P(("fsdp", "dp")),
    )
    out_specs = (
        P(("fsdp", "dp"), None, None),
        P(("fsdp", "dp"), None, None),
        P(("fsdp", "dp"), None, None),
        P(("fsdp", "dp"), None),
        P(("fsdp", "dp"), None),
        P(("fsdp", "dp"), None),
        P(("fsdp", "dp"), None),
        P(("fsdp", "dp"), None),
        P(("fsdp", "dp"), None),
        P(("fsdp", "dp"), None),
        P(("fsdp", "dp"), None),
        P(("fsdp", "dp"), None),
        P(("fsdp", "dp"), None),
        P(("fsdp", "dp"), None),
        P(("fsdp", "dp")),
        P(("fsdp", "dp")),
        P(("fsdp", "dp")),
        P(("fsdp", "dp")),
    )
    return jax.shard_map(local, mesh=mesh, in_specs=in_specs, out_specs=out_specs, check_vma=False)
```

profile of v0, /device:TPU:0, one launch (start us, length us, event | category | flops | bytes accessed | tf_op | source)
XLA Modules:
  0.0 2710.7 jit_solution(4828714981738198742)
XLA Ops:
  18.2 42.2 %all-reduce.9 = (bf16[1024]{0:T(1024)(128)(2,1)S(1)}, bf16[512]{0:T(512)(128)(2,1)S(1)}, bf16[1024]{0:T(1024)(128)(2,1)S(1)}, bf16[1024]{0:T(1024)(128)(2,1)S(1)}) all-reduce(bf16[1024]{0:T(1024)(128)(2,1)S(1)} %dynamic-update-slice, bf16[512]{0:T(512)(128)(2,1)S(1)} %dynamic-update-slice.1, ...), channel_id=1, replica_groups=mesh['fsdp'=4,'dp'=8] {'fsdp','dp'}, use_global_device_ids=true, to_apply=%add | all-reduce | flops 3584 | bytes 14336
  69.2 54.4 %all-gather.22.cloned.1.call-done = bf16[1024,512]{1,0:T(8,128)(2,1)} async-done(((bf16[32,512]{1,0:T(8,128)(2,1)}), bf16[1024,512]{1,0:T(8,128)(2,1)}) %all-gather.22.cloned.1.call-update) | async-done | bytes 1048592 | tf_op jit(solution)/shard_map/all_gather | solution.py:281
  125.1 14.9 convert_bitcast_fusion
  140.1 39.3 %all-gather.16.cloned.1.call-done = bf16[1024,512]{1,0:T(8,128)(2,1)} async-done(((bf16[32,512]{1,0:T(8,128)(2,1)}), bf16[1024,512]{1,0:T(8,128)(2,1)}) %all-gather.16.cloned.1.call-update) | async-done | bytes 1048592 | tf_op jit(solution)/shard_map/all_gather | solution.py:262
  180.9 54.1 %all-gather.14.cloned.1.call-done = bf16[1024,512]{1,0:T(8,128)(2,1)} async-done(((bf16[32,512]{1,0:T(8,128)(2,1)}), bf16[1024,512]{1,0:T(8,128)(2,1)}) %all-gather.14.cloned.1.call-update) | async-done | bytes 1048592 | tf_op jit(solution)/shard_map/all_gather | solution.py:261
  239.4 53.9 %all-gather.12.cloned.1.call-done = bf16[1024,1024]{1,0:T(8,128)(2,1)} async-done(((bf16[32,1024]{1,0:T(8,128)(2,1)}), bf16[1024,1024]{1,0:T(8,128)(2,1)}) %all-gather.12.cloned.1.call-update) | async-done | bytes 2097168 | tf_op jit(solution)/shard_map/all_gather | solution.py:260
  305.8 45.8 %all-gather.18.cloned.1.call-done = bf16[1024,1024]{1,0:T(8,128)(2,1)} async-done(((bf16[32,1024]{1,0:T(8,128)(2,1)}), bf16[1024,1024]{1,0:T(8,128)(2,1)}) %all-gather.18.cloned.1.call-update) | async-done | bytes 2097168 | tf_op jit(solution)/shard_map/all_gather | solution.py:263
  354.1 55.9 %all-gather.20.cloned.1.call-done = bf16[1024,1024]{1,0:T(8,128)(2,1)} async-done(((bf16[32,1024]{1,0:T(8,128)(2,1)}), bf16[1024,1024]{1,0:T(8,128)(2,1)}) %all-gather.20.cloned.1.call-update) | async-done | bytes 2097168 | tf_op jit(solution)/shard_map/all_gather | solution.py:280
  417.4 42.3 %while.52 = (s32[]{:T(128)}, bf16[8,2,128,128]{2,3,1,0:T(8,128)(2,1)}, f32[8,2,128,2]{2,3,1,0:T(2,128)S(1)}, bf16[8,2,128,128]{2,3,1,0:T(8,128)(2,1)}, bf16[8,2,2048,128]{2,3,1,0:T(8,128)(2,1)}, /*index=5*/s32[]{:T(128)}) while((s32[]{:T(128)}, bf16[8,2,128,128]{2,3,1,0:T(8,128)(2,1)}, f32[8,2,128,2]{2,3,1,0:T(2,128)S(1)}, ...), condition=%wide.region_9.10_spmd, body=%wide.region_6.9_spmd.sunk | while | flops 273710592 | bytes 16138333 | solution.py:131
  459.7 8.8 all-gather.26.cloned.1.call-done
  473.0 64.5 %all-gather.32.cloned.1.call-done = bf16[2816,1024]{1,0:T(8,128)(2,1)} async-done(((bf16[88,1024]{1,0:T(8,128)(2,1)}), bf16[2816,1024]{1,0:T(8,128)(2,1)}) %all-gather.32.cloned.1.call-update) | async-done | bytes 5767184 | tf_op jit(solution)/shard_map/all_gather | solution.py:294
  543.6 62.8 %all-gather.30.cloned.1.call-done = bf16[1024,2816]{1,0:T(8,128)(2,1)} async-done(((bf16[32,2816]{1,0:T(8,128)(2,1)}), bf16[1024,2816]{1,0:T(8,128)(2,1)}) %all-gather.30.cloned.1.call-update) | async-done | bytes 5767184 | tf_op jit(solution)/shard_map/all_gather | solution.py:293
  612.5 63.1 %all-gather.28.cloned.1.call-done = bf16[1024,2816]{1,0:T(8,128)(2,1)} async-done(((bf16[32,2816]{1,0:T(8,128)(2,1)}), bf16[1024,2816]{1,0:T(8,128)(2,1)}) %all-gather.28.cloned.1.call-update) | async-done | bytes 5767184 | tf_op jit(solution)/shard_map/all_gather | solution.py:292
  675.6 9.3 fusion.50
  695.3 72.5 %while.53 = (s32[]{:T(128)}, bf16[8,2,128,128]{2,3,1,0:T(8,128)(2,1)}, bf16[8,2,2048,128]{2,3,1,0:T(8,128)(2,1)}, bf16[8,2,128,128]{2,3,1,0:T(8,128)(2,1)}, bf16...) while((s32[]{:T(128)}, ...), condition=%wide.region_14.15_spmd, body=%wide.region_12.14_spmd.sunk | while | flops 681082368 | bytes 39135348 | solution.py:181
  774.0 48.8 %while.55 = (s32[]{:T(128)}, bf16[8,2,128,128]{2,3,1,0:T(8,128)(2,1)S(1)}, bf16[8,2,128,128]{2,3,1,0:T(8,128)(2,1)}, f32[8,128,2,128]{1,3,2,0:T(8,128)}, bf16[8,...) while((s32[]{:T(128)}, ...), condition=%wide.region_19.20_spmd.clone, body=%wide.region_16.19_spmd.clone.sunk | while | flops 42860032 | bytes 4123033 | solution.py:188
  833.1 12.7 fusion.51
  881.6 7.4 convolution_bitcast_fusion.6
  889.1 7.3 convolution_bitcast_fusion.5
  897.4 7.2 convolution_bitcast_fusion.4
  913.0 40.6 %all-reduce.8 = (f32[1024]{0:T(1024)S(1)}, f32[1024]{0:T(1024)S(1)}, f32[1024]{0:T(1024)S(1)}, f32[512]{0:T(512)S(1)}) all-reduce(f32[1024]{0:T(1024)S(1)} %get-tuple-element.328, f32[1024]{0:T(1024)S(1)} %get-tuple-element.326, f32[1024]{0:T(1024)S(1)} %get-tuple-element.324, ...), channel_id=13, replica_groups=mesh['fsdp'=4,'dp'=8] {'fsdp','dp'}, use_global_device_ids=true, to_apply=%region_33.34.clone | all-reduce | flops 3584 | bytes 28672
  963.6 14.6 bitcast_convert_fusion
  978.2 124.9 %reduce-scatter.16.cloned.1.call-done = f32[32,512]{1,0:T(8,128)} async-done(((f32[1024,512]{1,0:T(8,128)}), f32[32,512]{1,0:T(8,128)}) %reduce-scatter.16.cloned.1.call-update) | async-done | bytes 65552 | tf_op jit(solution)/shard_map/reduce_scatter | solution.py:412
  1103.1 137.2 %reduce-scatter.22.cloned.1.call-done = f32[32,512]{1,0:T(8,128)} async-done(((f32[1024,512]{1,0:T(8,128)}), f32[32,512]{1,0:T(8,128)}) %reduce-scatter.22.cloned.1.call-update) | async-done | bytes 65552 | tf_op jit(solution)/shard_map/reduce_scatter | solution.py:368
  1240.3 137.1 %reduce-scatter.24.cloned.1.call-done = f32[32,512]{1,0:T(8,128)} async-done(((f32[1024,512]{1,0:T(8,128)}), f32[32,512]{1,0:T(8,128)}) %reduce-scatter.24.cloned.1.call-update) | async-done | bytes 65552 | tf_op jit(solution)/shard_map/reduce_scatter | solution.py:369
  1377.4 143.2 %reduce-scatter.12.cloned.1.call-done = f32[32,1024]{1,0:T(8,128)} async-done(((f32[1024,1024]{1,0:T(8,128)}), f32[32,1024]{1,0:T(8,128)}) %reduce-scatter.12.cloned.1.call-update) | async-done | bytes 131088 | tf_op jit(solution)/shard_map/reduce_scatter | solution.py:410
  1520.6 143.7 %reduce-scatter.18.cloned.1.call-done = f32[32,1024]{1,0:T(8,128)} async-done(((f32[1024,1024]{1,0:T(8,128)}), f32[32,1024]{1,0:T(8,128)}) %reduce-scatter.18.cloned.1.call-update) | async-done | bytes 131088 | tf_op jit(solution)/shard_map/reduce_scatter | solution.py:413
  1664.2 143.3 %reduce-scatter.20.cloned.1.call-done = f32[32,1024]{1,0:T(8,128)} async-done(((f32[1024,1024]{1,0:T(8,128)}), f32[32,1024]{1,0:T(8,128)}) %reduce-scatter.20.cloned.1.call-update) | async-done | bytes 131088 | tf_op jit(solution)/shard_map/reduce_scatter | solution.py:367
  1807.6 143.6 %reduce-scatter.26.cloned.1.call-done = f32[32,1024]{1,0:T(8,128)} async-done(((f32[1024,1024]{1,0:T(8,128)}), f32[32,1024]{1,0:T(8,128)}) %reduce-scatter.26.cloned.1.call-update) | async-done | bytes 131088 | tf_op jit(solution)/shard_map/reduce_scatter | solution.py:370
  1951.2 249.2 %reduce-scatter.28.cloned.1.call-done = f32[32,2816]{1,0:T(8,128)} async-done(((f32[1024,2816]{1,0:T(8,128)}), f32[32,2816]{1,0:T(8,128)}) %reduce-scatter.28.cloned.1.call-update) | async-done | bytes 360464 | tf_op jit(solution)/shard_map/reduce_scatter | solution.py:328
  2200.4 251.8 %reduce-scatter.30.cloned.1.call-done = f32[32,2816]{1,0:T(8,128)} async-done(((f32[1024,2816]{1,0:T(8,128)}), f32[32,2816]{1,0:T(8,128)}) %reduce-scatter.30.cloned.1.call-update) | async-done | bytes 360464 | tf_op jit(solution)/shard_map/reduce_scatter | solution.py:329
  2452.2 251.3 %reduce-scatter.32.cloned.1.call-done = f32[88,1024]{1,0:T(8,128)} async-done(((f32[2816,1024]{1,0:T(8,128)}), f32[88,1024]{1,0:T(8,128)}) %reduce-scatter.32.cloned.1.call-update) | async-done | bytes 360464 | tf_op jit(solution)/shard_map/reduce_scatter | solution.py:330
  (542 shorter events, 315.2 us)
Async XLA Ops:
  7.2 56.9 %copy-start.31 = (s32[2]{0:T(128)S(1)}, s32[2]{0:T(128)}, u32[]{:S(2)}) copy-start(s32[2]{0:T(128)} %param.30) | copy-start | bytes 28
  7.2 60.5 %all-gather.24.cloned.1.call-start = ((), (), s32[]{:S(2)}) async-start(), calls=%async_computation.17 | async-start | bytes 1081344 | tf_op jit(solution)/shard_map/all_gather | solution.py:282
  7.9 115.7 %all-gather.22.cloned.1.call-start = ((), (), s32[]{:S(2)}) async-start(), calls=%async_computation.16 | async-start | bytes 1081344 | tf_op jit(solution)/shard_map/all_gather | solution.py:281
  8.7 170.7 %all-gather.16.cloned.1.call-start = ((), (), s32[]{:S(2)}) async-start(), calls=%async_computation.13 | async-start | bytes 1081344 | tf_op jit(solution)/shard_map/all_gather | solution.py:262
  9.4 225.6 %all-gather.14.cloned.1.call-start = ((), (), s32[]{:S(2)}) async-start(), calls=%async_computation.12 | async-start | bytes 1081344 | tf_op jit(solution)/shard_map/all_gather | solution.py:261
  10.0 283.3 %all-gather.12.cloned.1.call-start = ((), (), s32[]{:S(2)}) async-start(), calls=%async_computation.11 | async-start | bytes 2162688 | tf_op jit(solution)/shard_map/all_gather | solution.py:260
  10.6 341.0 %all-gather.18.cloned.1.call-start = ((), (), s32[]{:S(2)}) async-start(), calls=%async_computation.14 | async-start | bytes 2162688 | tf_op jit(solution)/shard_map/all_gather | solution.py:263
  11.2 398.9 %all-gather.20.cloned.1.call-start = ((), (), s32[]{:S(2)}) async-start(), calls=%async_computation.15 | async-start | bytes 2162688 | tf_op jit(solution)/shard_map/all_gather | solution.py:280
  11.9 456.6 %all-gather.26.cloned.1.call-start = ((), (), s32[]{:S(2)}) async-start(), calls=%async_computation.18 | async-start | bytes 2162688 | tf_op jit(solution)/shard_map/all_gather | solution.py:283
  12.7 524.8 %all-gather.32.cloned.1.call-start = ((), (), s32[]{:S(2)}) async-start(), calls=%async_computation.21 | async-start | bytes 5947392 | tf_op jit(solution)/shard_map/all_gather | solution.py:294
  13.4 593.1 %all-gather.30.cloned.1.call-start = ((), (), s32[]{:S(2)}) async-start(), calls=%async_computation.20 | async-start | bytes 5947392 | tf_op jit(solution)/shard_map/all_gather | solution.py:293
  14.0 661.7 %all-gather.28.cloned.1.call-start = ((), (), s32[]{:S(2)}) async-start(), calls=%async_computation.19 | async-start | bytes 5947392 | tf_op jit(solution)/shard_map/all_gather | solution.py:292
  14.7 963.5 %reduce-scatter.14.cloned.1.call-start = ((), (), s32[]{:S(2)}) async-start(), calls=%async_computation.23 | async-start | bytes 2162688 | tf_op jit(solution)/shard_map/reduce_scatter | solution.py:411
  69.2 55.9 %copy-start.21 = (bf16[1024,512]{0,1:T(8,128)(2,1)}, bf16[1024,512]{0,1:T(8,128)(2,1)S(1)}, u32[]{:S(2)}) copy-start(bf16[1024,512]{0,1:T(8,128)(2,1)S(1)} %copy.128) | copy-start | bytes 3145732
  140.1 97.2 %copy-start.3 = (bf16[2,128,1024]{2,1,0:T(8,128)(2,1)S(1)}, bf16[2,128,1024]{2,1,0:T(8,128)(2,1)}, u32[]{:S(2)}) copy-start(bf16[2,128,1024]{2,1,0:T(8,128)(2,1)} %param.28) | copy-start | bytes 1572868
  180.9 58.5 %copy-start.25 = (bf16[1024,512]{0,1:T(8,128)(2,1)}, bf16[1024,512]{0,1:T(8,128)(2,1)S(1)}, u32[]{:S(2)}) copy-start(bf16[1024,512]{0,1:T(8,128)(2,1)S(1)} %copy.120) | copy-start | bytes 3145732
  305.8 45.8 %copy-start.12 = (f32[8,128,2,128]{1,3,2,0:T(8,128)}, f32[8,128,2,128]{1,3,2,0:T(8,128)S(1)}, u32[]{:S(2)}) copy-start(f32[8,128,2,128]{1,3,2,0:T(8,128)S(1)} %get-tuple-element.812) | copy-start | bytes 3145732
  305.8 48.2 %copy-start.13 = (bf16[8,2,128,128]{2,3,1,0:T(8,128)(2,1)}, bf16[8,2,128,128]{2,3,1,0:T(8,128)(2,1)S(1)}, u32[]{:S(2)}) copy-start(bf16[8,2,128,128]{2,3,1,0:T(8,128)(2,1)S(1)} %get-tuple-element.176) | copy-start | bytes 1572868
  305.8 48.2 %copy-start.16 = (bf16[8,2,128,128]{2,3,1,0:T(8,128)(2,1)}, bf16[8,2,128,128]{2,3,1,0:T(8,128)(2,1)S(1)}, u32[]{:S(2)}) copy-start(bf16[8,2,128,128]{2,3,1,0:T(8,128)(2,1)S(1)} %get-tuple-element.813) | copy-start | bytes 1572868
  305.8 48.2 %copy-start.28 = (bf16[8,2,128,128]{2,3,1,0:T(8,128)(2,1)}, bf16[8,2,128,128]{2,3,1,0:T(8,128)(2,1)S(1)}, u32[]{:S(2)}) copy-start(bf16[8,2,128,128]{2,3,1,0:T(8,128)(2,1)S(1)} %get-tuple-element.822) | copy-start | bytes 1572868
  774.0 48.8 %copy-start.4 = (bf16[2,128,1024]{2,1,0:T(8,128)(2,1)S(1)}, bf16[2,128,1024]{2,1,0:T(8,128)(2,1)}, u32[]{:S(2)}) copy-start(bf16[2,128,1024]{2,1,0:T(8,128)(2,1)} %param.28) | copy-start | bytes 1572868
  830.0 273.1 %reduce-scatter.16.cloned.1.call-start = ((), (), s32[]{:S(2)}) async-start(), calls=%async_computation.24 | async-start | bytes 2162688 | tf_op jit(solution)/shard_map/reduce_scatter | solution.py:412
  833.0 407.3 %reduce-scatter.22.cloned.1.call-start = ((), (), s32[]{:S(2)}) async-start(), calls=%async_computation.27 | async-start | bytes 2162688 | tf_op jit(solution)/shard_map/reduce_scatter | solution.py:368
  851.0 526.4 %reduce-scatter.24.cloned.1.call-start = ((), (), s32[]{:S(2)}) async-start(), calls=%async_computation.28 | async-start | bytes 2162688 | tf_op jit(solution)/shard_map/reduce_scatter | solution.py:369
  854.0 666.6 %reduce-scatter.12.cloned.1.call-start = ((), (), s32[]{:S(2)}) async-start(), calls=%async_computation.22 | async-start | bytes 4325376 | tf_op jit(solution)/shard_map/reduce_scatter | solution.py:410
  862.5 801.7 %reduce-scatter.18.cloned.1.call-start = ((), (), s32[]{:S(2)}) async-start(), calls=%async_computation.25 | async-start | bytes 4325376 | tf_op jit(solution)/shard_map/reduce_scatter | solution.py:413
  866.3 941.2 %reduce-scatter.20.cloned.1.call-start = ((), (), s32[]{:S(2)}) async-start(), calls=%async_computation.26 | async-start | bytes 4325376 | tf_op jit(solution)/shard_map/reduce_scatter | solution.py:367
  875.6 1075.5 %reduce-scatter.26.cloned.1.call-start = ((), (), s32[]{:S(2)}) async-start(), calls=%async_computation.29 | async-start | bytes 4325376 | tf_op jit(solution)/shard_map/reduce_scatter | solution.py:370
  880.6 1319.8 %reduce-scatter.28.cloned.1.call-start = ((), (), s32[]{:S(2)}) async-start(), calls=%async_computation.30 | async-start | bytes 11894784 | tf_op jit(solution)/shard_map/reduce_scatter | solution.py:328
  889.0 1563.1 %reduce-scatter.30.cloned.1.call-start = ((), (), s32[]{:S(2)}) async-start(), calls=%async_computation.31 | async-start | bytes 11894784 | tf_op jit(solution)/shard_map/reduce_scatter | solution.py:329
  896.4 1807.1 %reduce-scatter.32.cloned.1.call-start = ((), (), s32[]{:S(2)}) async-start(), calls=%async_computation.32 | async-start | bytes 11894784 | tf_op jit(solution)/shard_map/reduce_scatter | solution.py:330
  913.0 45.3 %copy-start.7 = (f32[2,128,1024]{2,1,0:T(8,128)S(1)}, f32[2,128,1024]{2,1,0:T(8,128)}, u32[]{:S(2)}) copy-start(f32[2,128,1024]{2,1,0:T(8,128)} %copy-done.5) | copy-start | bytes 3145732
  (22 other events, 114.3 us)
Sparse Core Ops, SparseCore 0:
  11.0 56.6 all-gather.23
  70.7 52.8 all-gather.21
  126.6 52.7 all-gather.15
  182.2 52.7 all-gather.13
  237.8 55.4 all-gather.11
  296.1 55.4 all-gather.17
  354.6 55.3 all-gather.19
  413.0 55.4 all-gather.25
  471.4 66.0 all-gather.31
  540.2 66.1 all-gather.29
  609.4 66.1 all-gather.27
  830.1 136.3 reduce-scatter.13
  969.5 133.5 reduce-scatter.15
  1105.8 134.4 reduce-scatter.21
  1243.1 134.2 reduce-scatter.23
  1380.1 140.4 reduce-scatter.11
  1523.3 140.9 reduce-scatter.17
  1667.0 140.5 reduce-scatter.19
  1810.4 140.7 reduce-scatter.25
  1953.9 246.4 reduce-scatter.27
  2203.3 248.8 reduce-scatter.29
  2455.0 248.3 reduce-scatter.31
where the time goes:
time: 2720 us; the launch traced here: 2710 us
  waiting for transfers between devices  2240 us (82%)
  matrix products  189 us (7%)
  local copies, waits for them, and re-layouts  151 us (6%)
  blocking collectives  82.7 us (3%)
  other arithmetic  31.7 us (1%)
    reduce_scatter x1, waiting for transfers between devices, local(): lax.psum_scatter(grad_up_w, ('fsdp', 'dp'), scatter_dimension=0, tiled=True)  252 us
    reduce_scatter x1, waiting for transfers between devices, local(): lax.psum_scatter(grad_down_w, ('fsdp', 'dp'), scatter_dimension=0, tiled=...  251 us
    reduce_scatter x1, waiting for transfers between devices, local(): lax.psum_scatter(grad_gate_w, ('fsdp', 'dp'), scatter_dimension=0, tiled=...  249 us
    reduce_scatter x1, waiting for transfers between devices, local(): lax.psum_scatter(grad_out_one, ('fsdp', 'dp'), scatter_dimension=0, tiled...  144 us
    reduce_scatter x1, waiting for transfers between devices, local(): lax.psum_scatter(grad_out_two, ('fsdp', 'dp'), scatter_dimension=0, tiled...  144 us
    reduce_scatter x1, waiting for transfers between devices, local(): lax.psum_scatter(grad_query_two, ('fsdp', 'dp'), scatter_dimension=0, til...  143 us
    reduce_scatter x1, waiting for transfers between devices, local(): lax.psum_scatter(grad_query_one, ('fsdp', 'dp'), scatter_dimension=0, til...  143 us
    reduce_scatter x1, waiting for transfers between devices, local(): lax.psum_scatter(grad_key_two, ('fsdp', 'dp'), scatter_dimension=0, tiled...  137 us
  transfers between devices with their start and end apart: 22, of which 21 were waited for; matrix products, arithmetic and copies ran while one was open for 8% of the time, Pallas kernels for 0%

commit v1 on v0

v1 whole, which is shorter than its diff:
```python
import functools

import jax
import jax.numpy as jnp
import numpy as np
from jax import lax
from jax.experimental import pallas as pl
from jax.experimental.pallas import tpu as pltpu
from jax.sharding import PartitionSpec as P

HEADS = 16
HD = 64
BUCKETS = 32
KVH = 8
PAIR = 2 * HD
AXES = ("fsdp", "dp")
norm_eps = 1e-06
masked_score = -1000000000.0
bucket_reach = 128
f32 = jnp.float32
bf16 = jnp.bfloat16
VMEM_LIMIT = 56 * 1024 * 1024


def reversed_buckets():
    distance = (-np.arange(bucket_reach)) % bucket_reach
    exact_count = BUCKETS // 2
    spread = (
        np.log(np.maximum(distance, 1) / exact_count)
        / np.log(bucket_reach / exact_count)
        * (BUCKETS - exact_count)
    )
    far_bucket = np.minimum(exact_count + np.floor(spread).astype(np.int64), BUCKETS - 1)
    bucket_id = np.where(distance < exact_count, distance, far_bucket)
    return (bucket_id[None] == np.arange(BUCKETS)[:, None]).astype(np.float32)


def dot(a, b, ca=1, cb=0):
    return lax.dot_general(a, b, (((ca,), (cb,)), ((), ())), preferred_element_type=f32)


def call(kernel, ins, in_specs, out_shape, out_specs, name, after=(), grid=(1,), scratch=(), prefetch=None):
    lead = 0 if prefetch is None else 1
    n = lead + len(ins)

    def body(*refs):
        kernel(*refs[:n], *refs[n + len(after) :])

    spec = pltpu.PrefetchScalarGridSpec(
        num_scalar_prefetch=lead,
        grid=grid,
        in_specs=list(in_specs) + [pl.BlockSpec(memory_space=pl.ANY)] * len(after),
        out_specs=out_specs,
        scratch_shapes=list(scratch),
    )
    front = () if prefetch is None else (prefetch,)
    return pl.pallas_call(
        body,
        grid_spec=spec,
        out_shape=out_shape,
        compiler_params=pltpu.CompilerParams(vmem_limit_bytes=VMEM_LIMIT),
        cost_estimate=pl.CostEstimate(flops=1000, bytes_accessed=1000, transcendentals=0),
        name=name,
    )(*front, *ins, *after)


def whole(shape):
    return pl.BlockSpec(shape, lambda *_: (0,) * len(shape))


def struct(shape, dtype):
    return jax.ShapeDtypeStruct(shape, dtype)


def smem():
    return pl.BlockSpec(memory_space=pltpu.SMEM)


class Links:
    names = ("hi", "core", "ring", "lo")

    def __init__(self, mesh):
        nf, nd = mesh.shape["fsdp"], mesh.shape["dp"]
        self.nf, self.nd, self.size = nf, nd, nd // 2
        size = self.size
        self.lengths = {"hi": nf // 2, "core": 2, "ring": size, "lo": 2}
        spots = [(f, d) for f in range(nf) for d in range(nd)]

        def pairs(move):
            out = []
            for f, d in spots:
                g, e = move(f, d)
                out.append((f * nd + d, g * nd + e))
            return out

        self.pairs = {
            "core": pairs(lambda f, d: (f ^ 1, d)),
            "hi": pairs(lambda f, d: (f ^ 2, d)),
            "both": pairs(lambda f, d: (f ^ 3, d)),
            "lo": pairs(lambda f, d: (f, d ^ 1)),
        }
        for s in range(1, size):
            self.pairs[s] = pairs(lambda f, d: (f, ((d // 2 + s) % size) * 2 + d % 2))

    def locate(self):
        f, d = lax.axis_index("fsdp"), lax.axis_index("dp")
        self.hi, self.core, self.ring, self.lo = f // 2, f % 2, d // 2, d % 2
        self.spot = jnp.stack([self.hi, self.core, self.ring, self.lo]).astype(jnp.int32)

    def send(self, a, way):
        return lax.ppermute(a, AXES, self.pairs[way])

    def spread_ring(self, shard, after=()):
        return [shard] + [self.send(tie(shard, *after), s) for s in range(1, self.size)]

    def quarters(self, wide):
        mine = self.hi * 2 + self.core
        out = [lax.dynamic_index_in_dim(wide, mine, 0, keepdims=False)]
        for flip, way in ((1, "core"), (2, "hi"), (3, "both")):
            theirs = lax.dynamic_index_in_dim(wide, mine ^ flip, 0, keepdims=False)
            out.append(self.send(theirs, way))
        return jnp.stack(out)

    def unquarter(self, near):
        mine = self.hi * 2 + self.core
        return jnp.stack(
            [lax.dynamic_index_in_dim(near, mine ^ f, 0, keepdims=False) for f in range(self.nf)]
        )

    def grow(self, stack, order, first=(), second=(), third=()):
        one, two = order
        got = self.send(tie(stack, *first), one)
        pair = jnp.stack([stack, got])
        far = self.send(tie(pair, *second), two)
        near_far = [{}, {one: 1}]
        entries = [(pair, near_far), (far, [{**f, two: 1} for f in near_far])]
        for array, fars in list(entries):
            entries.append(
                (self.send(tie(array, *third), "core"), [{**f, "core": 1} for f in fars])
            )
        return Blocks(self, entries)


class Blocks:
    def __init__(self, links, entries, quads=False):
        self.links = links
        self.arrays = [a for a, _ in entries]
        self.fars = [f for _, f in entries]
        self.quads = quads
        _, _, self.r, self.c = self.arrays[0].shape
        self.count = len(entries)

    def specs(self, width=None, index=0):
        return [
            pl.BlockSpec((*a.shape[:3], width or self.c), lambda *_: (0, 0, 0, index))
            for a in self.arrays
        ]

    def put(self, spot, refs, *outs):
        size = self.links.size
        quads = [(0, 0), (0, 1), (1, 0), (1, 1)] if self.quads else [None]
        r = self.r // len(quads)
        for ref, fars in zip(refs, self.fars):
            for i, far in enumerate(fars):
                at_lo = 1 - spot[3] if far.get("lo") else spot[3]
                for t in range(size):
                    at_ring = lax.rem(spot[2] + (size - t), size)
                    for q, quad in enumerate(quads):
                        far_hi, far_core = quad or (far.get("hi"), far.get("core"))
                        at_hi = 1 - spot[0] if far_hi else spot[0]
                        at_core = 1 - spot[1] if far_core else spot[1]
                        row = (((at_hi * 2 + at_core) * size + at_ring) * 2 + at_lo) * r
                        rows = pl.ds(pl.multiple_of(row, r), r)
                        left = 0
                        for out in outs:
                            width = out.shape[-1]
                            out[rows, :] = ref[i, t, q * r : (q + 1) * r, left : left + width]
                            left += width


def tie(x, *after):
    return lax.optimization_barrier((x, *after))[0] if after else x


def assemble(links, near, far, after=()):
    size = links.size
    _, r, c = near.shape

    def kernel(spot, near_ref, far_ref, out, held, sems_in, sems_out):
        copies = []
        for k, ref in enumerate((near_ref, far_ref)):
            at_lo = 1 - spot[3] if k else spot[3]
            for t in range(size):
                at_ring = lax.rem(spot[2] + (size - t), size)
                copies.append(
                    (
                        pltpu.make_async_copy(ref.at[t], held.at[k, t], sems_in.at[k, t]),
                        pltpu.make_async_copy(held.at[k, t], out.at[at_ring, at_lo], sems_out.at[k, t]),
                    )
                )
        for one, _ in copies:
            one.start()
        for one, two in copies:
            one.wait()
            two.start()
        for _, two in copies:
            two.wait()

    out = call(
        kernel,
        [links.spot, near, far],
        [smem()] + [pl.BlockSpec(memory_space=pl.ANY)] * 2,
        struct((size, 2, r, c), bf16),
        pl.BlockSpec(memory_space=pl.ANY),
        "assemble",
        after=after,
        scratch=[
            pltpu.VMEM((2, size, r, c), bf16),
            pltpu.SemaphoreType.DMA((2, size)),
            pltpu.SemaphoreType.DMA((2, size)),
        ],
    )
    return out.reshape(-1, c)


class Leaf:
    def __init__(self, array, axes, held=(), width=None, index=0):
        self.array, self.axes, self.held = array, axes, dict(held)
        self.width = width or array.shape[-1]
        self.index = index

    def hold(self, way, far):
        held = dict(self.held)
        if way in self.axes:
            held[way] = far
        return Leaf(self.array, self.axes, held, self.width, self.index)

    def free(self):
        return [a for a in self.axes if a not in self.held]

    def spec(self, ring_steps):
        shape, pick = [], []
        for i, a in enumerate(self.axes):
            if a in self.held:
                shape.append(None)
                pick.append(("far" if self.held[a] else "here", Links.names.index(a)))
            elif a == "ring" and ring_steps:
                shape.append(1)
                pick.append(("step", 0))
            else:
                shape.append(self.array.shape[i])
                pick.append(("zero", 0))

        def index(t, spot):
            out = []
            for kind, i in pick:
                if kind == "far":
                    out.append(1 - spot[i])
                elif kind == "here":
                    out.append(spot[i])
                else:
                    out.append(t if kind == "step" else 0)
            return (*out, 0, self.index)

        return pl.BlockSpec((*shape, self.array.shape[-2], self.width), index)


class Scatter:
    def __init__(self, links, jobs):
        self.links = links
        self.jobs = [([*leaves], list(order)) for leaves, order in jobs]
        self.last = None

    def step(self, after=()):
        links = self.links
        size = links.size
        ways = [order.pop(0) for _, order in self.jobs]
        ins, specs, outs, out_specs, plan = [], [], [], [], []
        for (leaves, _), way in zip(self.jobs, ways):
            moving = [leaf.hold(way, True) for leaf in leaves]
            free = moving[0].free()
            ins += [leaf.array for leaf in moving]
            specs += [leaf.spec(True) for leaf in moving]
            shape = tuple(links.lengths[a] for a in free) + (moving[0].array.shape[-2], moving[0].width)
            outs.append(struct(shape, bf16))
            block = tuple(1 if a == "ring" else links.lengths[a] for a in free) + shape[-2:]
            at = free.index("ring")
            out_specs.append(
                pl.BlockSpec(
                    block,
                    functools.partial(
                        lambda at, rank, t, spot: tuple(t if i == at else 0 for i in range(rank)),
                        at,
                        len(block),
                    ),
                )
            )
            plan.append((len(moving), free))

        def kernel(spot, *refs):
            n = 0
            for (count, _), out in zip(plan, refs[len(ins) :]):
                total = refs[n][...].astype(f32)
                for ref in refs[n + 1 : n + count]:
                    total = total + ref[...].astype(f32)
                out[...] = total.astype(bf16)
                n += count

        sent = call(
            kernel, ins, specs, outs, out_specs, "combine", after=after, grid=(size,), prefetch=links.spot
        )
        jobs = []
        for (leaves, order), way, away, (_, free) in zip(self.jobs, ways, sent, plan):
            kept = [leaf.hold(way, False) for leaf in leaves]
            jobs.append((kept + [Leaf(links.send(away, way), free)], order))
        self.jobs = jobs
        return sent[:1]

    def spread(self, after=()):
        links = self.links
        size = links.size
        ins, specs, groups, where = [], [], {}, []
        for leaves, _ in self.jobs:
            ins += [leaf.array for leaf in leaves]
            specs += [leaf.spec(False) for leaf in leaves]
            free = [a for a in leaves[0].free() if a != "ring"]
            key = tuple(links.lengths[a] for a in free) + (leaves[0].array.shape[-2],)
            left = groups.get(key, 0)
            groups[key] = left + leaves[0].width
            where.append((key, left, leaves[0].width, len(leaves), leaves[0].free().index("ring")))
        keys = list(groups)
        outs = []
        for key in keys:
            shape = key + (groups[key],)
            outs += [struct(shape, f32)] + [struct(shape, bf16)] * (size - 1)

        def kernel(spot, *refs):
            n, m = 0, len(ins)
            for key, left, width, count, at in where:
                base = m + keys.index(key) * size
                for s in range(size):
                    ring = lax.rem(spot[2] + s, size)
                    total = None
                    for ref in refs[n : n + count]:
                        term = (ref[ring] if at == 0 else ref[:, :, ring]).astype(f32)
                        total = term if total is None else total + term
                    out = refs[base + s]
                    out[..., left : left + width] = total.astype(out.dtype)
                n += count

        sent = call(
            kernel, ins, specs, outs, [whole(o.shape) for o in outs], "spread", after=after, prefetch=links.spot
        )
        totals = {}
        for i, key in enumerate(keys):
            group = sent[i * size : (i + 1) * size]
            total = group[0]
            for s in range(1, size):
                total = total + links.send(group[s], s).astype(f32)
            totals[key] = total
        self.results = [totals[key][..., left : left + width] for key, left, width, _, _ in where]
        return sent[:1]


def norm_scale(rows):
    return lax.rsqrt(jnp.mean(rows * rows, axis=-1, keepdims=True) + norm_eps)


def norm_back(grad_normed, rows, gain):
    scale = norm_scale(rows)
    scaled = grad_normed * gain
    inner_mean = jnp.mean(scaled * rows, axis=-1, keepdims=True)
    grad_rows = scale * scaled - rows * (scale * scale * scale) * inner_mean
    return grad_rows, jnp.sum(grad_normed * rows * scale, axis=0, keepdims=True)


def swap_halves(block):
    return pltpu.roll(block.astype(f32), HD, 1).astype(bf16)


def low_lanes(shape):
    return lax.broadcasted_iota(jnp.int32, shape, 1) < HD


def heads_low(block):
    keep = low_lanes(block.shape)
    zero = jnp.zeros_like(block)
    return jnp.concatenate(
        [jnp.where(keep, block, zero), jnp.where(keep, swap_halves(block), zero)], axis=0
    )


def heads_high(block):
    keep = low_lanes(block.shape)
    zero = jnp.zeros_like(block)
    return jnp.concatenate(
        [jnp.where(keep, zero, swap_halves(block)), jnp.where(keep, zero, block)], axis=0
    )


def merge_low(both):
    half = both.shape[0] // 2
    even, odd = both[:half], both[half:]
    return jnp.where(low_lanes(even.shape), even, pltpu.roll(odd, HD, 1))


def merge_high(both):
    half = both.shape[0] // 2
    even, odd = both[:half], both[half:]
    return jnp.where(low_lanes(even.shape), pltpu.roll(even, HD, 1), odd)


def toeplitz(row, length):
    return pltpu.roll(jnp.broadcast_to(row, (length, length)), 0, 1, stride=1, stride_axis=0)


def diagonal_sums(flipped):
    turned = pltpu.roll(flipped, 1, 1, stride=1, stride_axis=0)
    return jnp.sum(turned, axis=0, keepdims=True)


def causal_probs(low, keyval, table, g, length, valid_len):
    s = dot(low, keyval, 1, 1)
    bias = jnp.concatenate(
        [toeplitz(table[2 * g : 2 * g + 1], length), toeplitz(table[2 * g + 1 : 2 * g + 2], length)],
        axis=0,
    )
    i = lax.broadcasted_iota(jnp.int32, (length, length), 0)
    j = lax.broadcasted_iota(jnp.int32, (length, length), 1)
    valid = (j <= i) & (j < valid_len)
    valid = jnp.concatenate([valid, valid], axis=0)
    s = jnp.where(valid, s + bias, masked_score)
    e = jnp.exp(s - jnp.max(s, axis=-1, keepdims=True))
    return e / jnp.sum(e, axis=-1, keepdims=True)


def split_rows(lhs_t, rhs, core, keep, away):
    half = keep.shape[1]
    for hi in range(keep.shape[0]):
        for out, at in ((keep, core), (away, 1 - core)):
            row = pl.multiple_of((hi * 2 + at) * half, half)
            out[hi] = dot(lhs_t[pl.ds(row, half), :], rhs).astype(bf16)


def project_memory(links, memory, blocks):
    seqs, count, width = memory.shape
    cols = KVH * PAIR
    tile = 512
    n = blocks.count

    def kernel(spot, mem_ref, *refs):
        held = refs[:n]
        out_ref, small_ref, w_ref, wt_ref = refs[n:]

        @pl.when((pl.program_id(0) == 0) & (pl.program_id(1) == 0))
        def _():
            blocks.put(spot, held, w_ref)
            wt_ref[...] = w_ref[:, :cols].T
            small_ref[...] = w_ref[:, cols:].astype(f32).T[:8]

        out_ref[0] = dot(wt_ref[...], mem_ref[0], 1, 1).astype(bf16)

    return call(
        kernel,
        [links.spot, memory] + blocks.arrays,
        [smem(), pl.BlockSpec((1, tile, width), lambda b, t: (b, t, 0))] + blocks.specs(),
        (struct((seqs, cols, count), bf16), struct((8, width), f32)),
        [pl.BlockSpec((1, cols, tile), lambda b, t: (b, 0, t)), whole((8, width))],
        "project_memory",
        grid=(seqs, count // tile),
        scratch=[pltpu.VMEM((width, blocks.c), bf16), pltpu.VMEM((cols, width), bf16)],
    )


def causal_forward(links, x, blocks, gain, table, lengths, after):
    seqs, length, width = x.shape
    rows = seqs * length
    cols = 2 * width
    n = blocks.count

    def kernel(spot, len_ref, x_ref, gain_ref, tab_ref, *refs):
        x1_ref, n1_ref, qkv_ref, o1_ref, w_ref, wo_ref = refs[n:]
        blocks.put(spot, refs[:n], w_ref, wo_ref)
        xf = x_ref[...].astype(f32)
        n1 = (xf * norm_scale(xf) * gain_ref[...]).astype(bf16)
        n1_ref[...] = n1
        qkv_ref[...] = dot(n1, w_ref[...]).astype(bf16)
        tab = tab_ref[...]
        for g in range(KVH):
            lanes = slice(g * PAIR, (g + 1) * PAIR)
            kv_lanes = slice(width + g * PAIR, width + (g + 1) * PAIR)
            for b in range(seqs):
                part = slice(b * length, (b + 1) * length)
                keyval = qkv_ref[part, kv_lanes]
                p = causal_probs(
                    heads_low(qkv_ref[part, lanes]), keyval, tab, g, length, len_ref[b]
                )
                o1_ref[part, lanes] = merge_high(dot(p.astype(bf16), keyval)).astype(bf16)
        x1_ref[...] = xf + dot(o1_ref[...], wo_ref[...])

    return call(
        kernel,
        [links.spot, lengths, x.reshape(rows, width), gain, table] + blocks.arrays,
        [smem(), smem(), whole((rows, width)), whole((1, width)), whole(table.shape)]
        + blocks.specs(),
        (
            struct((rows, width), f32),
            struct((rows, width), bf16),
            struct((rows, cols), bf16),
            struct((rows, width), bf16),
        ),
        [whole((rows, width)), whole((rows, width)), whole((rows, cols)), whole((rows, width))],
        "causal_forward",
        after=after,
        scratch=[pltpu.VMEM((width, cols), bf16), pltpu.VMEM((width, width), bf16)],
    )


def cross_forward(links, x1, keyval, blocks, gain_cross, gain_feed):
    rows, width = x1.shape
    seqs, _, count = keyval.shape
    length = rows // seqs
    n = blocks.count

    def kernel(spot, x1_ref, kv_ref, g2_ref, g3_ref, *refs):
        n2_ref, q2_ref, o2_ref, x2_ref, n3_ref, p_ref, wq_ref, wo_ref = refs[n:]
        b, g = pl.program_id(0), pl.program_id(1)

        @pl.when((b == 0) & (g == 0))
        def _():
            blocks.put(spot, refs[:n], wq_ref, wo_ref)
            x1v = x1_ref[...]
            n2 = (x1v * norm_scale(x1v) * g2_ref[...]).astype(bf16)
            n2_ref[...] = n2
            q2_ref[...] = dot(n2, wq_ref[...]).astype(bf16)

        part = pl.ds(pl.multiple_of(b * length, length), length)
        lanes = pl.ds(pl.multiple_of(g * PAIR, PAIR), PAIR)
        kv = kv_ref[0]
        s = dot(heads_low(q2_ref[part, lanes]), kv)
        e = jnp.exp(s - jnp.max(s, axis=-1, keepdims=True))
        p = (e * (1.0 / jnp.sum(e, axis=-1, keepdims=True))).astype(bf16)
        p_ref[0] = p
        o2_ref[part, lanes] = merge_high(dot(p, kv, 1, 1)).astype(bf16)

        @pl.when((b == seqs - 1) & (g == KVH - 1))
        def _():
            x2 = x1_ref[...] + dot(o2_ref[...], wo_ref[...])
            x2_ref[...] = x2
            n3_ref[...] = (x2 * norm_scale(x2) * g3_ref[...]).astype(bf16)

    return call(
        kernel,
        [links.spot, x1, keyval, gain_cross, gain_feed] + blocks.arrays,
        [
            smem(),
            whole((rows, width)),
            pl.BlockSpec((1, PAIR, count), lambda b, g: (b, g, 0)),
            whole((1, width)),
            whole((1, width)),
        ]
        + blocks.specs(),
        (
            struct((rows, width), bf16),
            struct((rows, width), bf16),
            struct((rows, width), bf16),
            struct((rows, width), f32),
            struct((rows, width), bf16),
            struct((seqs * KVH, 2 * length, count), bf16),
        ),
        [whole((rows, width))] * 5
        + [pl.BlockSpec((1, 2 * length, count), lambda b, g: (b * KVH + g, 0, 0))],
        "cross_forward",
        grid=(seqs, KVH),
        scratch=[pltpu.VMEM((width, width), bf16)] * 2,
    )


def stack_rows(refs, out):
    rows = refs[0].shape[0]
    for i, ref in enumerate(refs):
        out[i * rows : (i + 1) * rows] = ref[...]


def feed_through(links, n3s, cots, blocks, w_down, after):
    rows, width = n3s[0].shape
    units = w_down.shape[0]
    n = blocks.count
    c0 = np.float32(np.sqrt(2.0 / np.pi))
    c1 = np.float32(0.044715)
    cuts = [slice(i, min(i + 256, units)) for i in range(0, units, 256)]

    def kernel(spot, *refs):
        wd_ref = refs[8]
        held = refs[9 : 9 + n]
        hid_ref, dgate_ref, dup_ref, dn_ref, dn_hi_ref, dn_away_ref = refs[9 + n : 15 + n]
        wg_ref, wu_ref, n3_all, cot_all = refs[15 + n :]
        blocks.put(spot, held, wg_ref, wu_ref)
        stack_rows(refs[:4], n3_all)
        stack_rows(refs[4:8], cot_all)
        for cut in cuts:
            gate = dot(n3_all[...], wg_ref[:, cut])
            up = dot(n3_all[...], wu_ref[:, cut])
            dh = dot(cot_all[...], wd_ref[cut, :], 1, 1)
            square = gate * gate
            t = jnp.tanh(c0 * (gate + c1 * (square * gate)))
            cdf = 0.5 * (1.0 + t)
            value = gate * cdf
            slope = cdf + 0.5 * gate * (1.0 - t * t) * (c0 * (1.0 + 3.0 * c1 * square))
            hid_ref[:, cut] = (value * up).astype(bf16)
            dgate_ref[:, cut] = (dh * up * slope).astype(bf16)
            dup_ref[:, cut] = (dh * value).astype(bf16)
        for i in range(0, width, 256):
            at = slice(i, i + 256)
            dn = dot(dgate_ref[...], wg_ref[at, :], 1, 1) + dot(dup_ref[...], wu_ref[at, :], 1, 1)
            dn_ref[:, at] = dn[:rows]
            dn_away_ref[:rows, at] = dn[rows : 2 * rows].astype(bf16)
            dn_hi_ref[:, at] = dn[2 * rows : 3 * rows]
            dn_away_ref[rows:, at] = dn[3 * rows :].astype(bf16)

    return call(
        kernel,
        [links.spot, *n3s, *cots, w_down] + blocks.arrays,
        [smem()] + [whole((rows, width))] * 8 + [whole(w_down.shape)] + blocks.specs(),
        (
            struct((4 * rows, units), bf16),
            struct((4 * rows, units), bf16),
            struct((4 * rows, units), bf16),
            struct((rows, width), f32),
            struct((rows, width), f32),
            struct((2 * rows, width), bf16),
        ),
        [whole((4 * rows, units))] * 3 + [whole((rows, width))] * 2 + [whole((2 * rows, width))],
        "feed_through",
        after=after,
        scratch=[
            pltpu.VMEM((width, units), bf16),
            pltpu.VMEM((width, units), bf16),
            pltpu.VMEM((4 * rows, width), bf16),
            pltpu.VMEM((4 * rows, width), bf16),
        ],
    )


def feed_weight_grads(n3s, cots, hidden, dgate, dup, w_down, after):
    rows, width = n3s[0].shape
    units = hidden.shape[1]

    def kernel(*refs):
        hid_ref, dgate_ref, dup_ref, wd_ref = refs[8:12]
        y_ref, y_hi_ref, y_away_ref, gu_ref, gd_ref, n3t_ref, cot_all, hid_t = refs[12:]
        for i in range(4):
            n3t_ref[:, i * rows : (i + 1) * rows] = refs[i][...].T
        stack_rows(refs[4:8], cot_all)
        hid_t[...] = hid_ref[...].T
        for i in range(0, width, 256):
            gu_ref[i : i + 256, :units] = dot(n3t_ref[i : i + 256], dgate_ref[...]).astype(bf16)
            gu_ref[i : i + 256, units:] = dot(n3t_ref[i : i + 256], dup_ref[...]).astype(bf16)
        for i in range(0, units, 352):
            gd_ref[i : i + 352] = dot(hid_t[i : i + 352], cot_all[...]).astype(bf16)
        for i in range(0, width, 256):
            at = slice(i, i + 256)
            y = dot(hid_ref[...], wd_ref[:, at])
            y_ref[:, at] = y[:rows]
            y_away_ref[:rows, at] = y[rows : 2 * rows].astype(bf16)
            y_hi_ref[:, at] = y[2 * rows : 3 * rows]
            y_away_ref[rows:, at] = y[3 * rows :].astype(bf16)

    return call(
        kernel,
        [*n3s, *cots, hidden, dgate, dup, w_down],
        [whole((rows, width))] * 8 + [whole((4 * rows, units))] * 3 + [whole(w_down.shape)],
        (
            struct((rows, width), f32),
            struct((rows, width), f32),
            struct((2 * rows, width), bf16),
            struct((width, 2 * units), bf16),
            struct((units, width), bf16),
        ),
        [whole((rows, width))] * 2
        + [whole((2 * rows, width)), whole((width, 2 * units)), whole((units, width))],
        "feed_weight_grads",
        after=after,
        scratch=[
            pltpu.VMEM((width, 4 * rows), bf16),
            pltpu.VMEM((4 * rows, width), bf16),
            pltpu.VMEM((units, 4 * rows), bf16),
        ],
    )


def cross_enter(links, x2, gain_feed, dn3, dn3_core, dn3_hi, cotangent, o2, out_blocks, after):
    rows, width = x2.shape
    n = out_blocks.count
    split = (2, width // 4, width)

    def kernel(spot, x2_ref, g_ref, dn_ref, dn_core_ref, dn_hi_ref, cot_ref, o2_ref, *refs):
        dx_ref, do_ref, keep_ref, away_ref, gg_ref, w_ref, o2t_ref = refs[n:]
        out_blocks.put(spot, refs[:n], w_ref)
        dn = dn_ref[...] + dn_core_ref[...].astype(f32) + dn_hi_ref[...].astype(f32)
        grad_rows, grad_gain = norm_back(dn, x2_ref[...], g_ref[...])
        gg_ref[...] = grad_gain
        dx2 = cot_ref[...].astype(f32) + grad_rows
        dx_ref[...] = dx2
        da = dx2.astype(bf16)
        do_ref[...] = dot(da, w_ref[...], 1, 1).astype(bf16)
        o2t_ref[...] = o2_ref[...].T
        split_rows(o2t_ref, da, spot[1], keep_ref, away_ref)

    return call(
        kernel,
        [links.spot, x2, gain_feed, dn3, dn3_core, dn3_hi, cotangent, o2] + out_blocks.arrays,
        [smem(), whole((rows, width)), whole((1, width))]
        + [whole((rows, width))] * 5
        + out_blocks.specs(width, 1),
        (
            struct((rows, width), f32),
            struct((rows, width), bf16),
            struct(split, bf16),
            struct(split, bf16),
            struct((1, width), f32),
        ),
        [whole((rows, width))] * 2 + [whole(split)] * 2 + [whole((1, width))],
        "cross_enter",
        after=after,
        scratch=[pltpu.VMEM((width, width), bf16), pltpu.VMEM((width, rows), bf16)],
    )


def cross_backward(q2, do2, o2, keyval, probs, after):
    rows, width = q2.shape
    seqs, cols, count = keyval.shape
    length = rows // seqs
    chunk = 512

    def kernel(q_ref, do_ref, o_ref, kv_ref, p_ref, dq_ref, dkv_ref):
        q, do = q_ref[...], do_ref[...]
        low, high = heads_low(q), heads_high(do)
        low_t, high_t = low.T, high.T
        product = do.astype(f32) * o_ref[...].astype(f32)
        keep = low_lanes(product.shape)
        inner = jnp.concatenate(
            [
                jnp.sum(jnp.where(keep, product, 0.0), axis=-1, keepdims=True),
                jnp.sum(jnp.where(keep, 0.0, product), axis=-1, keepdims=True),
            ],
            axis=0,
        )
        dq = jnp.zeros((2 * length, PAIR), f32)
        for c in range(count // chunk):
            cut = slice(c * chunk, (c + 1) * chunk)
            kv = kv_ref[0, :, cut]
            p = p_ref[0, :, cut]
            dp = dot(high, kv)
            ds = (p.astype(f32) * (dp - inner)).astype(bf16)
            dq += dot(ds, kv, 1, 1)
            dkv_ref[0, :, cut] = (dot(low_t, ds) + dot(high_t, p)).astype(bf16)
        dq_ref[...] = merge_low(dq).astype(bf16)

    heads_block = pl.BlockSpec((length, PAIR), lambda b, g: (b, g))
    kv_block = pl.BlockSpec((1, PAIR, count), lambda b, g: (b, g, 0))
    return call(
        kernel,
        [q2, do2, o2, keyval, probs],
        [
            heads_block,
            heads_block,
            heads_block,
            kv_block,
            pl.BlockSpec((1, 2 * length, count), lambda b, g: (b * KVH + g, 0, 0)),
        ],
        (struct((rows, width), bf16), struct((seqs, cols, count), bf16)),
        [heads_block, kv_block],
        "cross_backward",
        after=after,
        grid=(seqs, KVH),
    )


def keyval_weight_grad(links, memory, grad_keyval, small, after):
    seqs, count, width = memory.shape
    cols = grad_keyval.shape[1]
    tile = 512
    steps = count // tile
    wide = cols + EXTRA
    split = (2, width // 4, wide)

    def kernel(spot, mem_ref, dkv_ref, small_ref, keep_ref, away_ref, acc_ref):
        b, t = pl.program_id(0), pl.program_id(1)

        @pl.when((b == 0) & (t == 0))
        def _():
            acc_ref[...] = jnp.zeros_like(acc_ref)
            acc_ref[cols : cols + 8] = small_ref[...]

        acc_ref[:cols] += dot(dkv_ref[0], mem_ref[0])

        @pl.when((b == seqs - 1) & (t == steps - 1))
        def _():
            half = split[1]
            for hi in range(2):
                for out, at in ((keep_ref, spot[1]), (away_ref, 1 - spot[1])):
                    lanes = pl.ds(pl.multiple_of((hi * 2 + at) * half, half), half)
                    out[hi] = acc_ref[:, lanes].T.astype(bf16)

    return call(
        kernel,
        [links.spot, memory, grad_keyval, small],
        [
            smem(),
            pl.BlockSpec((1, tile, width), lambda b, t: (b, t, 0)),
            pl.BlockSpec((1, cols, tile), lambda b, t: (b, 0, t)),
            whole((8, width)),
        ],
        (struct(split, bf16), struct(split, bf16)),
        [whole(split)] * 2,
        "keyval_weight_grad",
        after=after,
        grid=(seqs, steps),
        scratch=[pltpu.VMEM((wide, width), f32)],
    )


def memory_gradient(links, grad_keyval, blocks, after):
    seqs, cols, count = grad_keyval.shape
    width = cols
    tile = 512
    n = blocks.count

    def kernel(spot, dkv_ref, *refs):
        out_ref, w_ref = refs[n:]

        @pl.when((pl.program_id(0) == 0) & (pl.program_id(1) == 0))
        def _():
            blocks.put(spot, refs[:n], w_ref)

        out_ref[0] = dot(dkv_ref[0].T, w_ref[...], 1, 1).astype(bf16)

    return call(
        kernel,
        [links.spot, grad_keyval] + blocks.arrays,
        [smem(), pl.BlockSpec((1, cols, tile), lambda b, t: (b, 0, t))] + blocks.specs(cols, 0),
        struct((seqs, count, width), bf16),
        pl.BlockSpec((1, tile, width), lambda b, t: (b, t, 0)),
        "memory_gradient",
        after=after,
        grid=(seqs, count // tile),
        scratch=[pltpu.VMEM((width, cols), bf16)],
    )


def causal_enter(links, dx2, x1, gain_cross, n2, dq2, o1, out_blocks, query_blocks, after):
    rows, width = x1.shape
    n, m = out_blocks.count, out_blocks.count + query_blocks.count
    split = (2, width // 4, 2 * width)

    def kernel(spot, dx2_ref, x1_ref, g_ref, n2_ref, dq2_ref, o1_ref, *refs):
        dx_ref, do_ref, keep_ref, away_ref, gg_ref, wo_ref, wq_ref, o1t_ref, n2t_ref = refs[m:]
        out_blocks.put(spot, refs[:n], wo_ref)
        query_blocks.put(spot, refs[n:m], wq_ref)
        dq2 = dq2_ref[...]
        grad_rows, grad_gain = norm_back(dot(dq2, wq_ref[...], 1, 1), x1_ref[...], g_ref[...])
        gg_ref[...] = grad_gain
        dx1 = dx2_ref[...] + grad_rows
        dx_ref[...] = dx1
        da = dx1.astype(bf16)
        do_ref[...] = dot(da, wo_ref[...], 1, 1).astype(bf16)
        o1t_ref[...] = o1_ref[...].T
        split_rows(o1t_ref, da, spot[1], keep_ref.at[:, :, :width], away_ref.at[:, :, :width])
        n2t_ref[...] = n2_ref[...].T
        split_rows(n2t_ref, dq2, spot[1], keep_ref.at[:, :, width:], away_ref.at[:, :, width:])

    return call(
        kernel,
        [links.spot, dx2, x1, gain_cross, n2, dq2, o1] + out_blocks.arrays + query_blocks.arrays,
        [smem(), whole((rows, width)), whole((rows, width)), whole((1, width))]
        + [whole((rows, width))] * 3
        + out_blocks.specs(width, 2)
        + query_blocks.specs(width, 0),
        (
            struct((rows, width), f32),
            struct((rows, width), bf16),
            struct(split, bf16),
            struct(split, bf16),
            struct((1, width), f32),
        ),
        [whole((rows, width))] * 2 + [whole(split)] * 2 + [whole((1, width))],
        "causal_enter",
        after=after,
        scratch=[
            pltpu.VMEM((width, width), bf16),
            pltpu.VMEM((width, width), bf16),
            pltpu.VMEM((width, rows), bf16),
            pltpu.VMEM((width, rows), bf16),
        ],
    )


def causal_backward(links, lengths, dx1, do1, qkv1, n1, x, gain_causal, table, blocks, after):
    rows, width = n1.shape
    cols = qkv1.shape[1]
    seqs = lengths.shape[0]
    length = rows // seqs
    n = blocks.count
    split = (2, width // 4, cols)

    def kernel(spot, len_ref, dx1_ref, do_ref, qkv_ref, n1_ref, x_ref, g1_ref, tab_ref, *refs):
        keep_ref, away_ref, gg1_ref, bias_ref, dx_ref, w_ref, dqkv_ref, n1t_ref = refs[n:]
        blocks.put(spot, refs[:n], w_ref)
        tab = tab_ref[...]
        i = lax.broadcasted_iota(jnp.int32, (length, length), 0)
        j = lax.broadcasted_iota(jnp.int32, (length, length), 1)
        flip = jnp.where(i + j == length - 1, 1.0, 0.0).astype(bf16)
        for g in range(KVH):
            lanes = slice(g * PAIR, (g + 1) * PAIR)
            kv_lanes = slice(width + g * PAIR, width + (g + 1) * PAIR)
            even_sum = jnp.zeros((length, length), f32)
            odd_sum = jnp.zeros((length, length), f32)
            for b in range(seqs):
                part = slice(b * length, (b + 1) * length)
                keyval = qkv_ref[part, kv_lanes]
                low = heads_low(qkv_ref[part, lanes])
                high = heads_high(do_ref[part, lanes])
                p = causal_probs(low, keyval, tab, g, length, len_ref[b])
                dp = dot(high, keyval, 1, 1)
                ds = (p * (dp - jnp.sum(p * dp, axis=-1, keepdims=True))).astype(bf16)
                even_sum += dot(flip, ds[:length])
                odd_sum += dot(flip, ds[length:])
                dqkv_ref[part, lanes] = merge_low(dot(ds, keyval)).astype(bf16)
                dqkv_ref[part, kv_lanes] = (
                    dot(ds.T, low) + dot(p.astype(bf16).T, high)
                ).astype(bf16)
            bias_ref[2 * g : 2 * g + 1] = diagonal_sums(even_sum)
            bias_ref[2 * g + 1 : 2 * g + 2] = diagonal_sums(odd_sum)
        dqkv = dqkv_ref[...]
        n1t_ref[...] = n1_ref[...].T
        split_rows(n1t_ref, dqkv, spot[1], keep_ref, away_ref)
        grad_rows, grad_gain = norm_back(
            dot(dqkv, w_ref[...], 1, 1), x_ref[...].astype(f32), g1_ref[...]
        )
        gg1_ref[...] = grad_gain
        dx_ref[...] = (dx1_ref[...] + grad_rows).astype(bf16)

    return call(
        kernel,
        [links.spot, lengths, dx1, do1, qkv1, n1, x, gain_causal, table] + blocks.arrays,
        [smem(), smem(), whole((rows, width)), whole((rows, width)), whole((rows, cols))]
        + [whole((rows, width))] * 2
        + [whole((1, width)), whole(table.shape)]
        + blocks.specs(cols, 0),
        (
            struct(split, bf16),
            struct(split, bf16),
            struct((1, width), f32),
            struct((HEADS, bucket_reach), f32),
            struct((rows, width), bf16),
        ),
        [whole(split)] * 2 + [whole((1, width)), whole((HEADS, bucket_reach)), whole((rows, width))],
        "causal_backward",
        after=after,
        scratch=[
            pltpu.VMEM((width, cols), bf16),
            pltpu.VMEM((rows, cols), bf16),
            pltpu.VMEM((width, rows), bf16),
        ],
    )


def interleave(w_key, w_value):
    r = w_key.shape[0]
    return jnp.concatenate(
        [w_key.reshape(r, KVH, HD), w_value.reshape(r, KVH, HD)], axis=2
    ).reshape(r, KVH * PAIR)


def part_keyval(pair):
    r = pair.shape[0]
    both = pair.reshape(r, KVH, 2, HD)
    return both[:, :, 0].reshape(r, KVH * HD), both[:, :, 1].reshape(r, KVH * HD)


XY = ("lo", "hi")
YX = ("hi", "lo")
EXTRA = 128


def local(
    links,
    inputs,
    memory,
    lengths,
    cotangent,
    causal_query,
    causal_key,
    causal_value,
    causal_out,
    cross_query,
    cross_key,
    cross_value,
    cross_out,
    feed_gate,
    feed_up,
    feed_down,
    gain_causal,
    gain_cross,
    gain_feed,
    bias_table,
):
    links.locate()
    seqs, length, width = inputs.shape
    rows = seqs * length
    r = causal_query.shape[0]
    devices = links.nf * links.nd
    table_part = bias_table.shape[0]
    x = inputs.reshape(rows, width)
    cot = cotangent.reshape(rows, width)

    small = jnp.concatenate(
        [
            gain_causal[:, None],
            gain_cross[:, None],
            gain_feed[:, None],
            jnp.pad(bias_table[:, None], ((0, r - table_part), (0, 0))),
            jnp.zeros((r, EXTRA - 4), bf16),
        ],
        axis=1,
    )
    first_shard = jnp.concatenate([interleave(cross_key, cross_value), small], axis=1)
    causal_shard = jnp.concatenate(
        [causal_query, interleave(causal_key, causal_value), causal_out], axis=1
    )
    second_shard = jnp.concatenate([causal_shard, cross_query, cross_out], axis=1)
    units = feed_gate.shape[1] // links.nf
    feed_wide = jnp.stack(
        [
            jnp.concatenate([w[:, f * units : (f + 1) * units] for w in (feed_gate, feed_up)], axis=1)
            for f in range(links.nf)
        ]
    )

    first_pieces = links.spread_ring(first_shard)
    feed_near = links.quarters(tie(feed_wide, first_pieces[-1])).reshape(4 * r, 2 * units)
    second_pieces = links.spread_ring(second_shard, first_pieces[1:])
    first_blocks = links.grow(jnp.stack(first_pieces), XY)
    cot_core = links.send(tie(cot, first_blocks.arrays[-1]), "core")
    keyval, small_all = project_memory(links, memory, first_blocks)
    feed_pieces = links.spread_ring(feed_near, second_pieces[1:])

    cut = causal_shard.shape[1]
    causal_stack = jnp.stack([p[:, :cut] for p in second_pieces])
    cross_stack = jnp.stack([p[:, cut:] for p in second_pieces])
    causal_blocks = links.grow(causal_stack, XY)
    cross_blocks = links.grow(cross_stack, YX)
    down_pieces = links.spread_ring(feed_down, feed_pieces[1:])
    feed_stack = jnp.stack(feed_pieces)
    feed_far = links.send(tie(feed_stack, cross_blocks.arrays[1]), "lo")
    feed_blocks = Blocks(
        links, [(feed_stack[None], [{}]), (feed_far[None], [{"lo": 1}])], quads=True
    )
    cot_hi = links.send(tie(cot, causal_blocks.arrays[1]), "hi")
    cot_both = links.send(cot_hi, "core")
    cots = (cot, cot_core, cot_hi, cot_both)

    gain_one, gain_two, gain_three = (small_all[i : i + 1] for i in range(3))
    bias_all = small_all[3].reshape(devices, r)[:, :table_part].reshape(HEADS, BUCKETS)
    onehot = jnp.asarray(reversed_buckets())
    table = jnp.dot(bias_all.astype(bf16), onehot.astype(bf16), preferred_element_type=f32)

    x1, n1, qkv1, o1 = causal_forward(
        links, inputs, causal_blocks, gain_one, table, lengths, (keyval,)
    )
    down_stack = jnp.stack(down_pieces)
    down_far = links.send(tie(down_stack, feed_far), "lo")
    n2, q2, o2, x2, n3, probs = cross_forward(links, x1, keyval, cross_blocks, gain_two, gain_three)
    n3_hi = links.send(n3, "hi")
    n3_core = links.send(n3, "core")
    n3_both = links.send(n3_hi, "core")
    n3s = (n3, n3_core, n3_hi, n3_both)
    w_down = assemble(links, down_stack, down_far, (x2,))
    hidden, dgate, dup, dn3, dn3_hi, dn3_away = feed_through(
        links, n3s, cots, feed_blocks, w_down, ()
    )

    def over_four(own, hi, away, after=()):
        got = links.send(tie(away, *after), "core")
        passed = (hi + got[rows:].astype(f32)).astype(bf16)
        return own, got[:rows], links.send(passed, "hi")

    dn3_terms = over_four(dn3, dn3_hi, dn3_away)
    y, y_hi, y_away, grad_gu, grad_down = feed_weight_grads(
        n3s, cots, hidden, dgate, dup, w_down, ()
    )

    def split(a, way_axes):
        return a.reshape(tuple(links.lengths[w] for w in way_axes) + (-1, a.shape[-1]))

    every = ("hi", "core", "ring", "lo")
    apart = ("hi", "ring", "lo")
    feed_sums = Scatter(
        links,
        [
            ([Leaf(split(grad_gu, every), every)], ("lo",)),
            ([Leaf(split(grad_down, ("ring", "lo")), ("ring", "lo"))], ("lo",)),
        ],
    )

    def halves(keep, away, *windows):
        keep, away = split(keep, apart), split(away, apart)
        got = links.send(away, "core")
        return [
            ([Leaf(keep, apart, (), w, i), Leaf(got, apart, (), w, i)], order)
            for w, i, order in windows
        ]

    done = feed_sums.step((y,))
    dx2, do2, keep, away, grad_gain_three = cross_enter(
        links, x2, gain_three, *dn3_terms, cot, o2, cross_blocks, done
    )
    jobs_o2 = halves(keep, away, (width, 0, YX))
    y_terms = over_four(y, y_hi, y_away, (dx2,))
    dq2, grad_keyval = cross_backward(q2, do2, o2, keyval, probs, (dx2,))
    dx1, do1, keep, away, grad_gain_two = causal_enter(
        links, dx2, x1, gain_two, n2, dq2, o1, causal_blocks, cross_blocks, ()
    )
    jobs_o1q2 = halves(keep, away, (width, 0, XY), (width, 1, YX))
    done = feed_sums.spread((dx1,))
    early_sums = Scatter(links, jobs_o2 + jobs_o1q2)
    done = early_sums.step(done)
    keep, away, grad_gain_one, grad_bias, input_grad = causal_backward(
        links, lengths, dx1, do1, qkv1, n1, x, gain_one, table, causal_blocks, done
    )
    jobs_qkv1 = halves(keep, away, (width, 0, XY), (width, 1, YX))
    done = early_sums.step((input_grad,))

    grad_table = lax.dot_general(
        grad_bias, onehot, (((1,), (1,)), ((), ())), precision=lax.Precision.HIGHEST
    )
    table_rows = jnp.pad(
        grad_table.reshape(devices, table_part), ((0, 0), (0, r - table_part))
    ).reshape(1, width)
    small_rows = jnp.concatenate(
        [grad_gain_one, grad_gain_two, grad_gain_three, table_rows, jnp.zeros((4, width), f32)],
        axis=0,
    )
    middle_sums = Scatter(links, jobs_qkv1)
    done = middle_sums.step(done)
    keep, away = keyval_weight_grad(links, memory, grad_keyval, small_rows, done)
    jobs_kv2 = halves(keep, away, (KVH * PAIR + EXTRA, 0, YX))
    late_sums = Scatter(links, jobs_kv2)
    done = early_sums.spread((keep,))
    done = middle_sums.step(done)
    done = late_sums.step(done)
    memory_grad = memory_gradient(links, grad_keyval, first_blocks, done)
    done = middle_sums.spread((memory_grad,))
    done = late_sums.step(done)
    late_sums.spread(done)

    layer_out = (x2 + sum(t.astype(f32) for t in y_terms)).astype(bf16)
    sum_gu, sum_down = feed_sums.results
    sum_o2, sum_o1, sum_q2 = early_sums.results
    sum_q1, sum_kv1 = middle_sums.results
    sum_kv2, sum_small = late_sums.results[0][:, :width], late_sums.results[0][:, width:]
    sum_k1, sum_v1 = part_keyval(sum_kv1)
    sum_k2, sum_v2 = part_keyval(sum_kv2)

    wide = sum_gu.reshape(links.nf, r, 2 * units)
    mine = links.hi * 2 + links.core
    near = [lax.dynamic_index_in_dim(wide, mine, 0, keepdims=False)]
    for flip, way in ((1, "core"), (2, "hi"), (3, "both")):
        theirs = lax.dynamic_index_in_dim(wide, mine ^ flip, 0, keepdims=False).astype(bf16)
        near.append(links.send(theirs, way).astype(f32))
    wide = links.unquarter(jnp.stack(near))
    sum_gate, sum_up = (
        wide[:, :, i * units : (i + 1) * units].transpose(1, 0, 2).reshape(r, links.nf * units)
        for i in range(2)
    )
    return (
        layer_out.reshape(seqs, length, width),
        input_grad.reshape(seqs, length, width),
        memory_grad,
        sum_q1,
        sum_k1,
        sum_v1,
        sum_o1,
        sum_q2,
        sum_k2,
        sum_v2,
        sum_o2,
        sum_gate,
        sum_up,
        sum_down,
        sum_small[:, 0],
        sum_small[:, 1],
        sum_small[:, 2],
        sum_small[:table_part, 3],
    )


def solution(mesh):
    three = P(AXES, None, None)
    two = P(AXES, None)
    one = P(AXES)
    in_specs = (three, three, one, three) + (two,) * 11 + (one,) * 4
    out_specs = (three,) * 3 + (two,) * 11 + (one,) * 4
    body = functools.partial(local, Links(mesh))
    return jax.shard_map(body, mesh=mesh, in_specs=in_specs, out_specs=out_specs, check_vma=False)
```

time: 2720 us -> 593 us (0.22)
  waiting for transfers between devices: 2240 us -> 229 us
  Pallas kernels: 0 us -> 219 us
  matrix products: 189 us -> 0.84 us
  local copies, waits for them, and re-layouts: 151 us -> 35.2 us
  starting transfers between devices: 1.09 us -> 86.9 us
  blocking collectives: 82.7 us -> 0 us
    reduce_scatter x11 -> x0, waiting for transfers between devices: 1730 us -> none  [the longest x1 252 us: local(): lax.psum_scatter(grad_up_w, ('fsdp', 'dp'), scatter_dimension=0, tiled=True)]
    all_gather x11 -> x0, waiting for transfers between devices: 506 us -> none  [the longest x1 64.5 us: local(): lax.all_gather(feed_down, ('fsdp', 'dp'), axis=0, tiled=True)]
    ppermute x0 -> x75, waiting for transfers between devices: none -> 229 us  [send(): return lax.ppermute(a, AXES, self.pairs[way])]
    pallas_call x0 -> x23, Pallas kernels: none -> 219 us  [call(): pl.pallas_call(body, grid_spec=spec, out_shape=out_shape, compiler_params...]
    dot_general x141 -> x2, matrix products: 189 us -> 0.84 us  [the longest x1 0.72 us: local(): jnp.dot(bias_all.astype(bf16), onehot.astype(bf16), preferred_element_typ...]
    ppermute x0 -> x75, starting transfers between devices: none -> 86.9 us  [send(): return lax.ppermute(a, AXES, self.pairs[way])]
    unnamed x2 -> x0, blocking collectives: 82.7 us -> none
    dynamic_slice x64 -> x3, local copies, waits for them, and re-layouts: 36 us -> 0.09 us  [the longest x1 0.05 us: unquarter(): lax.dynamic_index_in_dim(near, mine ^ f, 0, keepdims=False)]
  transfers between devices with their start and end apart: 22 -> 75, of which waited for: 21 -> 26; matrix products, arithmetic and copies ran while one was open for 8% -> 4% of each run, Pallas kernels for 0% -> 35%
where the time goes in v1:
time: 593 us; the launch traced here: 585 us
  waiting for transfers between devices  229 us (39%)
  Pallas kernels  219 us (37%)
  starting transfers between devices  86.9 us (15%)
  local copies, waits for them, and re-layouts  35.2 us (6%)
  other arithmetic  12.6 us (2%)
    ppermute x75, waiting for transfers between devices, send(): return lax.ppermute(a, AXES, self.pairs[way])  229 us
    pallas_call x23, Pallas kernels, call(): pl.pallas_call(body, grid_spec=spec, out_shape=out_shape, compiler_params...  219 us
    ppermute x75, starting transfers between devices, send(): return lax.ppermute(a, AXES, self.pairs[way])  86.9 us
    unnamed x114, local copies, waits for them, and re-layouts  13.8 us
  transfers between devices with their start and end apart: 75, of which 26 were waited for; matrix products, arithmetic and copies ran while one was open for 4% of the time, Pallas kernels for 35%

profile of v1, /device:TPU:0, one launch (start us, length us, event | category | flops | bytes accessed | tf_op | source)
XLA Modules:
  0.0 585.4 jit_solution(15892414013574740122)
XLA Ops:
  5.8 5.1 collective-permute-start.2
  23.5 4.8 collective-permute-done.9
  29.8 18.2 %collective-permute-done.8 = bf16[32,5120]{1,0:T(8,128)(2,1)S(1)} collective-permute-done((bf16[32,5120]{1,0:T(8,128)(2,1)S(1)}, bf16[32,5120]{1,0:T(8,128)(2,1)S(1)}, u32[]{:S(2)}, u32[]{:S(2)}) %collective-permute-start.8) | collective-permute-done | bytes 327712 | tf_op jit(solution)/shard_map/ppermute | solution.py:111
  49.9 18.4 %collective-permute-done.10 = bf16[4,32,3072]{2,1,0:T(8,128)(2,1)S(1)} collective-permute-done((bf16[4,32,3072]{2,1,0:T(8,128)(2,1)S(1)}, bf16[4,32,3072]{2,1,0:T(8,128)(2,1)S(1)}, u32[]{:S(2)}, u32[]{:S(2)}) %collective-permute-start.10) | collective-permute-done | bytes 786464 | tf_op jit(solution)/shard_map/ppermute | solution.py:111
  72.5 44.6 %collective-permute-done.14 = bf16[4,32,2048]{2,1,0:T(8,128)(2,1)S(1)} collective-permute-done((bf16[4,32,2048]{2,1,0:T(8,128)(2,1)S(1)}, bf16[4,32,2048]{2,1,0:T(8,128)(2,1)S(1)}, u32[]{:S(2)}, u32[]{:S(2)}) %collective-permute-start.14) | collective-permute-done | bytes 524320 | tf_op jit(solution)/shard_map/ppermute | solution.py:111
  120.3 13.9 %collective-permute-done.28 = bf16[128,1408]{1,0:T(8,128)(2,1)S(1)} collective-permute-done((bf16[128,1408]{1,0:T(8,128)(2,1)S(1)}, bf16[128,1408]{1,0:T(8,128)(2,1)S(1)}, u32[]{:S(2)}, u32[]{:S(2)}) %collective-permute-start.28) | collective-permute-done | bytes 360480 | tf_op jit(solution)/shard_map/ppermute | solution.py:111
  144.1 15.4 %project_memory.1 = (bf16[2,1024,2048]{2,1,0:T(8,128)(2,1)}, f32[8,1024]{1,0:T(8,128)}) custom-call(s32[4]{0:T(128)} %pad_add_fusion.refs_0_, bf16[2,2048,1024]{2,1,0:T(8,128)(2,1)} %refs_1_.7, bf16[2,4,32,1152]{3,2,1,0:T(8,128)(2,1)} %copy-done.7, bf16[2,4,32,1152]{3,2,1,0:T(8,128)(2,1)} %copy-done.12, bf16[2,4,32,1152]{3,2,1,0:T(8,128)(2,1)} %copy-done.13, ...), custom_call_target="tpu_custom_call" | custom-call | flops 1000 | bytes 1000 | tf_op jit(solution)/shard_map/project_memory/pallas_call | solution.py:57
  162.0 5.1 collective-permute-start.32
  169.3 9.5 %causal_forward.1 = (f32[256,1024]{1,0:T(8,128)}, bf16[256,1024]{1,0:T(8,128)(2,1)}, bf16[256,2048]{1,0:T(8,128)(2,1)}, bf16[256,1024]{1,0:T(8,128)(2,1)}) custom-call(s32[4]{0:T(128)} %pad_add_fusion.refs_0_, s32[2]{0:T(128)} %refs_1_.6, bf16[256,1024]{1,0:T(8,128)(2,1)} %bitcast.145, f32[1,1024]{1,0:T(1,128)} %get-tuple-element.227.refs_3_.refs_7_, ...), custom_call_target="tpu_custom_call" | custom-call | flops 1000 | bytes 1000 | tf_op jit(solution)/shard_map/causal_forward/pallas_call | solution.py:57
  178.8 34.8 %cross_forward.1 = (bf16[256,1024]{1,0:T(8,128)(2,1)}, bf16[256,1024]{1,0:T(8,128)(2,1)}, bf16[256,1024]{1,0:T(8,128)(2,1)}, f32[256,1024]{1,0:T(8,128)}, bf16[2...) custom-call(s32[4]{0:T(128)} %pad_add_fusion.refs_0_, f32[256,1024]{1,0:T(8,128)} %get-tuple-element.104.refs_1_.refs_2_, ...), custom_call_target="tpu_custom_call" | custom-call | flops 1000 | bytes 1000 | tf_op jit(solution)/shard_map/cross_forward/pallas_call | solution.py:57
  214.9 11.3 %collective-permute-done.31 = bf16[88,1024]{1,0:T(8,128)(2,1)S(1)} collective-permute-done((bf16[88,1024]{1,0:T(8,128)(2,1)S(1)}, bf16[88,1024]{1,0:T(8,128)(2,1)S(1)}, u32[]{:S(2)}, u32[]{:S(2)}) %collective-permute-start.31) | collective-permute-done | bytes 180256 | tf_op jit(solution)/shard_map/ppermute | solution.py:111
  228.8 15.7 %collective-permute-done.34.refs_2_ = bf16[4,88,1024]{2,1,0:T(8,128)(2,1)S(1)} collective-permute-done((bf16[4,88,1024]{2,1,0:T(8,128)(2,1)S(1)}, bf16[4,88,1024]{2,1,0:T(8,128)(2,1)S(1)}, u32[]{:S(2)}, u32[]{:S(2)}) %collective-permute-start.34) | collective-permute-done | bytes 720928 | tf_op jit(solution)/shard_map/ppermute | solution.py:111
  249.6 13.8 %feed_through.1 = (bf16[1024,704]{1,0:T(8,128)(2,1)}, bf16[1024,704]{1,0:T(8,128)(2,1)}, bf16[1024,704]{1,0:T(8,128)(2,1)}, f32[256,1024]{1,0:T(8,128)}, f32[256,1024]{1,0:T(8,128)}, /*index=5*/bf16[512,1024]{1,0:T(8,128)(2,1)}) custom-call(s32[4]{0:T(128)} %pad_add_fusion.refs_0_, bf16[256,1024]{1,0:T(8,128)(2,1)} %get-tuple-element.106.refs_1_.refs_0_, ...), custom_call_target="tpu_custom_call" | custom-call | flops 1000 | bytes 1000 | tf_op jit(solution)/shard_map/feed_through/pallas_call | solution.py:57
  269.2 12.3 %feed_weight_grads.1 = (f32[256,1024]{1,0:T(8,128)}, f32[256,1024]{1,0:T(8,128)}, bf16[512,1024]{1,0:T(8,128)(2,1)}, bf16[1024,1408]{1,0:T(8,128)(2,1)}, bf16[704,1024]{1,0:T(8,128)(2,1)}) custom-call(bf16[256,1024]{1,0:T(8,128)(2,1)} %get-tuple-element.106.refs_1_.refs_0_, bf16[256,1024]{1,0:T(8,128)(2,1)} %copy-done.21, bf16[256,1024]{1,0:T(8,128)(2,1)} %copy-done.18, ...), custom_call_target="tpu_custom_call" | custom-call | flops 1000 | bytes 1000 | tf_op jit(solution)/shard_map/feed_weight_grads/pallas_call | solution.py:57
  281.6 4.4 combine.7
  289.1 6.0 %cross_enter.1 = (f32[256,1024]{1,0:T(8,128)}, bf16[256,1024]{1,0:T(8,128)(2,1)}, bf16[2,256,1024]{2,1,0:T(8,128)(2,1)}, bf16[2,256,1024]{2,1,0:T(8,128)(2,1)}, f32[1,1024]{1,0:T(1,128)}) custom-call(s32[4]{0:T(128)} %pad_add_fusion.refs_0_, f32[256,1024]{1,0:T(8,128)} %get-tuple-element.105.refs_3_.refs_1_, f32[1,1024]{1,0:T(1,128)} %get-tuple-element.225.refs_4_.refs_2_, ...), custom_call_target="tpu_custom_call" | custom-call | flops 1000 | bytes 1000 | tf_op jit(solution)/shard_map/cross_enter/pallas_call | solution.py:57
  295.1 25.5 %cross_backward.1 = (bf16[256,1024]{1,0:T(8,128)(2,1)}, bf16[2,1024,2048]{2,1,0:T(8,128)(2,1)}) custom-call(bf16[256,1024]{1,0:T(8,128)(2,1)} %get-tuple-element.130.refs_0_, bf16[256,1024]{1,0:T(8,128)(2,1)} %get-tuple-element.131.refs_1_, bf16[256,1024]{1,0:T(8,128)(2,1)} %get-tuple-element.122.refs_7_.refs_2_, ...), custom_call_target="tpu_custom_call" | custom-call | flops 1000 | bytes 1000 | tf_op jit(solution)/shard_map/cross_backward/pallas_call | solution.py:57
  320.6 8.4 %causal_enter.1 = (f32[256,1024]{1,0:T(8,128)}, bf16[256,1024]{1,0:T(8,128)(2,1)}, bf16[2,256,2048]{2,1,0:T(8,128)(2,1)}, bf16[2,256,2048]{2,1,0:T(8,128)(2,1)}, f32[1,1024]{1,0:T(1,128)}) custom-call(s32[4]{0:T(128)} %pad_add_fusion.refs_0_, f32[256,1024]{1,0:T(8,128)} %get-tuple-element.126.refs_5_.refs_1_, ...), custom_call_target="tpu_custom_call" | custom-call | flops 1000 | bytes 1000 | tf_op jit(solution)/shard_map/causal_enter/pallas_call | solution.py:57
  329.8 17.8 %collective-permute-done.42.refs_4_ = bf16[4,88,1024]{2,1,0:T(8,128)(2,1)S(1)} collective-permute-done((bf16[4,88,1024]{2,1,0:T(8,128)(2,1)S(1)}, bf16[4,88,1024]{2,1,0:T(8,128)(2,1)S(1)}, u32[]{:S(2)}, u32[]{:S(2)}) %collective-permute-start.42) | collective-permute-done | bytes 720928 | tf_op jit(solution)/shard_map/ppermute | solution.py:111
  349.0 4.7 spread.4
  355.7 5.6 collective-permute-done.74
  363.2 7.7 %collective-permute-done.73 = bf16[88,1024]{1,0:T(8,128)(2,1)S(1)} collective-permute-done((bf16[88,1024]{1,0:T(8,128)(2,1)}, bf16[88,1024]{1,0:T(8,128)(2,1)S(1)}, u32[]{:S(2)}, u32[]{:S(2)}) %collective-permute-start.73) | collective-permute-done | bytes 180256 | tf_op jit(solution)/shard_map/ppermute | solution.py:111
  370.9 16.0 %collective-permute-start.66 = (bf16[2,2,32,1408]{3,2,1,0:T(8,128)(2,1)}, bf16[2,2,32,1408]{3,2,1,0:T(8,128)(2,1)S(1)}, u32[]{:S(2)}, u32[]{:S(2)}) collective-permute-start(bf16[2,2,32,1408]{3,2,1,0:T(8,128)(2,1)} %get-tuple-element.177), channel_id=1, source_target_pairs={{0,2},{1,3},{2,4},{3,5},{4,6},{5,7},{6,0},{7,1},{8,10},{9,11},{10,... | collective-permute-start | bytes 1081352 | tf_op jit(solution)/shard_map/ppermute | solution.py:111
  388.7 12.1 %collective-permute-done.67 = bf16[2,2,32,1408]{3,2,1,0:T(8,128)(2,1)S(1)} collective-permute-done((bf16[2,2,32,1408]{3,2,1,0:T(8,128)(2,1)}, bf16[2,2,32,1408]{3,2,1,0:T(8,128)(2,1)S(1)}, u32[]{:S(2)}, u32[]{:S(2)}) %collective-permute-start.67) | collective-permute-done | bytes 360480 | tf_op jit(solution)/shard_map/ppermute | solution.py:111
  402.7 4.7 combine.8
  407.4 15.3 %causal_backward.1 = (bf16[2,256,2048]{2,1,0:T(8,128)(2,1)}, bf16[2,256,2048]{2,1,0:T(8,128)(2,1)}, f32[1,1024]{1,0:T(1,128)}, f32[16,128]{1,0:T(8,128)}, bf16[256,1024]{1,0:T(8,128)(2,1)}) custom-call(s32[4]{0:T(128)} %pad_add_fusion.refs_0_, s32[2]{0:T(128)} %refs_1_.6, f32[256,1024]{1,0:T(8,128)} %get-tuple-element.135.refs_5_.refs_2_, ...), custom_call_target="tpu_custom_call" | custom-call | flops 1000 | bytes 1000 | tf_op jit(solution)/shard_map/causal_backward/pallas_call | solution.py:57
  434.4 10.5 %collective-permute-done.44.refs_3_ = bf16[4,2,32,1024]{3,2,1,0:T(8,128)(2,1)S(1)} collective-permute-done((bf16[4,2,32,1024]{3,2,1,0:T(8,128)(2,1)}, bf16[4,2,32,1024]{3,2,1,0:T(8,128)(2,1)S(1)}, u32[]{:S(2)}, u32[]{:S(2)}) %collective-permute-start.44) | collective-permute-done | bytes 524320 | tf_op jit(solution)/shard_map/ppermute | solution.py:111
  444.9 9.8 %collective-permute-done.46.refs_9_.refs_11_ = bf16[4,2,32,1024]{3,2,1,0:T(8,128)(2,1)} collective-permute-done((bf16[4,2,32,1024]{3,2,1,0:T(8,128)(2,1)}, bf16[4,2,32,1024]{3,2,1,0:T(8,128)(2,1)}, u32[]{:S(2)}, u32[]{:S(2)}) %collective-permute-start.46) | collective-permute-done | bytes 524320 | tf_op jit(solution)/shard_map/ppermute | solution.py:111
  461.9 4.4 combine.10
  466.3 15.5 %keyval_weight_grad.1 = (bf16[2,256,1152]{2,1,0:T(8,128)(2,1)}, bf16[2,256,1152]{2,1,0:T(8,128)(2,1)}) custom-call(s32[4]{0:T(128)} %pad_add_fusion.refs_0_, bf16[2,2048,1024]{2,1,0:T(8,128)(2,1)} %refs_1_.7, bf16[2,1024,2048]{2,1,0:T(8,128)(2,1)} %get-tuple-element.147.refs_2_.refs_1_, f32[8,1024]{1,0:T(8,128)} %concatenate.44.refs_3_, ...), custom_call_target="tpu_custom_call" | custom-call | flops 1000 | bytes 1000 | tf_op jit(solution)/shard_map/keyval_weight_grad/pallas_call | solution.py:57
  488.2 15.8 %collective-permute-done.51.refs_8_ = bf16[4,32,1024]{2,1,0:T(8,128)(2,1)S(1)} collective-permute-done((bf16[4,32,1024]{2,1,0:T(8,128)(2,1)S(1)}, bf16[4,32,1024]{2,1,0:T(8,128)(2,1)S(1)}, u32[]{:S(2)}, u32[]{:S(2)}) %collective-permute-start.51) | collective-permute-done | bytes 262176 | tf_op jit(solution)/shard_map/ppermute | solution.py:111
  531.0 14.6 %memory_gradient.1.refs_9_ = bf16[2,2048,1024]{2,1,0:T(8,128)(2,1)} custom-call(s32[4]{0:T(128)} %pad_add_fusion.refs_0_, bf16[2,1024,2048]{2,1,0:T(8,128)(2,1)} %get-tuple-element.147.refs_2_.refs_1_, bf16[2,4,32,1152]{3,2,1,0:T(8,128)(2,1)} %copy-done.7, bf16[2,4,32,1152]{3,2,1,0:T(8,128)(2,1)} %copy-done.12, bf16[2,4,32,1152]{3,2,1,0:T(8,128)(2,1)} %copy-done.13, ...), custom_call_target="tpu_custom_call" | custom-call | flops 1000 | bytes 1000 | tf_op jit(solution)/shard_map/memory_gradient/pallas_call | solution.py:57
  (339 shorter events, 161.7 us)
Async XLA Ops:
  19.9 28.2 %collective-permute-start.8 = (bf16[32,5120]{1,0:T(8,128)(2,1)S(1)}, bf16[32,5120]{1,0:T(8,128)(2,1)S(1)}, u32[]{:S(2)}, u32[]{:S(2)}) collective-permute-start(bf16[32,5120]{1,0:T(8,128)(2,1)S(1)} %constant_dynamic-update-slice_fusion), channel_id=1, source_target_pairs={{0,4},{1,5},{2,6},{3,7},{4,0},{5,1},{6,2},{7,3},{8,12},{9,13},{10,... | collective-permute-start | bytes 983048 | tf_op jit(solution)/shard_map/ppermute | solution.py:111
  19.9 28.2 %collective-permute-start.7 = (bf16[32,5120]{1,0:T(8,128)(2,1)S(1)}, bf16[32,5120]{1,0:T(8,128)(2,1)S(1)}, u32[]{:S(2)}, u32[]{:S(2)}) collective-permute-start(bf16[32,5120]{1,0:T(8,128)(2,1)S(1)} %constant_dynamic-update-slice_fusion), channel_id=1, source_target_pairs={{0,2},{1,3},{2,4},{3,5},{4,6},{5,7},{6,0},{7,1},{8,10},{9,11},{10,... | collective-permute-start | bytes 983048 | tf_op jit(solution)/shard_map/ppermute | solution.py:111
  21.9 48.9 %collective-permute-start.3 = (bf16[4,32,1152]{2,1,0:T(8,128)(2,1)S(1)}, bf16[4,32,1152]{2,1,0:T(8,128)(2,1)S(1)}, u32[]{:S(2)}, u32[]{:S(2)}) collective-permute-start(bf16[4,32,1152]{2,1,0:T(8,128)(2,1)S(1)} %get-tuple-element.214), channel_id=1, source_target_pairs={{0,1},{1,0},{2,3},{3,2},{4,5},{5,4},{6,7},{7,6},{8,9},{9,8},{10,11... | collective-permute-start | bytes 884744 | tf_op jit(solution)/shard_map/ppermute | solution.py:111
  23.5 46.7 %collective-permute-start.26 = (bf16[32,1408]{1,0:T(8,128)(2,1)S(1)}, bf16[32,1408]{1,0:T(8,128)(2,1)S(1)}, u32[]{:S(2)}, u32[]{:S(2)}) collective-permute-start(bf16[32,1408]{1,0:T(8,128)(2,1)S(1)} %get-tuple-element.210), channel_id=1, source_target_pairs={{0,24},{1,25},{2,26},{3,27},{4,28},{5,29},{6,30},{7,31},{8,16},{9,... | collective-permute-start | bytes 270344 | tf_op jit(solution)/shard_map/ppermute | solution.py:111
  28.3 42.4 %collective-permute-start.25 = (bf16[32,1408]{1,0:T(8,128)(2,1)S(1)}, bf16[32,1408]{1,0:T(8,128)(2,1)S(1)}, u32[]{:S(2)}, u32[]{:S(2)}) collective-permute-start(bf16[32,1408]{1,0:T(8,128)(2,1)S(1)} %get-tuple-element.211), channel_id=1, source_target_pairs={{0,16},{1,17},{2,18},{3,19},{4,20},{5,21},{6,22},{7,23},{8,24},{9,... | collective-permute-start | bytes 270344 | tf_op jit(solution)/shard_map/ppermute | solution.py:111
  68.5 66.4 %collective-permute-start.11 = (bf16[2,4,32,3072]{3,2,1,0:T(8,128)(2,1)S(1)}, bf16[2,4,32,3072]{3,2,1,0:T(8,128)(2,1)}, u32[]{:S(2)}, u32[]{:S(2)}) collective-permute-start(bf16[2,4,32,3072]{3,2,1,0:T(8,128)(2,1)S(1)} %pad_maximum_fusion.refs_5_.refs_7_.refs_9_), channel_id=1, source_target_pairs={{0,16},{1,17},{2,18},{3,19},{4,20},{5,21},{6,22},{7,23},{8,24},{9,... | collective-permute-start | bytes 4718600 | tf_op jit(solution)/shard_map/ppermute | solution.py:111
  70.1 46.9 %collective-permute-start.14 = (bf16[4,32,2048]{2,1,0:T(8,128)(2,1)S(1)}, bf16[4,32,2048]{2,1,0:T(8,128)(2,1)S(1)}, u32[]{:S(2)}, u32[]{:S(2)}) collective-permute-start(bf16[4,32,2048]{2,1,0:T(8,128)(2,1)S(1)} %get-tuple-element.205), channel_id=1, source_target_pairs={{0,16},{1,17},{2,18},{3,19},{4,20},{5,21},{6,22},{7,23},{8,24},{9,... | collective-permute-start | bytes 1572872 | tf_op jit(solution)/shard_map/ppermute | solution.py:111
  70.9 63.9 %collective-permute-start.4 = (bf16[2,4,32,1152]{3,2,1,0:T(8,128)(2,1)S(1)}, bf16[2,4,32,1152]{3,2,1,0:T(8,128)(2,1)S(1)}, u32[]{:S(2)}, u32[]{:S(2)}) collective-permute-start(bf16[2,4,32,1152]{3,2,1,0:T(8,128)(2,1)S(1)} %pad_maximum_fusion.7.refs_2_), channel_id=1, source_target_pairs={{0,16},{1,17},{2,18},{3,19},{4,20},{5,21},{6,22},{7,23},{8,24},{9,... | collective-permute-start | bytes 1769480 | tf_op jit(solution)/shard_map/ppermute | solution.py:111
  72.5 47.4 %collective-permute-start.27 = (bf16[128,1408]{1,0:T(8,128)(2,1)S(1)}, bf16[128,1408]{1,0:T(8,128)(2,1)S(1)}, u32[]{:S(2)}, u32[]{:S(2)}) collective-permute-start(bf16[128,1408]{1,0:T(8,128)(2,1)S(1)} %bitcast.149), channel_id=1, source_target_pairs={{0,2},{1,3},{2,4},{3,5},{4,6},{5,7},{6,0},{7,1},{8,10},{9,11},{10,... | collective-permute-start | bytes 1081352 | tf_op jit(solution)/shard_map/ppermute | solution.py:111
  117.2 22.8 %collective-permute-start.15 = (bf16[2,4,32,2048]{3,2,1,0:T(8,128)(2,1)S(1)}, bf16[2,4,32,2048]{3,2,1,0:T(8,128)(2,1)}, u32[]{:S(2)}, u32[]{:S(2)}) collective-permute-start(bf16[2,4,32,2048]{3,2,1,0:T(8,128)(2,1)S(1)} %pad_maximum_fusion.2.refs_5_.refs_8_.refs_11_), channel_id=1, source_target_pairs={{0,1},{1,0},{2,3},{3,2},{4,5},{5,4},{6,7},{7,6},{8,9},{9,8},{10,11... | collective-permute-start | bytes 3145736 | tf_op jit(solution)/shard_map/ppermute | solution.py:111
  134.2 27.7 %collective-permute-start.12 = (bf16[2,4,32,3072]{3,2,1,0:T(8,128)(2,1)S(1)}, bf16[2,4,32,3072]{3,2,1,0:T(8,128)(2,1)}, u32[]{:S(2)}, u32[]{:S(2)}) collective-permute-start(bf16[2,4,32,3072]{3,2,1,0:T(8,128)(2,1)S(1)} %pad_maximum_fusion.refs_5_.refs_7_.refs_9_), channel_id=1, source_target_pairs={{0,8},{1,9},{2,10},{3,11},{4,12},{5,13},{6,14},{7,15},{8,0},{9,1},... | collective-permute-start | bytes 4718600 | tf_op jit(solution)/shard_map/ppermute | solution.py:111
  134.8 32.9 %collective-permute-start.13 = (bf16[2,4,32,3072]{3,2,1,0:T(8,128)(2,1)}, bf16[2,4,32,3072]{3,2,1,0:T(8,128)(2,1)}, u32[]{:S(2)}, u32[]{:S(2)}) collective-permute-start(bf16[2,4,32,3072]{3,2,1,0:T(8,128)(2,1)} %collective-permute-done.11.refs_6_.refs_8_.refs_10_), channel_id=1, source_target_pairs={{0,8},{1,9},{2,10},{3,11},{4,12},{5,13},{6,14},{7,15},{8,0},{9,1},... | collective-permute-start | bytes 4718600 | tf_op jit(solution)/shard_map/ppermute | solution.py:111
  140.0 86.3 %collective-permute-start.33 = (bf16[4,128,1408]{2,1,0:T(8,128)(2,1)}, bf16[4,128,1408]{2,1,0:T(8,128)(2,1)}, u32[]{:S(2)}, u32[]{:S(2)}) collective-permute-start(bf16[4,128,1408]{2,1,0:T(8,128)(2,1)} %get-tuple-element.112), channel_id=1, source_target_pairs={{0,1},{1,0},{2,3},{3,2},{4,5},{5,4},{6,7},{7,6},{8,9},{9,8},{10,11... | collective-permute-start | bytes 4325384 | tf_op jit(solution)/shard_map/ppermute | solution.py:111
  141.8 37.0 %collective-permute-start.16 = (bf16[2,4,32,2048]{3,2,1,0:T(8,128)(2,1)S(1)}, bf16[2,4,32,2048]{3,2,1,0:T(8,128)(2,1)}, u32[]{:S(2)}, u32[]{:S(2)}) collective-permute-start(bf16[2,4,32,2048]{3,2,1,0:T(8,128)(2,1)S(1)} %pad_maximum_fusion.2.refs_5_.refs_8_.refs_11_), channel_id=1, source_target_pairs={{0,8},{1,9},{2,10},{3,11},{4,12},{5,13},{6,14},{7,15},{8,0},{9,1},... | collective-permute-start | bytes 3145736 | tf_op jit(solution)/shard_map/ppermute | solution.py:111
  143.5 35.3 %collective-permute-start.17 = (bf16[2,4,32,2048]{3,2,1,0:T(8,128)(2,1)}, bf16[2,4,32,2048]{3,2,1,0:T(8,128)(2,1)}, u32[]{:S(2)}, u32[]{:S(2)}) collective-permute-start(bf16[2,4,32,2048]{3,2,1,0:T(8,128)(2,1)} %collective-permute-done.15.refs_6_.refs_9_.refs_12_), channel_id=1, source_target_pairs={{0,8},{1,9},{2,10},{3,11},{4,12},{5,13},{6,14},{7,15},{8,0},{9,1},... | collective-permute-start | bytes 3145736 | tf_op jit(solution)/shard_map/ppermute | solution.py:111
  162.0 52.2 %collective-permute-start.32 = (bf16[88,1024]{1,0:T(8,128)(2,1)S(1)}, bf16[88,1024]{1,0:T(8,128)(2,1)S(1)}, u32[]{:S(2)}, u32[]{:S(2)}) collective-permute-start(bf16[88,1024]{1,0:T(8,128)(2,1)S(1)} %copy-done.44), channel_id=1, source_target_pairs={{0,6},{1,7},{2,0},{3,1},{4,2},{5,3},{6,4},{7,5},{8,14},{9,15},{10,... | collective-permute-start | bytes 540680 | tf_op jit(solution)/shard_map/ppermute | solution.py:111
  167.8 59.9 %collective-permute-start.22 = (bf16[256,1024]{1,0:T(8,128)(2,1)S(1)}, bf16[256,1024]{1,0:T(8,128)(2,1)S(1)}, u32[]{:S(2)}, u32[]{:S(2)}) collective-permute-start(bf16[256,1024]{1,0:T(8,128)(2,1)S(1)} %bitcast.143), channel_id=1, source_target_pairs={{0,16},{1,17},{2,18},{3,19},{4,20},{5,21},{6,22},{7,23},{8,24},{9,... | collective-permute-start | bytes 1572872 | tf_op jit(solution)/shard_map/ppermute | solution.py:111
  286.0 61.6 %collective-permute-start.41 = (bf16[2,2,4,32,1408]{4,3,2,1,0:T(8,128)(2,1)}, bf16[2,2,4,32,1408]{4,3,2,1,0:T(8,128)(2,1)S(1)}, u32[]{:S(2)}, u32[]{:S(2)}) collective-permute-start(bf16[2,2,4,32,1408]{4,3,2,1,0:T(8,128)(2,1)} %get-tuple-element.125.refs_12_), channel_id=1, source_target_pairs={{0,1},{1,0},{2,3},{3,2},{4,5},{5,4},{6,7},{7,6},{8,9},{9,8},{10,11... | collective-permute-start | bytes 4325384 | tf_op jit(solution)/shard_map/ppermute | solution.py:111
  329.1 71.9 %collective-permute-start.40 = (bf16[2,4,2,32,2048]{4,3,2,1,0:T(8,128)(2,1)}, bf16[2,4,2,32,2048]{4,3,2,1,0:T(8,128)(2,1)S(1)}, u32[]{:S(2)}, u32[]{:S(2)}) collective-permute-start(bf16[2,4,2,32,2048]{4,3,2,1,0:T(8,128)(2,1)} %bitcast.182), channel_id=1, source_target_pairs={{0,8},{1,9},{2,10},{3,11},{4,12},{5,13},{6,14},{7,15},{8,0},{9,1},... | collective-permute-start | bytes 6291464 | tf_op jit(solution)/shard_map/ppermute | solution.py:111
  355.7 45.2 %collective-permute-start.39 = (bf16[2,4,2,32,1024]{4,3,2,1,0:T(8,128)(2,1)S(1)}, bf16[2,4,2,32,1024]{4,3,2,1,0:T(8,128)(2,1)S(1)}, u32[]{:S(2)}, u32[]{:S(2)}) collective-permute-start(bf16[2,4,2,32,1024]{4,3,2,1,0:T(8,128)(2,1)S(1)} %bitcast.185), channel_id=1, source_target_pairs={{0,8},{1,9},{2,10},{3,11},{4,12},{5,13},{6,14},{7,15},{8,0},{9,1},... | collective-permute-start | bytes 3145736 | tf_op jit(solution)/shard_map/ppermute | solution.py:111
  361.3 27.4 %collective-permute-start.68 = (bf16[2,2,32,1408]{3,2,1,0:T(8,128)(2,1)}, bf16[2,2,32,1408]{3,2,1,0:T(8,128)(2,1)S(1)}, u32[]{:S(2)}, u32[]{:S(2)}) collective-permute-start(bf16[2,2,32,1408]{3,2,1,0:T(8,128)(2,1)} %get-tuple-element.179), channel_id=1, source_target_pairs={{0,6},{1,7},{2,0},{3,1},{4,2},{5,3},{6,4},{7,5},{8,14},{9,15},{10,... | collective-permute-start | bytes 1081352 | tf_op jit(solution)/shard_map/ppermute | solution.py:111
  370.9 29.9 %collective-permute-start.67 = (bf16[2,2,32,1408]{3,2,1,0:T(8,128)(2,1)}, bf16[2,2,32,1408]{3,2,1,0:T(8,128)(2,1)S(1)}, u32[]{:S(2)}, u32[]{:S(2)}) collective-permute-start(bf16[2,2,32,1408]{3,2,1,0:T(8,128)(2,1)} %get-tuple-element.178), channel_id=1, source_target_pairs={{0,4},{1,5},{2,6},{3,7},{4,0},{5,1},{6,2},{7,3},{8,12},{9,13},{10,... | collective-permute-start | bytes 1081352 | tf_op jit(solution)/shard_map/ppermute | solution.py:111
  370.9 29.9 %collective-permute-start.66 = (bf16[2,2,32,1408]{3,2,1,0:T(8,128)(2,1)}, bf16[2,2,32,1408]{3,2,1,0:T(8,128)(2,1)S(1)}, u32[]{:S(2)}, u32[]{:S(2)}) collective-permute-start(bf16[2,2,32,1408]{3,2,1,0:T(8,128)(2,1)} %get-tuple-element.177), channel_id=1, source_target_pairs={{0,2},{1,3},{2,4},{3,5},{4,6},{5,7},{6,0},{7,1},{8,10},{9,11},{10,... | collective-permute-start | bytes 1081352 | tf_op jit(solution)/shard_map/ppermute | solution.py:111
  388.7 93.2 %collective-permute-start.37 = (bf16[512,1024]{1,0:T(8,128)(2,1)}, bf16[512,1024]{1,0:T(8,128)(2,1)}, u32[]{:S(2)}, u32[]{:S(2)}) collective-permute-start(bf16[512,1024]{1,0:T(8,128)(2,1)} %get-tuple-element.127), channel_id=1, source_target_pairs={{0,8},{1,9},{2,10},{3,11},{4,12},{5,13},{6,14},{7,15},{8,0},{9,1},... | collective-permute-start | bytes 3145736 | tf_op jit(solution)/shard_map/ppermute | solution.py:111
  422.7 37.8 %collective-permute-start.43 = (bf16[2,4,2,32,2048]{4,3,2,1,0:T(8,128)(2,1)}, bf16[2,4,2,32,2048]{4,3,2,1,0:T(8,128)(2,1)S(1)}, u32[]{:S(2)}, u32[]{:S(2)}) collective-permute-start(bf16[2,4,2,32,2048]{4,3,2,1,0:T(8,128)(2,1)} %bitcast.183), channel_id=1, source_target_pairs={{0,8},{1,9},{2,10},{3,11},{4,12},{5,13},{6,14},{7,15},{8,0},{9,1},... | collective-permute-start | bytes 6291464 | tf_op jit(solution)/shard_map/ppermute | solution.py:111
  431.8 22.9 %collective-permute-start.46 = (bf16[4,2,32,1024]{3,2,1,0:T(8,128)(2,1)}, bf16[4,2,32,1024]{3,2,1,0:T(8,128)(2,1)}, u32[]{:S(2)}, u32[]{:S(2)}) collective-permute-start(bf16[4,2,32,1024]{3,2,1,0:T(8,128)(2,1)} %get-tuple-element.155), channel_id=1, source_target_pairs={{0,16},{1,17},{2,18},{3,19},{4,20},{5,21},{6,22},{7,23},{8,24},{9,... | collective-permute-start | bytes 1572872 | tf_op jit(solution)/shard_map/ppermute | solution.py:111
  459.0 27.6 %collective-permute-start.50 = (bf16[4,32,1024]{2,1,0:T(8,128)(2,1)}, bf16[4,32,1024]{2,1,0:T(8,128)(2,1)S(1)}, u32[]{:S(2)}, u32[]{:S(2)}) collective-permute-start(bf16[4,32,1024]{2,1,0:T(8,128)(2,1)} %get-tuple-element.156.refs_5_), channel_id=1, source_target_pairs={{0,1},{1,0},{2,3},{3,2},{4,5},{5,4},{6,7},{7,6},{8,9},{9,8},{10,11... | collective-permute-start | bytes 786440 | tf_op jit(solution)/shard_map/ppermute | solution.py:111
  481.8 42.2 %collective-permute-start.47 = (bf16[2,4,2,32,1152]{4,3,2,1,0:T(8,128)(2,1)}, bf16[2,4,2,32,1152]{4,3,2,1,0:T(8,128)(2,1)S(1)}, u32[]{:S(2)}, u32[]{:S(2)}) collective-permute-start(bf16[2,4,2,32,1152]{4,3,2,1,0:T(8,128)(2,1)} %bitcast.184), channel_id=1, source_target_pairs={{0,8},{1,9},{2,10},{3,11},{4,12},{5,13},{6,14},{7,15},{8,0},{9,1},... | collective-permute-start | bytes 3538952 | tf_op jit(solution)/shard_map/ppermute | solution.py:111
  483.9 30.2 %collective-permute-start.38 = (bf16[256,1024]{1,0:T(8,128)(2,1)}, bf16[256,1024]{1,0:T(8,128)(2,1)}, u32[]{:S(2)}, u32[]{:S(2)}) collective-permute-start(bf16[256,1024]{1,0:T(8,128)(2,1)} %add_convert_fusion.1), channel_id=1, source_target_pairs={{0,16},{1,17},{2,18},{3,19},{4,20},{5,21},{6,22},{7,23},{8,24},{9,... | collective-permute-start | bytes 1572872 | tf_op jit(solution)/shard_map/ppermute | solution.py:111
  486.0 28.2 %collective-permute-start.48 = (bf16[2,4,32,1024]{3,2,1,0:T(8,128)(2,1)S(1)}, bf16[2,4,32,1024]{3,2,1,0:T(8,128)(2,1)S(1)}, u32[]{:S(2)}, u32[]{:S(2)}) collective-permute-start(bf16[2,4,32,1024]{3,2,1,0:T(8,128)(2,1)S(1)} %copy-done.31), channel_id=1, source_target_pairs={{0,1},{1,0},{2,3},{3,2},{4,5},{5,4},{6,7},{7,6},{8,9},{9,8},{10,11... | collective-permute-start | bytes 1572872 | tf_op jit(solution)/shard_map/ppermute | solution.py:111
  522.7 22.9 %collective-permute-start.53 = (bf16[4,32,1024]{2,1,0:T(8,128)(2,1)}, bf16[4,32,1024]{2,1,0:T(8,128)(2,1)S(1)}, u32[]{:S(2)}, u32[]{:S(2)}) collective-permute-start(bf16[4,32,1024]{2,1,0:T(8,128)(2,1)} %get-tuple-element.164.refs_3_), channel_id=1, source_target_pairs={{0,16},{1,17},{2,18},{3,19},{4,20},{5,21},{6,22},{7,23},{8,24},{9,... | collective-permute-start | bytes 786440 | tf_op jit(solution)/shard_map/ppermute | solution.py:111
  529.6 26.4 %collective-permute-start.61 = (bf16[4,2,32,1152]{3,2,1,0:T(8,128)(2,1)}, bf16[4,2,32,1152]{3,2,1,0:T(8,128)(2,1)S(1)}, u32[]{:S(2)}, u32[]{:S(2)}) collective-permute-start(bf16[4,2,32,1152]{3,2,1,0:T(8,128)(2,1)} %combine.12.refs_6_), channel_id=1, source_target_pairs={{0,16},{1,17},{2,18},{3,19},{4,20},{5,21},{6,22},{7,23},{8,24},{9,... | collective-permute-start | bytes 1769480 | tf_op jit(solution)/shard_map/ppermute | solution.py:111
  (97 other events, 1165.3 us)

commit v2 on v1

--- a/solution.py
+++ b/solution.py
@@ -20,6 +20,7 @@
 f32 = jnp.float32
 bf16 = jnp.bfloat16
 VMEM_LIMIT = 56 * 1024 * 1024
+PLAN = 2e9
 
 
 def reversed_buckets():
@@ -39,7 +40,7 @@
     return lax.dot_general(a, b, (((ca,), (cb,)), ((), ())), preferred_element_type=f32)
 
 
-def call(kernel, ins, in_specs, out_shape, out_specs, name, after=(), grid=(1,), scratch=(), prefetch=None):
+def call(kernel, ins, in_specs, out_shape, out_specs, name, after=(), grid=(1,), scratch=(), prefetch=None, micros=1):
     lead = 0 if prefetch is None else 1
     n = lead + len(ins)
 
@@ -59,7 +60,9 @@
         grid_spec=spec,
         out_shape=out_shape,
         compiler_params=pltpu.CompilerParams(vmem_limit_bytes=VMEM_LIMIT),
-        cost_estimate=pl.CostEstimate(flops=1000, bytes_accessed=1000, transcendentals=0),
+        cost_estimate=pl.CostEstimate(
+            flops=int(micros * PLAN), bytes_accessed=1000, transcendentals=0
+        ),
         name=name,
     )(*front, *ins, *after)
 
@@ -77,125 +80,120 @@
 
 
 class Links:
-    names = ("hi", "core", "ring", "lo")
-
     def __init__(self, mesh):
         nf, nd = mesh.shape["fsdp"], mesh.shape["dp"]
         self.nf, self.nd, self.size = nf, nd, nd // 2
-        size = self.size
-        self.lengths = {"hi": nf // 2, "core": 2, "ring": size, "lo": 2}
+        self.bits = tuple(f"z{b}" for b in reversed(range(self.size.bit_length() - 1)))
+        self.names = ("hi", "core", "ring", "lo") + self.bits
         spots = [(f, d) for f in range(nf) for d in range(nd)]
 
-        def pairs(move):
-            out = []
-            for f, d in spots:
-                g, e = move(f, d)
-                out.append((f * nd + d, g * nd + e))
-            return out
-
-        self.pairs = {
-            "core": pairs(lambda f, d: (f ^ 1, d)),
-            "hi": pairs(lambda f, d: (f ^ 2, d)),
-            "both": pairs(lambda f, d: (f ^ 3, d)),
-            "lo": pairs(lambda f, d: (f, d ^ 1)),
-        }
-        for s in range(1, size):
-            self.pairs[s] = pairs(lambda f, d: (f, ((d // 2 + s) % size) * 2 + d % 2))
+        def pairs(flip_f, flip_d):
+            return [(f * nd + d, (f ^ flip_f) * nd + (d ^ flip_d)) for f, d in spots]
+
+        self.pairs = {"core": pairs(1, 0), "hi": pairs(2, 0), "both": pairs(3, 0), "lo": pairs(0, 1)}
+        self.masks = {}
+        for name in self.bits:
+            self.masks[name] = 1 << int(name[1:])
+            self.pairs[name] = pairs(0, 2 << int(name[1:]))
 
     def locate(self):
         f, d = lax.axis_index("fsdp"), lax.axis_index("dp")
         self.hi, self.core, self.ring, self.lo = f // 2, f % 2, d // 2, d % 2
-        self.spot = jnp.stack([self.hi, self.core, self.ring, self.lo]).astype(jnp.int32)
-
-    def send(self, a, way):
-        return lax.ppermute(a, AXES, self.pairs[way])
-
-    def spread_ring(self, shard, after=()):
-        return [shard] + [self.send(tie(shard, *after), s) for s in range(1, self.size)]
-
-    def quarters(self, wide):
+        zs = [(self.ring // self.masks[name]) % 2 for name in self.bits]
+        self.spot = jnp.stack([self.hi, self.core, self.ring, self.lo, *zs]).astype(jnp.int32)
+
+    def send(self, a, way, *after):
+        return lax.ppermute(tie(a, *after), AXES, self.pairs[way])
+
+    def grow(self, held, ways, *after, then=()):
+        array, fars = held
+        for way in ways:
+            got = self.send(array, way, *after)
+            after = ()
+            array = jnp.concatenate([tie(array, *then), got], axis=0)
+            fars = fars + [f | {way} for f in fars]
+        return array, fars
+
+    def quarters(self, wide, *after):
         mine = self.hi * 2 + self.core
         out = [lax.dynamic_index_in_dim(wide, mine, 0, keepdims=False)]
         for flip, way in ((1, "core"), (2, "hi"), (3, "both")):
             theirs = lax.dynamic_index_in_dim(wide, mine ^ flip, 0, keepdims=False)
-            out.append(self.send(theirs, way))
-        return jnp.stack(out)
-
-    def unquarter(self, near):
+            out.append(self.send(theirs, way, *after))
+        return jnp.concatenate(out, axis=0)
+
+    def unquarter(self, wide, after):
+        _, _, r, c = wide.shape
+        wide = wide.reshape(self.nf, r, c)
         mine = self.hi * 2 + self.core
-        return jnp.stack(
-            [lax.dynamic_index_in_dim(near, mine ^ f, 0, keepdims=False) for f in range(self.nf)]
-        )
-
-    def grow(self, stack, order, first=(), second=(), third=()):
-        one, two = order
-        got = self.send(tie(stack, *first), one)
-        pair = jnp.stack([stack, got])
-        far = self.send(tie(pair, *second), two)
-        near_far = [{}, {one: 1}]
-        entries = [(pair, near_far), (far, [{**f, two: 1} for f in near_far])]
-        for array, fars in list(entries):
-            entries.append(
-                (self.send(tie(array, *third), "core"), [{**f, "core": 1} for f in fars])
-            )
-        return Blocks(self, entries)
+        near = [tie(lax.dynamic_index_in_dim(wide, mine, 0, keepdims=False), *after)]
+        for flip, way in ((1, "core"), (2, "hi"), (3, "both")):
+            theirs = lax.dynamic_index_in_dim(wide, mine ^ flip, 0, keepdims=False).astype(bf16)
+            near.append(tie(self.send(theirs, way), *after).astype(f32))
+        near = jnp.stack(near)
+        return [lax.dynamic_index_in_dim(near, mine ^ f, 0, keepdims=False) for f in range(self.nf)]
 
 
 class Blocks:
-    def __init__(self, links, entries, quads=False):
+    def __init__(self, links, *helds, quads=False):
         self.links = links
-        self.arrays = [a for a, _ in entries]
-        self.fars = [f for _, f in entries]
+        self.arrays = [a for a, _ in helds]
+        self.fars = [f for _, f in helds]
         self.quads = quads
-        _, _, self.r, self.c = self.arrays[0].shape
-        self.count = len(entries)
+        _, self.r, self.c = self.arrays[0].shape
+        self.count = len(helds)
 
     def specs(self, width=None, index=0):
         return [
-            pl.BlockSpec((*a.shape[:3], width or self.c), lambda *_: (0, 0, 0, index))
+            pl.BlockSpec((*a.shape[:2], width or self.c), lambda *_: (0, 0, index))
             for a in self.arrays
         ]
 
     def put(self, spot, refs, *outs):
-        size = self.links.size
         quads = [(0, 0), (0, 1), (1, 0), (1, 1)] if self.quads else [None]
         r = self.r // len(quads)
         for ref, fars in zip(refs, self.fars):
             for i, far in enumerate(fars):
-                at_lo = 1 - spot[3] if far.get("lo") else spot[3]
-                for t in range(size):
-                    at_ring = lax.rem(spot[2] + (size - t), size)
-                    for q, quad in enumerate(quads):
-                        far_hi, far_core = quad or (far.get("hi"), far.get("core"))
-                        at_hi = 1 - spot[0] if far_hi else spot[0]
-                        at_core = 1 - spot[1] if far_core else spot[1]
-                        row = (((at_hi * 2 + at_core) * size + at_ring) * 2 + at_lo) * r
-                        rows = pl.ds(pl.multiple_of(row, r), r)
-                        left = 0
-                        for out in outs:
-                            width = out.shape[-1]
-                            out[rows, :] = ref[i, t, q * r : (q + 1) * r, left : left + width]
-                            left += width
+                for q, quad in enumerate(quads):
+                    far_hi, far_core = quad or ("hi" in far, "core" in far)
+                    at_hi = 1 - spot[0] if far_hi else spot[0]
+                    at_core = 1 - spot[1] if far_core else spot[1]
+                    row = ((at_hi * 2 + at_core) * self.links.nd + place_of(self.links, spot, far)) * r
+                    rows = pl.ds(pl.multiple_of(row, r), r)
+                    left = 0
+                    for out in outs:
+                        width = out.shape[-1]
+                        out[rows, :] = ref[i, q * r : (q + 1) * r, left : left + width]
+                        left += width
+
+
+def place_of(links, spot, far):
+    mask = sum(links.masks[name] for name in links.bits if name in far)
+    at_ring = jnp.bitwise_xor(spot[2], mask) if mask else spot[2]
+    at_lo = 1 - spot[3] if "lo" in far else spot[3]
+    return at_ring * 2 + at_lo
 
 
 def tie(x, *after):
     return lax.optimization_barrier((x, *after))[0] if after else x
 
 
-def assemble(links, near, far, after=()):
-    size = links.size
-    _, r, c = near.shape
-
-    def kernel(spot, near_ref, far_ref, out, held, sems_in, sems_out):
+def assemble(links, helds, after=()):
+    _, r, c = helds[0][0].shape
+    n = len(helds)
+    most = max(len(f) for _, f in helds)
+
+    def kernel(spot, *refs):
+        out, held, sems_in, sems_out = refs[n:]
         copies = []
-        for k, ref in enumerate((near_ref, far_ref)):
-            at_lo = 1 - spot[3] if k else spot[3]
-            for t in range(size):
-                at_ring = lax.rem(spot[2] + (size - t), size)
+        for k, (ref, (_, fars)) in enumerate(zip(refs, helds)):
+            for i, far in enumerate(fars):
                 copies.append(
                     (
-                        pltpu.make_async_copy(ref.at[t], held.at[k, t], sems_in.at[k, t]),
-                        pltpu.make_async_copy(held.at[k, t], out.at[at_ring, at_lo], sems_out.at[k, t]),
+                        pltpu.make_async_copy(ref.at[i], held.at[k, i], sems_in.at[k, i]),
+                        pltpu.make_async_copy(
+                            held.at[k, i], out.at[place_of(links, spot, far)], sems_out.at[k, i]
+                        ),
                     )
                 )
         for one, _ in copies:
@@ -208,158 +206,122 @@
 
     out = call(
         kernel,
-        [links.spot, near, far],
-        [smem()] + [pl.BlockSpec(memory_space=pl.ANY)] * 2,
-        struct((size, 2, r, c), bf16),
+        [links.spot] + [a for a, _ in helds],
+        [smem()] + [pl.BlockSpec(memory_space=pl.ANY)] * n,
+        struct((links.nd, r, c), bf16),
         pl.BlockSpec(memory_space=pl.ANY),
         "assemble",
+        micros=3,
         after=after,
         scratch=[
-            pltpu.VMEM((2, size, r, c), bf16),
-            pltpu.SemaphoreType.DMA((2, size)),
-            pltpu.SemaphoreType.DMA((2, size)),
+            pltpu.VMEM((n, most, r, c), bf16),
+            pltpu.SemaphoreType.DMA((n, most)),
+            pltpu.SemaphoreType.DMA((n, most)),
         ],
     )
     return out.reshape(-1, c)
 
 
 class Leaf:
-    def __init__(self, array, axes, held=(), width=None, index=0):
-        self.array, self.axes, self.held = array, axes, dict(held)
+    def __init__(self, array, axes, left=0, width=None, held=()):
+        self.array, self.axes, self.left, self.held = array, axes, left, dict(held)
         self.width = width or array.shape[-1]
-        self.index = index
 
     def hold(self, way, far):
         held = dict(self.held)
         if way in self.axes:
             held[way] = far
-        return Leaf(self.array, self.axes, held, self.width, self.index)
+        return Leaf(self.array, self.axes, self.left, self.width, held)
 
     def free(self):
-        return [a for a in self.axes if a not in self.held]
-
-    def spec(self, ring_steps):
-        shape, pick = [], []
-        for i, a in enumerate(self.axes):
-            if a in self.held:
-                shape.append(None)
-                pick.append(("far" if self.held[a] else "here", Links.names.index(a)))
-            elif a == "ring" and ring_steps:
-                shape.append(1)
-                pick.append(("step", 0))
-            else:
-                shape.append(self.array.shape[i])
-                pick.append(("zero", 0))
-
-        def index(t, spot):
-            out = []
-            for kind, i in pick:
-                if kind == "far":
-                    out.append(1 - spot[i])
-                elif kind == "here":
-                    out.append(spot[i])
-                else:
-                    out.append(t if kind == "step" else 0)
-            return (*out, 0, self.index)
-
-        return pl.BlockSpec((*shape, self.array.shape[-2], self.width), index)
-
-
-class Scatter:
-    def __init__(self, links, jobs):
-        self.links = links
-        self.jobs = [([*leaves], list(order)) for leaves, order in jobs]
-        self.last = None
-
-    def step(self, after=()):
-        links = self.links
-        size = links.size
-        ways = [order.pop(0) for _, order in self.jobs]
-        ins, specs, outs, out_specs, plan = [], [], [], [], []
-        for (leaves, _), way in zip(self.jobs, ways):
-            moving = [leaf.hold(way, True) for leaf in leaves]
-            free = moving[0].free()
-            ins += [leaf.array for leaf in moving]
-            specs += [leaf.spec(True) for leaf in moving]
-            shape = tuple(links.lengths[a] for a in free) + (moving[0].array.shape[-2], moving[0].width)
-            outs.append(struct(shape, bf16))
-            block = tuple(1 if a == "ring" else links.lengths[a] for a in free) + shape[-2:]
-            at = free.index("ring")
-            out_specs.append(
-                pl.BlockSpec(
-                    block,
-                    functools.partial(
-                        lambda at, rank, t, spot: tuple(t if i == at else 0 for i in range(rank)),
-                        at,
-                        len(block),
-                    ),
-                )
+        return tuple(a for a in self.axes if a not in self.held)
+
+    def spec(self, links):
+        shape = tuple(None if a in self.held else 2 for a in self.axes) + self.array.shape[-2:]
+        picks = [(self.held.get(a), links.names.index(a)) for a in self.axes]
+
+        def index(_, spot):
+            return (
+                *(0 if far is None else 1 - spot[i] if far else spot[i] for far, i in picks),
+                0,
+                0,
             )
-            plan.append((len(moving), free))
-
-        def kernel(spot, *refs):
-            n = 0
-            for (count, _), out in zip(plan, refs[len(ins) :]):
-                total = refs[n][...].astype(f32)
-                for ref in refs[n + 1 : n + count]:
-                    total = total + ref[...].astype(f32)
-                out[...] = total.astype(bf16)
-                n += count
-
-        sent = call(
-            kernel, ins, specs, outs, out_specs, "combine", after=after, grid=(size,), prefetch=links.spot
-        )
-        jobs = []
-        for (leaves, order), way, away, (_, free) in zip(self.jobs, ways, sent, plan):
-            kept = [leaf.hold(way, False) for leaf in leaves]
-            jobs.append((kept + [Leaf(links.send(away, way), free)], order))
-        self.jobs = jobs
-        return sent[:1]
-
-    def spread(self, after=()):
-        links = self.links
-        size = links.size
-        ins, specs, groups, where = [], [], {}, []
-        for leaves, _ in self.jobs:
-            ins += [leaf.array for leaf in leaves]
-            specs += [leaf.spec(False) for leaf in leaves]
-            free = [a for a in leaves[0].free() if a != "ring"]
-            key = tuple(links.lengths[a] for a in free) + (leaves[0].array.shape[-2],)
-            left = groups.get(key, 0)
-            groups[key] = left + leaves[0].width
-            where.append((key, left, leaves[0].width, len(leaves), leaves[0].free().index("ring")))
-        keys = list(groups)
-        outs = []
-        for key in keys:
-            shape = key + (groups[key],)
-            outs += [struct(shape, f32)] + [struct(shape, bf16)] * (size - 1)
-
-        def kernel(spot, *refs):
-            n, m = 0, len(ins)
-            for key, left, width, count, at in where:
-                base = m + keys.index(key) * size
-                for s in range(size):
-                    ring = lax.rem(spot[2] + s, size)
-                    total = None
-                    for ref in refs[n : n + count]:
-                        term = (ref[ring] if at == 0 else ref[:, :, ring]).astype(f32)
-                        total = term if total is None else total + term
-                    out = refs[base + s]
-                    out[..., left : left + width] = total.astype(out.dtype)
-                n += count
-
-        sent = call(
-            kernel, ins, specs, outs, [whole(o.shape) for o in outs], "spread", after=after, prefetch=links.spot
-        )
-        totals = {}
-        for i, key in enumerate(keys):
-            group = sent[i * size : (i + 1) * size]
-            total = group[0]
-            for s in range(1, size):
-                total = total + links.send(group[s], s).astype(f32)
-            totals[key] = total
-        self.results = [totals[key][..., left : left + width] for key, left, width, _, _ in where]
-        return sent[:1]
+
+        return pl.BlockSpec(shape, index)
+
+
+class Sum:
+    def __init__(self, leaves, ways):
+        self.leaves, self.ways = leaves, list(ways)
+
+
+def gather_terms(links, leaves_of):
+    ins = [leaf.array for leaves in leaves_of for leaf in leaves]
+    specs = [leaf.spec(links) for leaves in leaves_of for leaf in leaves]
+
+    def totals(refs):
+        n = 0
+        for leaves in leaves_of:
+            total = None
+            for leaf in leaves:
+                term = refs[n][..., leaf.left : leaf.left + leaf.width].astype(f32)
+                total = term if total is None else total + term
+                n += 1
+            yield total
+
+    return ins, specs, totals
+
+
+def advance(links, sums, after=()):
+    moves = []
+    for one in sums:
+        way = one.ways.pop(0)
+        moves.append((way, [leaf.hold(way, True) for leaf in one.leaves]))
+        one.leaves = [leaf.hold(way, False) for leaf in one.leaves]
+    groups, where = {}, []
+    for way, leaves in moves:
+        free = leaves[0].free()
+        key = (way, free, leaves[0].array.shape[-2])
+        left = groups.get(key, 0)
+        groups[key] = left + leaves[0].width
+        where.append((key, left, leaves[0].width))
+    keys = list(groups)
+    outs = [struct((2,) * len(free) + (r, groups[way, free, r]), bf16) for way, free, r in keys]
+    ins, specs, totals = gather_terms(links, [leaves for _, leaves in moves])
+
+    def kernel(spot, *refs):
+        for total, (key, left, width) in zip(totals(refs), where):
+            refs[len(ins) + keys.index(key)][..., left : left + width] = total.astype(bf16)
+
+    sent = call(
+        kernel, ins, specs, outs, [whole(o.shape) for o in outs], "combine", micros=3, after=after, prefetch=links.spot
+    )
+    got = {key: links.send(a, key[0]) for key, a in zip(keys, sent)}
+    for one, (key, left, width) in zip(sums, where):
+        one.leaves.append(Leaf(got[key], key[1], left, width))
+    return (sent[0],)
+
+
+def finish(links, sums, cuts, after=()):
+    ins, specs, totals = gather_terms(links, [one.leaves for one in sums])
+    outs = [
+        struct((2,) * len(one.leaves[0].free()) + (one.leaves[0].array.shape[-2], width), f32)
+        for one, widths in zip(sums, cuts)
+        for width in widths
+    ]
+
+    def kernel(spot, *refs):
+        n = len(ins)
+        for total, widths in zip(totals(refs), cuts):
+            left = 0
+            for width in widths:
+                refs[n][...] = total[..., left : left + width]
+                left += width
+                n += 1
+
+    return call(
+        kernel, ins, specs, outs, [whole(o.shape) for o in outs], "finish", micros=3, after=after, prefetch=links.spot
+    )
 
 
 def norm_scale(rows):
@@ -467,6 +429,7 @@
         (struct((seqs, cols, count), bf16), struct((8, width), f32)),
         [pl.BlockSpec((1, cols, tile), lambda b, t: (b, 0, t)), whole((8, width))],
         "project_memory",
+        micros=15,
         grid=(seqs, count // tile),
         scratch=[pltpu.VMEM((width, blocks.c), bf16), pltpu.VMEM((cols, width), bf16)],
     )
@@ -502,7 +465,7 @@
         kernel,
         [links.spot, lengths, x.reshape(rows, width), gain, table] + blocks.arrays,
         [smem(), smem(), whole((rows, width)), whole((1, width)), whole(table.shape)]
-        + blocks.specs(),
+        + blocks.specs(cols + width, 0),
         (
             struct((rows, width), f32),
             struct((rows, width), bf16),
@@ -511,16 +474,17 @@
         ),
         [whole((rows, width)), whole((rows, width)), whole((rows, cols)), whole((rows, width))],
         "causal_forward",
+        micros=9,
         after=after,
         scratch=[pltpu.VMEM((width, cols), bf16), pltpu.VMEM((width, width), bf16)],
     )
 
 
-def cross_forward(links, x1, keyval, blocks, gain_cross, gain_feed):
+def cross_forward(links, x1, keyval, blocks, gain_cross, gain_feed, after):
     rows, width = x1.shape
     seqs, _, count = keyval.shape
     length = rows // seqs
-    n = blocks.count
+    n = blocks.count * 2
 
     def kernel(spot, x1_ref, kv_ref, g2_ref, g3_ref, *refs):
         n2_ref, q2_ref, o2_ref, x2_ref, n3_ref, p_ref, wq_ref, wo_ref = refs[n:]
@@ -528,7 +492,8 @@
 
         @pl.when((b == 0) & (g == 0))
         def _():
-            blocks.put(spot, refs[:n], wq_ref, wo_ref)
+            blocks.put(spot, refs[: n // 2], wq_ref)
+            blocks.put(spot, refs[n // 2 : n], wo_ref)
             x1v = x1_ref[...]
             n2 = (x1v * norm_scale(x1v) * g2_ref[...]).astype(bf16)
             n2_ref[...] = n2
@@ -551,7 +516,7 @@
 
     return call(
         kernel,
-        [links.spot, x1, keyval, gain_cross, gain_feed] + blocks.arrays,
+        [links.spot, x1, keyval, gain_cross, gain_feed] + blocks.arrays * 2,
         [
             smem(),
             whole((rows, width)),
@@ -559,7 +524,8 @@
             whole((1, width)),
             whole((1, width)),
         ]
-        + blocks.specs(),
+        + blocks.specs(width, 3)
+        + blocks.specs(width, 4),
         (
             struct((rows, width), bf16),
             struct((rows, width), bf16),
@@ -571,6 +537,8 @@
         [whole((rows, width))] * 5
         + [pl.BlockSpec((1, 2 * length, count), lambda b, g: (b * KVH + g, 0, 0))],
         "cross_forward",
+        micros=34,
+        after=after,
         grid=(seqs, KVH),
         scratch=[pltpu.VMEM((width, width), bf16)] * 2,
     )
@@ -632,6 +600,7 @@
         ),
         [whole((4 * rows, units))] * 3 + [whole((rows, width))] * 2 + [whole((2 * rows, width))],
         "feed_through",
+        micros=14,
         after=after,
         scratch=[
             pltpu.VMEM((width, units), bf16),
@@ -680,6 +649,7 @@
         [whole((rows, width))] * 2
         + [whole((2 * rows, width)), whole((width, 2 * units)), whole((units, width))],
         "feed_weight_grads",
+        micros=12,
         after=after,
         scratch=[
             pltpu.VMEM((width, 4 * rows), bf16),
@@ -712,7 +682,7 @@
         [links.spot, x2, gain_feed, dn3, dn3_core, dn3_hi, cotangent, o2] + out_blocks.arrays,
         [smem(), whole((rows, width)), whole((1, width))]
         + [whole((rows, width))] * 5
-        + out_blocks.specs(width, 1),
+        + out_blocks.specs(width, 4),
         (
             struct((rows, width), f32),
             struct((rows, width), bf16),
@@ -722,6 +692,7 @@
         ),
         [whole((rows, width))] * 2 + [whole(split)] * 2 + [whole((1, width))],
         "cross_enter",
+        micros=6,
         after=after,
         scratch=[pltpu.VMEM((width, width), bf16), pltpu.VMEM((width, rows), bf16)],
     )
@@ -772,6 +743,7 @@
         (struct((rows, width), bf16), struct((seqs, cols, count), bf16)),
         [heads_block, kv_block],
         "cross_backward",
+        micros=25,
         after=after,
         grid=(seqs, KVH),
     )
@@ -801,7 +773,15 @@
             for hi in range(2):
                 for out, at in ((keep_ref, spot[1]), (away_ref, 1 - spot[1])):
                     lanes = pl.ds(pl.multiple_of((hi * 2 + at) * half, half), half)
-                    out[hi] = acc_ref[:, lanes].T.astype(bf16)
+                    for side in range(2):
+                        for g in range(0, KVH, 2):
+                            pair = [
+                                acc_ref[(g + i) * PAIR + side * HD : (g + i) * PAIR + (side + 1) * HD, lanes]
+                                for i in range(2)
+                            ]
+                            left = side * cols // 2 + g * HD
+                            out[hi, :, left : left + PAIR] = jnp.concatenate(pair, axis=0).T.astype(bf16)
+                    out[hi, :, cols:] = acc_ref[cols:, lanes].T.astype(bf16)
 
     return call(
         kernel,
@@ -815,6 +795,7 @@
         (struct(split, bf16), struct(split, bf16)),
         [whole(split)] * 2,
         "keyval_weight_grad",
+        micros=15,
         after=after,
         grid=(seqs, steps),
         scratch=[pltpu.VMEM((wide, width), f32)],
@@ -843,21 +824,22 @@
         struct((seqs, count, width), bf16),
         pl.BlockSpec((1, tile, width), lambda b, t: (b, t, 0)),
         "memory_gradient",
+        micros=15,
         after=after,
         grid=(seqs, count // tile),
         scratch=[pltpu.VMEM((width, cols), bf16)],
     )
 
 
-def causal_enter(links, dx2, x1, gain_cross, n2, dq2, o1, out_blocks, query_blocks, after):
+def causal_enter(links, dx2, x1, gain_cross, n2, dq2, o1, blocks, after):
     rows, width = x1.shape
-    n, m = out_blocks.count, out_blocks.count + query_blocks.count
+    n, m = blocks.count, 2 * blocks.count
     split = (2, width // 4, 2 * width)
 
     def kernel(spot, dx2_ref, x1_ref, g_ref, n2_ref, dq2_ref, o1_ref, *refs):
         dx_ref, do_ref, keep_ref, away_ref, gg_ref, wo_ref, wq_ref, o1t_ref, n2t_ref = refs[m:]
-        out_blocks.put(spot, refs[:n], wo_ref)
-        query_blocks.put(spot, refs[n:m], wq_ref)
+        blocks.put(spot, refs[:n], wo_ref)
+        blocks.put(spot, refs[n:m], wq_ref)
         dq2 = dq2_ref[...]
         grad_rows, grad_gain = norm_back(dot(dq2, wq_ref[...], 1, 1), x1_ref[...], g_ref[...])
         gg_ref[...] = grad_gain
@@ -872,11 +854,11 @@
 
     return call(
         kernel,
-        [links.spot, dx2, x1, gain_cross, n2, dq2, o1] + out_blocks.arrays + query_blocks.arrays,
+        [links.spot, dx2, x1, gain_cross, n2, dq2, o1] + blocks.arrays * 2,
         [smem(), whole((rows, width)), whole((rows, width)), whole((1, width))]
         + [whole((rows, width))] * 3
-        + out_blocks.specs(width, 2)
-        + query_blocks.specs(width, 0),
+        + blocks.specs(width, 2)
+        + blocks.specs(width, 3),
         (
             struct((rows, width), f32),
             struct((rows, width), bf16),
@@ -886,6 +868,7 @@
         ),
         [whole((rows, width))] * 2 + [whole(split)] * 2 + [whole((1, width))],
         "causal_enter",
+        micros=8,
         after=after,
         scratch=[
             pltpu.VMEM((width, width), bf16),
@@ -934,10 +917,18 @@
             bias_ref[2 * g + 1 : 2 * g + 2] = diagonal_sums(odd_sum)
         dqkv = dqkv_ref[...]
         n1t_ref[...] = n1_ref[...].T
-        split_rows(n1t_ref, dqkv, spot[1], keep_ref, away_ref)
         grad_rows, grad_gain = norm_back(
             dot(dqkv, w_ref[...], 1, 1), x_ref[...].astype(f32), g1_ref[...]
         )
+        split_rows(n1t_ref, dqkv[:, :width], spot[1], keep_ref.at[:, :, :width], away_ref.at[:, :, :width])
+        keep_low = low_lanes((rows, PAIR))
+        apart = [[], []]
+        for g in range(0, KVH, 2):
+            one, two = (dqkv[:, width + i * PAIR : width + (i + 1) * PAIR] for i in (g, g + 1))
+            apart[0].append(jnp.where(keep_low, one, swap_halves(two)))
+            apart[1].append(jnp.where(keep_low, swap_halves(one), two))
+        dkv = jnp.concatenate(apart[0] + apart[1], axis=1)
+        split_rows(n1t_ref, dkv, spot[1], keep_ref.at[:, :, width:], away_ref.at[:, :, width:])
         gg1_ref[...] = grad_gain
         dx_ref[...] = (dx1_ref[...] + grad_rows).astype(bf16)
 
@@ -957,6 +948,7 @@
         ),
         [whole(split)] * 2 + [whole((1, width)), whole((HEADS, bucket_reach)), whole((rows, width))],
         "causal_backward",
+        micros=15,
         after=after,
         scratch=[
             pltpu.VMEM((width, cols), bf16),
@@ -973,14 +965,6 @@
     ).reshape(r, KVH * PAIR)
 
 
-def part_keyval(pair):
-    r = pair.shape[0]
-    both = pair.reshape(r, KVH, 2, HD)
-    return both[:, :, 0].reshape(r, KVH * HD), both[:, :, 1].reshape(r, KVH * HD)
-
-
-XY = ("lo", "hi")
-YX = ("hi", "lo")
 EXTRA = 128
 
 
@@ -1038,27 +1022,50 @@
         ]
     )
 
-    first_pieces = links.spread_ring(first_shard)
-    feed_near = links.quarters(tie(feed_wide, first_pieces[-1])).reshape(4 * r, 2 * units)
-    second_pieces = links.spread_ring(second_shard, first_pieces[1:])
-    first_blocks = links.grow(jnp.stack(first_pieces), XY)
-    cot_core = links.send(tie(cot, first_blocks.arrays[-1]), "core")
-    keyval, small_all = project_memory(links, memory, first_blocks)
-    feed_pieces = links.spread_ring(feed_near, second_pieces[1:])
-
-    cut = causal_shard.shape[1]
-    causal_stack = jnp.stack([p[:, :cut] for p in second_pieces])
-    cross_stack = jnp.stack([p[:, cut:] for p in second_pieces])
-    causal_blocks = links.grow(causal_stack, XY)
-    cross_blocks = links.grow(cross_stack, YX)
-    down_pieces = links.spread_ring(feed_down, feed_pieces[1:])
-    feed_stack = jnp.stack(feed_pieces)
-    feed_far = links.send(tie(feed_stack, cross_blocks.arrays[1]), "lo")
-    feed_blocks = Blocks(
-        links, [(feed_stack[None], [{}]), (feed_far[None], [{"lo": 1}])], quads=True
-    )
-    cot_hi = links.send(tie(cot, causal_blocks.arrays[1]), "hi")
-    cot_both = links.send(cot_hi, "core")
+    bits = links.bits
+    near = [frozenset()]
+    lo_hi, hi_lo = ("lo", "hi"), ("hi", "lo")
+
+    first_ring = links.grow((first_shard[None], near), bits)
+    first_lo = links.grow(first_ring, ("lo",))
+    second_one = links.grow((second_shard[None], near), bits[:1], first_ring[0])
+    first_near = links.grow(first_lo, ("hi",))
+    cot_core = links.send(cot, "core", first_lo[0])
+    cot_hi = links.send(cot, "hi", first_lo[0])
+    first_far = links.send(first_near[0], "core"), [f | {"core"} for f in first_near[1]]
+    first_blocks = Blocks(links, first_near, first_far)
+    second_ring = links.grow(second_one, bits[1:], first_near[0])
+    feed_near = links.quarters(feed_wide, first_near[0], cot_core, cot_hi)
+
+    stack, fars = second_ring
+    half = stack.shape[2] // 2
+    left_one = links.grow((stack[..., :half], fars), ("lo",))
+    right_one = links.grow((stack[..., half:], fars), ("hi",))
+    keyval, small_all = project_memory(
+        links, tie(memory, stack, first_far[0], feed_near), first_blocks
+    )
+    down_one = links.grow((feed_down[None], near), bits[:1], stack, feed_near, then=(keyval,))
+    feed_one = links.grow((feed_near[None], near), bits[:1], stack, then=(keyval,))
+    left_two = links.send(left_one[0], "hi", keyval, down_one[0], feed_one[0])
+    right_two = links.send(right_one[0], "lo", keyval, down_one[0], feed_one[0])
+    down_ring = links.grow(down_one, bits[1:], keyval)
+    feed_ring = links.grow(feed_one, bits[1:], keyval)
+    n = len(fars)
+    second_near = jnp.concatenate(
+        [
+            jnp.concatenate([left_one[0], left_two], axis=0),
+            jnp.concatenate(
+                [right_one[0][:n], right_two[:n], right_one[0][n:], right_two[n:]], axis=0
+            ),
+        ],
+        axis=2,
+    )
+    second_near = tie(second_near, down_ring[0], feed_ring[0])
+    cot_both = links.send(cot_hi, "core", second_near)
+    second_fars = left_one[1] + [f | {"hi"} for f in left_one[1]]
+    second_far = links.send(second_near, "core"), [f | {"core"} for f in second_fars]
+    second_blocks = Blocks(links, (second_near, second_fars), second_far)
+    down_far = links.send(down_ring[0], "lo", right_two), [f | {"lo"} for f in down_ring[1]]
     cots = (cot, cot_core, cot_hi, cot_both)
 
     gain_one, gain_two, gain_three = (small_all[i : i + 1] for i in range(3))
@@ -1067,70 +1074,71 @@
     table = jnp.dot(bias_all.astype(bf16), onehot.astype(bf16), preferred_element_type=f32)
 
     x1, n1, qkv1, o1 = causal_forward(
-        links, inputs, causal_blocks, gain_one, table, lengths, (keyval,)
-    )
-    down_stack = jnp.stack(down_pieces)
-    down_far = links.send(tie(down_stack, feed_far), "lo")
-    n2, q2, o2, x2, n3, probs = cross_forward(links, x1, keyval, cross_blocks, gain_two, gain_three)
+        links, inputs, second_blocks, gain_one, table, lengths, (keyval, feed_ring[0], down_ring[0])
+    )
+    w_down = assemble(links, (down_ring, down_far), (x1,))
+    feed_far = links.send(feed_ring[0], "lo", x1), [f | {"lo"} for f in feed_ring[1]]
+    feed_blocks = Blocks(links, feed_ring, feed_far, quads=True)
+    n2, q2, o2, x2, n3, probs = cross_forward(
+        links, x1, keyval, second_blocks, gain_two, gain_three, (w_down,)
+    )
     n3_hi = links.send(n3, "hi")
     n3_core = links.send(n3, "core")
     n3_both = links.send(n3_hi, "core")
     n3s = (n3, n3_core, n3_hi, n3_both)
-    w_down = assemble(links, down_stack, down_far, (x2,))
     hidden, dgate, dup, dn3, dn3_hi, dn3_away = feed_through(
         links, n3s, cots, feed_blocks, w_down, ()
     )
 
-    def over_four(own, hi, away, after=()):
-        got = links.send(tie(away, *after), "core")
-        passed = (hi + got[rows:].astype(f32)).astype(bf16)
-        return own, got[:rows], links.send(passed, "hi")
-
-    dn3_terms = over_four(dn3, dn3_hi, dn3_away)
+    dn3_got = links.send(dn3_away, "core")
+    dn3_passed = (dn3_hi + dn3_got[rows:].astype(f32)).astype(bf16)
+    dn3_terms = (dn3, dn3_got[:rows], links.send(dn3_passed, "hi"))
     y, y_hi, y_away, grad_gu, grad_down = feed_weight_grads(
-        n3s, cots, hidden, dgate, dup, w_down, ()
-    )
-
-    def split(a, way_axes):
-        return a.reshape(tuple(links.lengths[w] for w in way_axes) + (-1, a.shape[-1]))
-
-    every = ("hi", "core", "ring", "lo")
-    apart = ("hi", "ring", "lo")
-    feed_sums = Scatter(
-        links,
-        [
-            ([Leaf(split(grad_gu, every), every)], ("lo",)),
-            ([Leaf(split(grad_down, ("ring", "lo")), ("ring", "lo"))], ("lo",)),
-        ],
-    )
-
-    def halves(keep, away, *windows):
-        keep, away = split(keep, apart), split(away, apart)
-        got = links.send(away, "core")
+        n3s, cots, hidden, dgate, dup, w_down, (dn3_passed,)
+    )
+
+    def split(a, axes):
+        return a.reshape((2,) * len(axes) + (-1, a.shape[-1]))
+
+    dp_axes = bits + ("lo",)
+    apart = ("hi",) + dp_axes
+    back = tuple(reversed(bits))
+
+    def halves(keep, away, ways, *windows):
+        got = split(links.send(away, "core"), apart)
+        keep = split(keep, apart)
         return [
-            ([Leaf(keep, apart, (), w, i), Leaf(got, apart, (), w, i)], order)
-            for w, i, order in windows
+            Sum([Leaf(keep, apart, left, width), Leaf(got, apart, left, width)], ways + back)
+            for left, width in windows
         ]
 
-    done = feed_sums.step((y,))
+    gu_axes = ("hi", "core") + dp_axes
+    feed_sums = [
+        Sum([Leaf(split(grad_gu, gu_axes), gu_axes)], ("lo",) + back),
+        Sum([Leaf(split(grad_down, dp_axes), dp_axes)], ("lo",) + back),
+    ]
+    done = advance(links, feed_sums, (y,))
     dx2, do2, keep, away, grad_gain_three = cross_enter(
-        links, x2, gain_three, *dn3_terms, cot, o2, cross_blocks, done
-    )
-    jobs_o2 = halves(keep, away, (width, 0, YX))
-    y_terms = over_four(y, y_hi, y_away, (dx2,))
+        links, x2, gain_three, *dn3_terms, cot, o2, second_blocks, done
+    )
+    early_sums = halves(keep, away, hi_lo, (0, width))
+    y_got = links.send(y_away, "core", dx2)
     dq2, grad_keyval = cross_backward(q2, do2, o2, keyval, probs, (dx2,))
     dx1, do1, keep, away, grad_gain_two = causal_enter(
-        links, dx2, x1, gain_two, n2, dq2, o1, causal_blocks, cross_blocks, ()
-    )
-    jobs_o1q2 = halves(keep, away, (width, 0, XY), (width, 1, YX))
-    done = feed_sums.spread((dx1,))
-    early_sums = Scatter(links, jobs_o2 + jobs_o1q2)
-    done = early_sums.step(done)
+        links, dx2, x1, gain_two, n2, dq2, o1, second_blocks, ()
+    )
+    early_sums += halves(keep, away, lo_hi, (0, 2 * width))
+    y_passed = (tie(y_hi, dx1) + y_got[rows:].astype(f32)).astype(bf16)
+    y_terms = (y, y_got[:rows], links.send(y_passed, "hi"))
     keep, away, grad_gain_one, grad_bias, input_grad = causal_backward(
-        links, lengths, dx1, do1, qkv1, n1, x, gain_one, table, causal_blocks, done
-    )
-    jobs_qkv1 = halves(keep, away, (width, 0, XY), (width, 1, YX))
-    done = early_sums.step((input_grad,))
+        links, lengths, dx1, do1, qkv1, n1, x, gain_one, table, second_blocks, ()
+    )
+    middle_sums = halves(keep, away, lo_hi, (0, width))
+    middle_sums += [
+        Sum([Leaf(leaf.array, leaf.axes, width, width) for leaf in middle_sums[0].leaves], hi_lo + back)
+    ]
+    done = advance(links, feed_sums, (input_grad,))
+    done = advance(links, early_sums, done)
 
     grad_table = lax.dot_general(
         grad_bias, onehot, (((1,), (1,)), ((), ())), precision=lax.Precision.HIGHEST
@@ -1142,36 +1150,29 @@
         [grad_gain_one, grad_gain_two, grad_gain_three, table_rows, jnp.zeros((4, width), f32)],
         axis=0,
     )
-    middle_sums = Scatter(links, jobs_qkv1)
-    done = middle_sums.step(done)
     keep, away = keyval_weight_grad(links, memory, grad_keyval, small_rows, done)
-    jobs_kv2 = halves(keep, away, (KVH * PAIR + EXTRA, 0, YX))
-    late_sums = Scatter(links, jobs_kv2)
-    done = early_sums.spread((keep,))
-    done = middle_sums.step(done)
-    done = late_sums.step(done)
+    late_sums = halves(keep, away, hi_lo, (0, KVH * PAIR + EXTRA))
+    done = advance(links, early_sums + middle_sums, (keep,))
     memory_grad = memory_gradient(links, grad_keyval, first_blocks, done)
-    done = middle_sums.spread((memory_grad,))
-    done = late_sums.step(done)
-    late_sums.spread(done)
+    done = advance(links, early_sums + middle_sums + late_sums, (memory_grad,))
+    done = advance(links, feed_sums + early_sums + middle_sums + late_sums, done)
+    done = advance(links, middle_sums + late_sums, done)
+    half = width // 2
+    while feed_sums[0].ways:
+        done = advance(links, feed_sums, done)
+    sum_gu, sum_down = finish(links, feed_sums, [(2 * units,), (width,)], done)
+    done = (sum_down,)
+    while late_sums[0].ways:
+        done = advance(links, [one for one in early_sums + middle_sums + late_sums if one.ways], done)
+    wide = links.unquarter(sum_gu, done)
+    sum_o2, sum_o1, sum_q2, sum_q1, sum_k1, sum_v1 = finish(
+        links, early_sums + middle_sums, [(width,), (width, width), (width,), (half, half)], done
+    )
+    sum_k2, sum_v2, sum_small = finish(links, late_sums, [(half, half, EXTRA)], (sum_o2,))
 
     layer_out = (x2 + sum(t.astype(f32) for t in y_terms)).astype(bf16)
-    sum_gu, sum_down = feed_sums.results
-    sum_o2, sum_o1, sum_q2 = early_sums.results
-    sum_q1, sum_kv1 = middle_sums.results
-    sum_kv2, sum_small = late_sums.results[0][:, :width], late_sums.results[0][:, width:]
-    sum_k1, sum_v1 = part_keyval(sum_kv1)
-    sum_k2, sum_v2 = part_keyval(sum_kv2)
-
-    wide = sum_gu.reshape(links.nf, r, 2 * units)
-    mine = links.hi * 2 + links.core
-    near = [lax.dynamic_index_in_dim(wide, mine, 0, keepdims=False)]
-    for flip, way in ((1, "core"), (2, "hi"), (3, "both")):
-        theirs = lax.dynamic_index_in_dim(wide, mine ^ flip, 0, keepdims=False).astype(bf16)
-        near.append(links.send(theirs, way).astype(f32))
-    wide = links.unquarter(jnp.stack(near))
     sum_gate, sum_up = (
-        wide[:, :, i * units : (i + 1) * units].transpose(1, 0, 2).reshape(r, links.nf * units)
+        jnp.concatenate([part[:, i * units : (i + 1) * units] for part in wide], axis=1)
         for i in range(2)
     )
     return (

time: 593 us -> 472 us (0.80)
  waiting for transfers between devices: 229 us -> 151 us
  starting transfers between devices: 86.9 us -> 56.2 us
  other arithmetic: 12.6 us -> 6.55 us
    ppermute x75 -> x60, waiting for transfers between devices: 229 us -> 151 us  [send(): return lax.ppermute(tie(a, *after), AXES, self.pairs[way])]
    ppermute x75 -> x60, starting transfers between devices: 86.9 us -> 56.2 us  [send(): return lax.ppermute(tie(a, *after), AXES, self.pairs[way])]
    unnamed x114 -> x123, local copies, waits for them, and re-layouts: 13.8 us -> 15.9 us
  transfers between devices with their start and end apart: 75 -> 60, of which waited for: 26 -> 24; matrix products, arithmetic and copies ran while one was open for 4% -> 3% of each run, Pallas kernels for 35% -> 42%
where the time goes in v2:
time: 472 us; the launch traced here: 467 us
  Pallas kernels  214 us (45%)
  waiting for transfers between devices  151 us (32%)
  starting transfers between devices  56.2 us (12%)
  local copies, waits for them, and re-layouts  35.1 us (7%)
  other arithmetic  6.55 us (1%)
    pallas_call x23, Pallas kernels, call(): pl.pallas_call(body, grid_spec=spec, out_shape=out_shape, compiler_params...  214 us
    ppermute x60, waiting for transfers between devices, send(): return lax.ppermute(tie(a, *after), AXES, self.pairs[way])  151 us
    ppermute x60, starting transfers between devices, send(): return lax.ppermute(tie(a, *after), AXES, self.pairs[way])  56.2 us
    unnamed x123, local copies, waits for them, and re-layouts  15.9 us
  transfers between devices with their start and end apart: 60, of which 24 were waited for; matrix products, arithmetic and copies ran while one was open for 3% of the time, Pallas kernels for 42%

profile of v2, /device:TPU:0, one launch (start us, length us, event | category | flops | bytes accessed | tf_op | source)
XLA Modules:
  0.0 466.8 jit_solution(3187277647560331564)
XLA Ops:
  5.7 4.1 collective-permute-start
  15.6 3.7 collective-permute-done.1
  23.3 3.6 collective-permute-done.3
  29.2 8.0 %collective-permute-done.2 = bf16[1,32,5120]{2,1,0:T(8,128)(2,1)S(1)} collective-permute-done((bf16[1,32,5120]{2,1,0:T(8,128)(2,1)S(1)}, bf16[1,32,5120]{2,1,0:T(8,128)(2,1)S(1)}, u32[]{:S(2)}, u32[]{:S(2)}) %collective-permute-start.2) | collective-permute-done | bytes 327712 | tf_op jit(solution)/shard_map/ppermute | solution.py:106
  37.2 6.2 %collective-permute-done.4 = bf16[8,32,1152]{2,1,0:T(8,128)(2,1)S(1)} collective-permute-done((bf16[8,32,1152]{2,1,0:T(8,128)(2,1)S(1)}, bf16[8,32,1152]{2,1,0:T(8,128)(2,1)S(1)}, u32[]{:S(2)}, u32[]{:S(2)}) %collective-permute-start.4) | collective-permute-done | bytes 589856 | tf_op jit(solution)/shard_map/ppermute | solution.py:106
  45.2 6.1 %collective-permute-done.8.refs_7_.refs_6_ = bf16[256,1024]{1,0:T(8,128)(2,1)} collective-permute-done((bf16[256,1024]{1,0:T(8,128)(2,1)}, bf16[256,1024]{1,0:T(8,128)(2,1)}, u32[]{:S(2)}, u32[]{:S(2)}) %collective-permute-start.8) | collective-permute-done | bytes 524320 | tf_op jit(solution)/shard_map/ppermute | solution.py:106
  59.3 3.6 collective-permute-start.13
  65.4 15.5 %project_memory.1 = (bf16[2,1024,2048]{2,1,0:T(8,128)(2,1)}, f32[8,1024]{1,0:T(8,128)}) custom-call(s32[6]{0:T(128)} %stack.66.refs_0_, bf16[2,2048,1024]{2,1,0:T(8,128)(2,1)} %refs_1_.6, bf16[16,32,1152]{2,1,0:T(8,128)(2,1)} %copy-done.30, bf16[16,32,1152]{2,1,0:T(8,128)(2,1)} %copy-done.34), custom_call_target="tpu_custom_call" | custom-call | flops 30000001024 | bytes 1000 | tf_op jit(solution)/shard_map/project_memory/pallas_call | solution.py:58
  81.1 5.8 %collective-permute-done.14 = bf16[1,128,1408]{2,1,0:T(8,128)(2,1)S(1)} collective-permute-done((bf16[1,128,1408]{2,1,0:T(8,128)(2,1)S(1)}, bf16[1,128,1408]{2,1,0:T(8,128)(2,1)S(1)}, u32[]{:S(2)}, u32[]{:S(2)}) %collective-permute-start.14) | collective-permute-done | bytes 360480 | tf_op jit(solution)/shard_map/ppermute | solution.py:106
  91.9 21.8 %collective-permute-done.18 = bf16[2,88,1024]{2,1,0:T(8,128)(2,1)S(1)} collective-permute-done((bf16[2,88,1024]{2,1,0:T(8,128)(2,1)S(1)}, bf16[2,88,1024]{2,1,0:T(8,128)(2,1)S(1)}, u32[]{:S(2)}, u32[]{:S(2)}) %collective-permute-start.18) | collective-permute-done | bytes 360480 | tf_op jit(solution)/shard_map/ppermute | solution.py:106
  125.1 6.9 %collective-permute-done.20.refs_6_.refs_8_.refs_9_.refs_10_ = bf16[16,32,5120]{2,1,0:T(8,128)(2,1)} collective-permute-done((bf16[16,32,5120]{2,1,0:T(8,128)(2,1)}, bf16[16,32,5120]{2,1,0:T(8,128)(2,1)}, u32[]{:S(2)}, u32[]{:S(2)}) %collective-permute-start.20) | collective-permute-done | bytes 5242912 | tf_op jit(solution)/shard_map/ppermute | solution.py:106
  132.1 9.6 %causal_forward.1 = (f32[256,1024]{1,0:T(8,128)}, bf16[256,1024]{1,0:T(8,128)(2,1)}, bf16[256,2048]{1,0:T(8,128)(2,1)}, bf16[256,1024]{1,0:T(8,128)(2,1)}) custom-call(s32[6]{0:T(128)} %stack.66.refs_0_, s32[2]{0:T(128)} %refs_1_.5, bf16[256,1024]{1,0:T(8,128)(2,1)} %bitcast.160, f32[1,1024]{1,0:T(1,128)} %get-tuple-element.262.refs_3_.refs_7_, ...), custom_call_target="tpu_custom_call" | custom-call | flops 17999998976 | bytes 1000 | tf_op jit(solution)/shard_map/causal_forward/pallas_call | solution.py:58
  147.0 35.2 %cross_forward.1 = (bf16[256,1024]{1,0:T(8,128)(2,1)}, bf16[256,1024]{1,0:T(8,128)(2,1)}, bf16[256,1024]{1,0:T(8,128)(2,1)}, f32[256,1024]{1,0:T(8,128)}, bf16[2...) custom-call(s32[6]{0:T(128)} %stack.66.refs_0_, f32[256,1024]{1,0:T(8,128)} %get-tuple-element.135.refs_3_.refs_1_.refs_2_, ...), custom_call_target="tpu_custom_call" | custom-call | flops 67999997952 | bytes 1000 | tf_op jit(solution)/shard_map/cross_forward/pallas_call | solution.py:58
  183.8 12.3 %collective-permute-done.23.refs_3_.refs_2_ = bf16[256,1024]{1,0:T(8,128)(2,1)S(1)} collective-permute-done((bf16[256,1024]{1,0:T(8,128)(2,1)}, bf16[256,1024]{1,0:T(8,128)(2,1)S(1)}, u32[]{:S(2)}, u32[]{:S(2)}) %collective-permute-start.23) | collective-permute-done | bytes 524320 | tf_op jit(solution)/shard_map/ppermute | solution.py:106
  199.9 13.8 %feed_through.1 = (bf16[1024,704]{1,0:T(8,128)(2,1)}, bf16[1024,704]{1,0:T(8,128)(2,1)}, bf16[1024,704]{1,0:T(8,128)(2,1)}, f32[256,1024]{1,0:T(8,128)}, f32[256,1024]{1,0:T(8,128)}, /*index=5*/bf16[512,1024]{1,0:T(8,128)(2,1)}) custom-call(s32[6]{0:T(128)} %stack.66.refs_0_, bf16[256,1024]{1,0:T(8,128)(2,1)} %get-tuple-element.138.refs_1_.refs_0_, ...), custom_call_target="tpu_custom_call" | custom-call | flops 28000000000 | bytes 1000 | tf_op jit(solution)/shard_map/feed_through/pallas_call | solution.py:58
  219.0 12.3 %feed_weight_grads.1 = (f32[256,1024]{1,0:T(8,128)}, f32[256,1024]{1,0:T(8,128)}, bf16[512,1024]{1,0:T(8,128)(2,1)}, bf16[1024,1408]{1,0:T(8,128)(2,1)}, bf16[704,1024]{1,0:T(8,128)(2,1)}) custom-call(bf16[256,1024]{1,0:T(8,128)(2,1)} %get-tuple-element.138.refs_1_.refs_0_, bf16[256,1024]{1,0:T(8,128)(2,1)} %copy-done.39, bf16[256,1024]{1,0:T(8,128)(2,1)} %copy-done.37, ...), custom_call_target="tpu_custom_call" | custom-call | flops 24000000000 | bytes 1000 | tf_op jit(solution)/shard_map/feed_weight_grads/pallas_call | solution.py:58
  231.3 3.7 combine.8
  238.6 6.1 %cross_enter.1 = (f32[256,1024]{1,0:T(8,128)}, bf16[256,1024]{1,0:T(8,128)(2,1)}, bf16[2,256,1024]{2,1,0:T(8,128)(2,1)}, bf16[2,256,1024]{2,1,0:T(8,128)(2,1)}, f32[1,1024]{1,0:T(1,128)}) custom-call(s32[6]{0:T(128)} %stack.66.refs_0_, f32[256,1024]{1,0:T(8,128)} %get-tuple-element.137.refs_1_, f32[1,1024]{1,0:T(1,128)} %get-tuple-element.260.refs_4_.refs_2_, ...), custom_call_target="tpu_custom_call" | custom-call | flops 12000000000 | bytes 1000 | tf_op jit(solution)/shard_map/cross_enter/pallas_call | solution.py:58
  244.7 25.5 %cross_backward.1 = (bf16[256,1024]{1,0:T(8,128)(2,1)}, bf16[2,1024,2048]{2,1,0:T(8,128)(2,1)}) custom-call(bf16[256,1024]{1,0:T(8,128)(2,1)} %get-tuple-element.157.refs_0_, bf16[256,1024]{1,0:T(8,128)(2,1)} %get-tuple-element.158.refs_1_, bf16[256,1024]{1,0:T(8,128)(2,1)} %get-tuple-element.149.refs_7_.refs_2_, ...), custom_call_target="tpu_custom_call" | custom-call | flops 49999998976 | bytes 1000 | tf_op jit(solution)/shard_map/cross_backward/pallas_call | solution.py:58
  270.2 8.4 %causal_enter.1 = (f32[256,1024]{1,0:T(8,128)}, bf16[256,1024]{1,0:T(8,128)(2,1)}, bf16[2,256,2048]{2,1,0:T(8,128)(2,1)}, bf16[2,256,2048]{2,1,0:T(8,128)(2,1)}, f32[1,1024]{1,0:T(1,128)}) custom-call(s32[6]{0:T(128)} %stack.66.refs_0_, f32[256,1024]{1,0:T(8,128)} %get-tuple-element.153.refs_5_.refs_1_, ...), custom_call_target="tpu_custom_call" | custom-call | flops 16000000000 | bytes 1000 | tf_op jit(solution)/shard_map/causal_enter/pallas_call | solution.py:58
  279.1 15.7 %causal_backward.1 = (bf16[2,256,2048]{2,1,0:T(8,128)(2,1)}, bf16[2,256,2048]{2,1,0:T(8,128)(2,1)}, f32[1,1024]{1,0:T(1,128)}, f32[16,128]{1,0:T(8,128)}, bf16[256,1024]{1,0:T(8,128)(2,1)}) custom-call(s32[6]{0:T(128)} %stack.66.refs_0_, s32[2]{0:T(128)} %refs_1_.5, f32[256,1024]{1,0:T(8,128)} %get-tuple-element.162.refs_2_, ...), custom_call_target="tpu_custom_call" | custom-call | flops 30000001024 | bytes 1000 | tf_op jit(solution)/shard_map/causal_backward/pallas_call | solution.py:58
  301.8 3.9 combine.10
  306.3 15.3 %keyval_weight_grad.1 = (bf16[2,256,1152]{2,1,0:T(8,128)(2,1)}, bf16[2,256,1152]{2,1,0:T(8,128)(2,1)}) custom-call(s32[6]{0:T(128)} %stack.66.refs_0_, bf16[2,2048,1024]{2,1,0:T(8,128)(2,1)} %refs_1_.6, bf16[2,1024,2048]{2,1,0:T(8,128)(2,1)} %get-tuple-element.168.refs_2_.refs_1_, f32[8,1024]{1,0:T(8,128)} %concatenate.112.refs_3_, ...), custom_call_target="tpu_custom_call" | custom-call | flops 30000001024 | bytes 1000 | tf_op jit(solution)/shard_map/keyval_weight_grad/pallas_call | solution.py:58
  322.9 13.1 %collective-permute-done.35.refs_3_.refs_9_ = bf16[2,2,2,32,1024]{4,3,2,1,0:T(8,128)(2,1)S(1)} collective-permute-done((bf16[2,2,2,32,1024]{4,3,2,1,0:T(8,128)(2,1)S(1)}, bf16[2,2,2,32,1024]{4,3,2,1,0:T(8,128)(2,1)S(1)}, u32[]{:S(2)}, u32[]{:S(2)}) %collective-permute-start.35) | collective-permute-done | bytes 524320 | tf_op jit(solution)/shard_map/ppermute | solution.py:106
  337.1 5.0 %combine.11 = (bf16[2,2,32,1024]{3,2,1,0:T(8,128)(2,1)}, bf16[2,2,32,2048]{3,2,1,0:T(8,128)(2,1)}, bf16[2,2,2,32,1024]{4,3,2,1,0:T(8,128)(2,1)}, bf16[2,2,2,32,1024]{4,3,2,1,0:T(8,128)(2,1)}) custom-call(s32[6]{0:T(128)} %stack.66.refs_0_, bf16[2,2,2,2,32,1024]{5,4,3,2,1,0:T(8,128)(2,1)} %bitcast.122, bf16[2,2,2,2,32,1024]{5,4,3,2,1,0:T(8,128)(2,1)} %bitcast.127, ...), custom_call_target="tpu_custom_call" | custom-call | flops 6000000000 | bytes 1000 | tf_op jit(solution)/shard_map/combine/pallas_call | solution.py:58
  346.2 14.6 %memory_gradient.1.refs_17_ = bf16[2,2048,1024]{2,1,0:T(8,128)(2,1)} custom-call(s32[6]{0:T(128)} %stack.66.refs_0_, bf16[2,1024,2048]{2,1,0:T(8,128)(2,1)} %get-tuple-element.168.refs_2_.refs_1_, bf16[16,32,1152]{2,1,0:T(8,128)(2,1)} %copy-done.30, bf16[16,32,1152]{2,1,0:T(8,128)(2,1)} %copy-done.34, bf16[2,2,32,1024]{3,2,1,0:T(8,128)(2,1)} %get-tuple-element.184.refs_4_), custom_call_target="tpu_custom_call" | custom-call | flops 30000001024 | bytes 1000 | tf_op jit(solution)/shard_map/memory_gradient/pallas_call | solution.py:58
  362.9 5.0 %collective-permute-done.41.refs_14_.refs_23_.refs_8_.refs_21_ = bf16[2,2,2,32,1024]{4,3,2,1,0:T(8,128)(2,1)S(1)} collective-permute-done((bf16[2,2,2,32,1024]{4,3,2,1,0:T(8,128)(2,1)}, bf16[2,2,2,32,1024]{4,3,2,1,0:T(8,128)(2,1)S(1)}, u32[]{:S(2)}, u32[]{:S(2)}) %collective-permute-start.41) | collective-permute-done | bytes 524320 | tf_op jit(solution)/shard_map/ppermute | solution.py:106
  368.7 4.8 %combine.12 = (bf16[2,32,3072]{2,1,0:T(8,128)(2,1)}, bf16[2,2,32,1024]{3,2,1,0:T(8,128)(2,1)}, bf16[2,2,32,1024]{3,2,1,0:T(8,128)(2,1)}, bf16[2,2,2,32,1152]{4,3,2,1,0:T(8,128)(2,1)}) custom-call(s32[6]{0:T(128)} %stack.66.refs_0_, bf16[2,2,2,2,32,1024]{5,4,3,2,1,0:T(8,128)(2,1)} %bitcast.123, bf16[2,2,2,2,32,1024]{5,4,3,2,1,0:T(8,128)(2,1)} %bitcast.128, ...), custom_call_target="tpu_custom_call" | custom-call | flops 6000000000 | bytes 1000 | tf_op jit(solution)/shard_map/combine/pallas_call | solution.py:58
  376.1 11.8 %collective-permute-done.45.refs_6_.refs_7_ = bf16[2,88,1024]{2,1,0:T(8,128)(2,1)S(1)} collective-permute-done((bf16[2,88,1024]{2,1,0:T(8,128)(2,1)S(1)}, bf16[2,88,1024]{2,1,0:T(8,128)(2,1)S(1)}, u32[]{:S(2)}, u32[]{:S(2)}) %collective-permute-start.45) | collective-permute-done | bytes 360480 | tf_op jit(solution)/shard_map/ppermute | solution.py:106
  390.5 5.1 %collective-permute-done.46.refs_20_.refs_4_.refs_16_ = bf16[2,2,32,1024]{3,2,1,0:T(8,128)(2,1)S(1)} collective-permute-done((bf16[2,2,32,1024]{3,2,1,0:T(8,128)(2,1)}, bf16[2,2,32,1024]{3,2,1,0:T(8,128)(2,1)S(1)}, u32[]{:S(2)}, u32[]{:S(2)}) %collective-permute-start.46) | collective-permute-done | bytes 262176 | tf_op jit(solution)/shard_map/ppermute | solution.py:106
  397.3 4.4 combine.13
  418.3 23.6 %collective-permute-done.55.refs_8_ = bf16[88,1024]{1,0:T(8,128)(2,1)S(1)} collective-permute-done((bf16[88,1024]{1,0:T(8,128)(2,1)S(1)}, bf16[88,1024]{1,0:T(8,128)(2,1)S(1)}, u32[]{:S(2)}, u32[]{:S(2)}) %collective-permute-start.55) | collective-permute-done | bytes 180256 | tf_op jit(solution)/shard_map/ppermute | solution.py:106
  (299 shorter events, 130.7 us)
Async XLA Ops:
  28.6 22.8 %collective-permute-start.8 = (bf16[256,1024]{1,0:T(8,128)(2,1)}, bf16[256,1024]{1,0:T(8,128)(2,1)}, u32[]{:S(2)}, u32[]{:S(2)}) collective-permute-start(bf16[256,1024]{1,0:T(8,128)(2,1)} %bitcast.19.refs_5_.refs_4_.refs_6_), channel_id=1, source_target_pairs={{0,16},{1,17},{2,18},{3,19},{4,20},{5,21},{6,22},{7,23},{8,24},{9,... | collective-permute-start | bytes 1572872 | tf_op jit(solution)/shard_map/ppermute | solution.py:106
  58.5 28.5 %collective-permute-start.16 = (bf16[4,32,2560]{2,1,0:T(8,128)(2,1)S(1)}, bf16[4,32,2560]{2,1,0:T(8,128)(2,1)S(1)}, u32[]{:S(2)}, u32[]{:S(2)}) collective-permute-start(bf16[4,32,2560]{2,1,0:T(8,128)(2,1)S(1)} %get-tuple-element.220), channel_id=1, source_target_pairs={{0,16},{1,17},{2,18},{3,19},{4,20},{5,21},{6,22},{7,23},{8,24},{9,... | collective-permute-start | bytes 1966088 | tf_op jit(solution)/shard_map/ppermute | solution.py:106
  59.3 21.7 %collective-permute-start.13 = (bf16[1,88,1024]{2,1,0:T(8,128)(2,1)S(1)}, bf16[1,88,1024]{2,1,0:T(8,128)(2,1)S(1)}, u32[]{:S(2)}, u32[]{:S(2)}) collective-permute-start(bf16[1,88,1024]{2,1,0:T(8,128)(2,1)S(1)} %bitcast.153), channel_id=1, source_target_pairs={{0,4},{1,5},{2,6},{3,7},{4,0},{5,1},{6,2},{7,3},{8,12},{9,13},{10,... | collective-permute-start | bytes 540680 | tf_op jit(solution)/shard_map/ppermute | solution.py:106
  62.8 24.1 %collective-permute-start.14 = (bf16[1,128,1408]{2,1,0:T(8,128)(2,1)S(1)}, bf16[1,128,1408]{2,1,0:T(8,128)(2,1)S(1)}, u32[]{:S(2)}, u32[]{:S(2)}) collective-permute-start(bf16[1,128,1408]{2,1,0:T(8,128)(2,1)S(1)} %fusion.4), channel_id=1, source_target_pairs={{0,4},{1,5},{2,6},{3,7},{4,0},{5,1},{6,2},{7,3},{8,12},{9,13},{10,... | collective-permute-start | bytes 1081352 | tf_op jit(solution)/shard_map/ppermute | solution.py:106
  62.9 27.8 %collective-permute-start.12 = (bf16[4,32,2560]{2,1,0:T(8,128)(2,1)S(1)}, bf16[4,32,2560]{2,1,0:T(8,128)(2,1)S(1)}, u32[]{:S(2)}, u32[]{:S(2)}) collective-permute-start(bf16[4,32,2560]{2,1,0:T(8,128)(2,1)S(1)} %get-tuple-element.219), channel_id=1, source_target_pairs={{0,1},{1,0},{2,3},{3,2},{4,5},{5,4},{6,7},{7,6},{8,9},{9,8},{10,11... | collective-permute-start | bytes 1966088 | tf_op jit(solution)/shard_map/ppermute | solution.py:106
  87.1 30.3 %collective-permute-start.17 = (bf16[8,32,2560]{2,1,0:T(8,128)(2,1)S(1)}, bf16[8,32,2560]{2,1,0:T(8,128)(2,1)S(1)}, u32[]{:S(2)}, u32[]{:S(2)}) collective-permute-start(bf16[8,32,2560]{2,1,0:T(8,128)(2,1)S(1)} %pad_maximum_fusion.2), channel_id=1, source_target_pairs={{0,1},{1,0},{2,3},{3,2},{4,5},{5,4},{6,7},{7,6},{8,9},{9,8},{10,11... | collective-permute-start | bytes 3932168 | tf_op jit(solution)/shard_map/ppermute | solution.py:106
  88.7 25.1 %collective-permute-start.19 = (bf16[2,128,1408]{2,1,0:T(8,128)(2,1)S(1)}, bf16[2,128,1408]{2,1,0:T(8,128)(2,1)S(1)}, u32[]{:S(2)}, u32[]{:S(2)}) collective-permute-start(bf16[2,128,1408]{2,1,0:T(8,128)(2,1)S(1)} %get-tuple-element.133), channel_id=1, source_target_pairs={{0,2},{1,3},{2,0},{3,1},{4,6},{5,7},{6,4},{7,5},{8,10},{9,11},{10,... | collective-permute-start | bytes 2162696 | tf_op jit(solution)/shard_map/ppermute | solution.py:106
  89.0 24.6 %collective-permute-start.18 = (bf16[2,88,1024]{2,1,0:T(8,128)(2,1)S(1)}, bf16[2,88,1024]{2,1,0:T(8,128)(2,1)S(1)}, u32[]{:S(2)}, u32[]{:S(2)}) collective-permute-start(bf16[2,88,1024]{2,1,0:T(8,128)(2,1)S(1)} %get-tuple-element.132), channel_id=1, source_target_pairs={{0,2},{1,3},{2,0},{3,1},{4,6},{5,7},{6,4},{7,5},{8,10},{9,11},{10,... | collective-permute-start | bytes 1081352 | tf_op jit(solution)/shard_map/ppermute | solution.py:106
  90.8 29.4 %collective-permute-start.15 = (bf16[8,32,2560]{2,1,0:T(8,128)(2,1)S(1)}, bf16[8,32,2560]{2,1,0:T(8,128)(2,1)S(1)}, u32[]{:S(2)}, u32[]{:S(2)}) collective-permute-start(bf16[8,32,2560]{2,1,0:T(8,128)(2,1)S(1)} %pad_maximum_fusion.1), channel_id=1, source_target_pairs={{0,16},{1,17},{2,18},{3,19},{4,20},{5,21},{6,22},{7,23},{8,24},{9,... | collective-permute-start | bytes 3932168 | tf_op jit(solution)/shard_map/ppermute | solution.py:106
  124.6 18.5 %collective-permute-start.21 = (bf16[4,88,1024]{2,1,0:T(8,128)(2,1)S(1)}, bf16[4,88,1024]{2,1,0:T(8,128)(2,1)S(1)}, u32[]{:S(2)}, u32[]{:S(2)}) collective-permute-start(bf16[4,88,1024]{2,1,0:T(8,128)(2,1)S(1)} %constant_dynamic-update-slice_fusion.13.refs_9_.refs_1_), channel_id=1, source_target_pairs={{0,1},{1,0},{2,3},{3,2},{4,5},{5,4},{6,7},{7,6},{8,9},{9,8},{10,11... | collective-permute-start | bytes 2162696 | tf_op jit(solution)/shard_map/ppermute | solution.py:106
  141.6 56.3 %collective-permute-start.26 = (bf16[4,128,1408]{2,1,0:T(8,128)(2,1)S(1)}, bf16[4,128,1408]{2,1,0:T(8,128)(2,1)S(1)}, u32[]{:S(2)}, u32[]{:S(2)}) collective-permute-start(bf16[4,128,1408]{2,1,0:T(8,128)(2,1)S(1)} %copy-done.22), channel_id=1, source_target_pairs={{0,1},{1,0},{2,3},{3,2},{4,5},{5,4},{6,7},{7,6},{8,9},{9,8},{10,11... | collective-permute-start | bytes 4325384 | tf_op jit(solution)/shard_map/ppermute | solution.py:106
  218.0 19.8 %collective-permute-start.28 = (bf16[256,1024]{1,0:T(8,128)(2,1)S(1)}, bf16[256,1024]{1,0:T(8,128)(2,1)S(1)}, u32[]{:S(2)}, u32[]{:S(2)}) collective-permute-start(bf16[256,1024]{1,0:T(8,128)(2,1)S(1)} %add_convert_fusion.2.refs_12_), channel_id=1, source_target_pairs={{0,16},{1,17},{2,18},{3,19},{4,20},{5,21},{6,22},{7,23},{8,24},{9,... | collective-permute-start | bytes 1572872 | tf_op jit(solution)/shard_map/ppermute | solution.py:106
  235.0 62.5 %collective-permute-start.33 = (bf16[2,2,2,2,32,1408]{5,4,3,2,1,0:T(8,128)(2,1)}, bf16[2,2,2,2,32,1408]{5,4,3,2,1,0:T(8,128)(2,1)}, u32[]{:S(2)}, u32[]{:S(2)}) collective-permute-start(bf16[2,2,2,2,32,1408]{5,4,3,2,1,0:T(8,128)(2,1)} %get-tuple-element.152.refs_10_), channel_id=1, source_target_pairs={{0,1},{1,0},{2,3},{3,2},{4,5},{5,4},{6,7},{7,6},{8,9},{9,8},{10,11... | collective-permute-start | bytes 4325384 | tf_op jit(solution)/shard_map/ppermute | solution.py:106
  235.7 61.8 %collective-permute-start.34 = (bf16[2,2,88,1024]{3,2,1,0:T(8,128)(2,1)}, bf16[2,2,88,1024]{3,2,1,0:T(8,128)(2,1)}, u32[]{:S(2)}, u32[]{:S(2)}) collective-permute-start(bf16[2,2,88,1024]{3,2,1,0:T(8,128)(2,1)} %get-tuple-element.173), channel_id=1, source_target_pairs={{0,1},{1,0},{2,3},{3,2},{4,5},{5,4},{6,7},{7,6},{8,9},{9,8},{10,11... | collective-permute-start | bytes 2162696 | tf_op jit(solution)/shard_map/ppermute | solution.py:106
  244.7 56.1 %collective-permute-start.31 = (bf16[2,256,1024]{2,1,0:T(8,128)(2,1)}, bf16[2,256,1024]{2,1,0:T(8,128)(2,1)S(1)}, u32[]{:S(2)}, u32[]{:S(2)}) collective-permute-start(bf16[2,256,1024]{2,1,0:T(8,128)(2,1)} %get-tuple-element.170), channel_id=1, source_target_pairs={{0,8},{1,9},{2,10},{3,11},{4,12},{5,13},{6,14},{7,15},{8,0},{9,1},... | collective-permute-start | bytes 3145736 | tf_op jit(solution)/shard_map/ppermute | solution.py:106
  278.6 22.2 %collective-permute-start.32 = (bf16[2,256,2048]{2,1,0:T(8,128)(2,1)}, bf16[2,256,2048]{2,1,0:T(8,128)(2,1)}, u32[]{:S(2)}, u32[]{:S(2)}) collective-permute-start(bf16[2,256,2048]{2,1,0:T(8,128)(2,1)} %get-tuple-element.172), channel_id=1, source_target_pairs={{0,8},{1,9},{2,10},{3,11},{4,12},{5,13},{6,14},{7,15},{8,0},{9,1},... | collective-permute-start | bytes 6291464 | tf_op jit(solution)/shard_map/ppermute | solution.py:106
  294.8 28.1 %collective-permute-start.37 = (bf16[2,256,2048]{2,1,0:T(8,128)(2,1)}, bf16[2,256,2048]{2,1,0:T(8,128)(2,1)S(1)}, u32[]{:S(2)}, u32[]{:S(2)}) collective-permute-start(bf16[2,256,2048]{2,1,0:T(8,128)(2,1)} %get-tuple-element.178), channel_id=1, source_target_pairs={{0,8},{1,9},{2,10},{3,11},{4,12},{5,13},{6,14},{7,15},{8,0},{9,1},... | collective-permute-start | bytes 6291464 | tf_op jit(solution)/shard_map/ppermute | solution.py:106
  305.6 30.3 %collective-permute-start.36 = (bf16[2,2,2,32,2048]{4,3,2,1,0:T(8,128)(2,1)}, bf16[2,2,2,32,2048]{4,3,2,1,0:T(8,128)(2,1)S(1)}, u32[]{:S(2)}, u32[]{:S(2)}) collective-permute-start(bf16[2,2,2,32,2048]{4,3,2,1,0:T(8,128)(2,1)} %get-tuple-element.176), channel_id=1, source_target_pairs={{0,1},{1,0},{2,3},{3,2},{4,5},{5,4},{6,7},{7,6},{8,9},{9,8},{10,11... | collective-permute-start | bytes 3145736 | tf_op jit(solution)/shard_map/ppermute | solution.py:106
  321.6 23.6 %collective-permute-start.42 = (bf16[2,256,1152]{2,1,0:T(8,128)(2,1)}, bf16[2,256,1152]{2,1,0:T(8,128)(2,1)S(1)}, u32[]{:S(2)}, u32[]{:S(2)}) collective-permute-start(bf16[2,256,1152]{2,1,0:T(8,128)(2,1)} %get-tuple-element.188), channel_id=1, source_target_pairs={{0,8},{1,9},{2,10},{3,11},{4,12},{5,13},{6,14},{7,15},{8,0},{9,1},... | collective-permute-start | bytes 3538952 | tf_op jit(solution)/shard_map/ppermute | solution.py:106
  322.9 52.2 %collective-permute-start.29 = (bf16[512,1024]{1,0:T(8,128)(2,1)S(1)}, bf16[512,1024]{1,0:T(8,128)(2,1)S(1)}, u32[]{:S(2)}, u32[]{:S(2)}) collective-permute-start(bf16[512,1024]{1,0:T(8,128)(2,1)S(1)} %copy-done.35), channel_id=1, source_target_pairs={{0,8},{1,9},{2,10},{3,11},{4,12},{5,13},{6,14},{7,15},{8,0},{9,1},... | collective-permute-start | bytes 3145736 | tf_op jit(solution)/shard_map/ppermute | solution.py:106
  342.1 18.6 %collective-permute-start.38 = (bf16[2,2,32,1024]{3,2,1,0:T(8,128)(2,1)}, bf16[2,2,32,1024]{3,2,1,0:T(8,128)(2,1)S(1)}, u32[]{:S(2)}, u32[]{:S(2)}) collective-permute-start(bf16[2,2,32,1024]{3,2,1,0:T(8,128)(2,1)} %get-tuple-element.184.refs_4_), channel_id=1, source_target_pairs={{0,1},{1,0},{2,3},{3,2},{4,5},{5,4},{6,7},{7,6},{8,9},{9,8},{10,11... | collective-permute-start | bytes 786440 | tf_op jit(solution)/shard_map/ppermute | solution.py:106
  345.2 22.7 %collective-permute-start.41 = (bf16[2,2,2,32,1024]{4,3,2,1,0:T(8,128)(2,1)}, bf16[2,2,2,32,1024]{4,3,2,1,0:T(8,128)(2,1)S(1)}, u32[]{:S(2)}, u32[]{:S(2)}) collective-permute-start(bf16[2,2,2,32,1024]{4,3,2,1,0:T(8,128)(2,1)} %get-tuple-element.187), channel_id=1, source_target_pairs={{0,16},{1,17},{2,18},{3,19},{4,20},{5,21},{6,22},{7,23},{8,24},{9,... | collective-permute-start | bytes 1572872 | tf_op jit(solution)/shard_map/ppermute | solution.py:106
  360.8 28.6 %collective-permute-start.44 = (bf16[2,2,2,32,1408]{4,3,2,1,0:T(8,128)(2,1)}, bf16[2,2,2,32,1408]{4,3,2,1,0:T(8,128)(2,1)S(1)}, u32[]{:S(2)}, u32[]{:S(2)}) collective-permute-start(bf16[2,2,2,32,1408]{4,3,2,1,0:T(8,128)(2,1)} %get-tuple-element.174.refs_5_), channel_id=1, source_target_pairs={{0,2},{1,3},{2,0},{3,1},{4,6},{5,7},{6,4},{7,5},{8,10},{9,11},{10,... | collective-permute-start | bytes 2162696 | tf_op jit(solution)/shard_map/ppermute | solution.py:106
  361.4 26.5 %collective-permute-start.45 = (bf16[2,88,1024]{2,1,0:T(8,128)(2,1)S(1)}, bf16[2,88,1024]{2,1,0:T(8,128)(2,1)S(1)}, u32[]{:S(2)}, u32[]{:S(2)}) collective-permute-start(bf16[2,88,1024]{2,1,0:T(8,128)(2,1)S(1)} %copy-done.43), channel_id=1, source_target_pairs={{0,2},{1,3},{2,0},{3,1},{4,6},{5,7},{6,4},{7,5},{8,10},{9,11},{10,... | collective-permute-start | bytes 1081352 | tf_op jit(solution)/shard_map/ppermute | solution.py:106
  373.5 22.1 %collective-permute-start.48 = (bf16[2,2,2,32,1152]{4,3,2,1,0:T(8,128)(2,1)}, bf16[2,2,2,32,1152]{4,3,2,1,0:T(8,128)(2,1)S(1)}, u32[]{:S(2)}, u32[]{:S(2)}) collective-permute-start(bf16[2,2,2,32,1152]{4,3,2,1,0:T(8,128)(2,1)} %get-tuple-element.193), channel_id=1, source_target_pairs={{0,16},{1,17},{2,18},{3,19},{4,20},{5,21},{6,22},{7,23},{8,24},{9,... | collective-permute-start | bytes 1769480 | tf_op jit(solution)/shard_map/ppermute | solution.py:106
  374.6 21.1 %collective-permute-start.43 = (bf16[2,32,3072]{2,1,0:T(8,128)(2,1)}, bf16[2,32,3072]{2,1,0:T(8,128)(2,1)S(1)}, u32[]{:S(2)}, u32[]{:S(2)}) collective-permute-start(bf16[2,32,3072]{2,1,0:T(8,128)(2,1)} %get-tuple-element.189.refs_28_), channel_id=1, source_target_pairs={{0,2},{1,3},{2,0},{3,1},{4,6},{5,7},{6,4},{7,5},{8,10},{9,11},{10,... | collective-permute-start | bytes 1179656 | tf_op jit(solution)/shard_map/ppermute | solution.py:106
  375.1 20.5 %collective-permute-start.46 = (bf16[2,2,32,1024]{3,2,1,0:T(8,128)(2,1)}, bf16[2,2,32,1024]{3,2,1,0:T(8,128)(2,1)S(1)}, u32[]{:S(2)}, u32[]{:S(2)}) collective-permute-start(bf16[2,2,32,1024]{3,2,1,0:T(8,128)(2,1)} %get-tuple-element.191), channel_id=1, source_target_pairs={{0,16},{1,17},{2,18},{3,19},{4,20},{5,21},{6,22},{7,23},{8,24},{9,... | collective-permute-start | bytes 786440 | tf_op jit(solution)/shard_map/ppermute | solution.py:106
  405.2 47.9 %collective-permute-start.49 = (bf16[32,3072]{1,0:T(8,128)(2,1)S(1)}, bf16[32,3072]{1,0:T(8,128)(2,1)S(1)}, u32[]{:S(2)}, u32[]{:S(2)}) collective-permute-start(bf16[32,3072]{1,0:T(8,128)(2,1)S(1)} %copy-done.49), channel_id=1, source_target_pairs={{0,4},{1,5},{2,6},{3,7},{4,0},{5,1},{6,2},{7,3},{8,12},{9,13},{10,... | collective-permute-start | bytes 589832 | tf_op jit(solution)/shard_map/ppermute | solution.py:106
  407.6 34.4 %collective-permute-start.54 = (bf16[2,2,32,1408]{3,2,1,0:T(8,128)(2,1)S(1)}, bf16[2,2,32,1408]{3,2,1,0:T(8,128)(2,1)S(1)}, u32[]{:S(2)}, u32[]{:S(2)}) collective-permute-start(bf16[2,2,32,1408]{3,2,1,0:T(8,128)(2,1)S(1)} %copy-done.44), channel_id=1, source_target_pairs={{0,4},{1,5},{2,6},{3,7},{4,0},{5,1},{6,2},{7,3},{8,12},{9,13},{10,... | collective-permute-start | bytes 1081352 | tf_op jit(solution)/shard_map/ppermute | solution.py:106
  408.2 33.7 %collective-permute-start.55 = (bf16[88,1024]{1,0:T(8,128)(2,1)S(1)}, bf16[88,1024]{1,0:T(8,128)(2,1)S(1)}, u32[]{:S(2)}, u32[]{:S(2)}) collective-permute-start(bf16[88,1024]{1,0:T(8,128)(2,1)S(1)} %copy-done.50), channel_id=1, source_target_pairs={{0,4},{1,5},{2,6},{3,7},{4,0},{5,1},{6,2},{7,3},{8,12},{9,13},{10,... | collective-permute-start | bytes 540680 | tf_op jit(solution)/shard_map/ppermute | solution.py:106
  415.5 37.7 %collective-permute-start.52 = (bf16[32,2048]{1,0:T(8,128)(2,1)}, bf16[32,2048]{1,0:T(8,128)(2,1)S(1)}, u32[]{:S(2)}, u32[]{:S(2)}) collective-permute-start(bf16[32,2048]{1,0:T(8,128)(2,1)} %get-tuple-element.198.refs_9_), channel_id=1, source_target_pairs={{0,4},{1,5},{2,6},{3,7},{4,0},{5,1},{6,2},{7,3},{8,12},{9,13},{10,... | collective-permute-start | bytes 393224 | tf_op jit(solution)/shard_map/ppermute | solution.py:106
  417.7 32.2 %collective-permute-start.53 = (bf16[2,32,1152]{2,1,0:T(8,128)(2,1)}, bf16[2,32,1152]{2,1,0:T(8,128)(2,1)S(1)}, u32[]{:S(2)}, u32[]{:S(2)}) collective-permute-start(bf16[2,32,1152]{2,1,0:T(8,128)(2,1)} %get-tuple-element.199), channel_id=1, source_target_pairs={{0,2},{1,3},{2,0},{3,1},{4,6},{5,7},{6,4},{7,5},{8,10},{9,11},{10,... | collective-permute-start | bytes 442376 | tf_op jit(solution)/shard_map/ppermute | solution.py:106
  (83 other events, 621.3 us)

commit v3 on v2

--- a/solution.py
+++ b/solution.py
@@ -21,6 +21,7 @@
 bf16 = jnp.bfloat16
 VMEM_LIMIT = 56 * 1024 * 1024
 PLAN = 2e9
+GROUPS = 4
 
 
 def reversed_buckets():
@@ -40,7 +41,7 @@
     return lax.dot_general(a, b, (((ca,), (cb,)), ((), ())), preferred_element_type=f32)
 
 
-def call(kernel, ins, in_specs, out_shape, out_specs, name, after=(), grid=(1,), scratch=(), prefetch=None, micros=1):
+def call(kernel, ins, in_specs, out_shape, out_specs, name, after=(), grid=(1,), scratch=(), prefetch=None, micros=1, aliases=None):
     lead = 0 if prefetch is None else 1
     n = lead + len(ins)
 
@@ -59,6 +60,7 @@
         body,
         grid_spec=spec,
         out_shape=out_shape,
+        input_output_aliases=aliases or {},
         compiler_params=pltpu.CompilerParams(vmem_limit_bytes=VMEM_LIMIT),
         cost_estimate=pl.CostEstimate(
             flops=int(micros * PLAN), bytes_accessed=1000, transcendentals=0
@@ -381,8 +383,19 @@
     return jnp.sum(turned, axis=0, keepdims=True)
 
 
-def causal_probs(low, keyval, table, g, length, valid_len):
-    s = dot(low, keyval, 1, 1)
+def batches(seqs):
+    return [[(b, g) for g in range(k, k + 4) for b in range(seqs)] for k in range(0, KVH, 4)]
+
+
+def rows_of(b, length):
+    return slice(b * length, (b + 1) * length)
+
+
+def lanes_of(g, left=0):
+    return slice(left + g * PAIR, left + (g + 1) * PAIR)
+
+
+def causal_probs(s, table, g, length, valid_len):
     bias = jnp.concatenate(
         [toeplitz(table[2 * g : 2 * g + 1], length), toeplitz(table[2 * g + 1 : 2 * g + 2], length)],
         axis=0,
@@ -407,7 +420,7 @@
 def project_memory(links, memory, blocks):
     seqs, count, width = memory.shape
     cols = KVH * PAIR
-    tile = 512
+    tile = 1024
     n = blocks.count
 
     def kernel(spot, mem_ref, *refs):
@@ -449,16 +462,18 @@
         n1_ref[...] = n1
         qkv_ref[...] = dot(n1, w_ref[...]).astype(bf16)
         tab = tab_ref[...]
-        for g in range(KVH):
-            lanes = slice(g * PAIR, (g + 1) * PAIR)
-            kv_lanes = slice(width + g * PAIR, width + (g + 1) * PAIR)
-            for b in range(seqs):
-                part = slice(b * length, (b + 1) * length)
-                keyval = qkv_ref[part, kv_lanes]
-                p = causal_probs(
-                    heads_low(qkv_ref[part, lanes]), keyval, tab, g, length, len_ref[b]
-                )
-                o1_ref[part, lanes] = merge_high(dot(p.astype(bf16), keyval)).astype(bf16)
+        for spots in batches(seqs):
+            held = [
+                (qkv_ref[rows_of(b, length), lanes_of(g)], qkv_ref[rows_of(b, length), lanes_of(g, width)])
+                for b, g in spots
+            ]
+            scores = [dot(heads_low(q), keyval, 1, 1) for q, keyval in held]
+            probs = [
+                causal_probs(s, tab, g, length, len_ref[b]).astype(bf16)
+                for s, (b, g) in zip(scores, spots)
+            ]
+            for p, (_, keyval), (b, g) in zip(probs, held, spots):
+                o1_ref[rows_of(b, length), lanes_of(g)] = merge_high(dot(p, keyval)).astype(bf16)
         x1_ref[...] = xf + dot(o1_ref[...], wo_ref[...])
 
     return call(
@@ -485,6 +500,7 @@
     seqs, _, count = keyval.shape
     length = rows // seqs
     n = blocks.count * 2
+    steps = KVH // GROUPS
 
     def kernel(spot, x1_ref, kv_ref, g2_ref, g3_ref, *refs):
         n2_ref, q2_ref, o2_ref, x2_ref, n3_ref, p_ref, wq_ref, wo_ref = refs[n:]
@@ -500,15 +516,19 @@
             q2_ref[...] = dot(n2, wq_ref[...]).astype(bf16)
 
         part = pl.ds(pl.multiple_of(b * length, length), length)
-        lanes = pl.ds(pl.multiple_of(g * PAIR, PAIR), PAIR)
-        kv = kv_ref[0]
-        s = dot(heads_low(q2_ref[part, lanes]), kv)
-        e = jnp.exp(s - jnp.max(s, axis=-1, keepdims=True))
-        p = (e * (1.0 / jnp.sum(e, axis=-1, keepdims=True))).astype(bf16)
-        p_ref[0] = p
-        o2_ref[part, lanes] = merge_high(dot(p, kv, 1, 1)).astype(bf16)
-
-        @pl.when((b == seqs - 1) & (g == KVH - 1))
+        lanes = [pl.ds(pl.multiple_of((g * GROUPS + i) * PAIR, PAIR), PAIR) for i in range(GROUPS)]
+        scores = [
+            dot(heads_low(q2_ref[part, lanes[i]]), kv_ref[0, i * PAIR : (i + 1) * PAIR])
+            for i in range(GROUPS)
+        ]
+        for i, s in enumerate(scores):
+            e = jnp.exp(s - jnp.max(s, axis=-1, keepdims=True))
+            p_ref[i] = (e * (1.0 / jnp.sum(e, axis=-1, keepdims=True))).astype(bf16)
+        for i in range(GROUPS):
+            mixed = dot(p_ref[i], kv_ref[0, i * PAIR : (i + 1) * PAIR], 1, 1)
+            o2_ref[part, lanes[i]] = merge_high(mixed).astype(bf16)
+
+        @pl.when((b == seqs - 1) & (g == steps - 1))
         def _():
             x2 = x1_ref[...] + dot(o2_ref[...], wo_ref[...])
             x2_ref[...] = x2
@@ -520,7 +540,7 @@
         [
             smem(),
             whole((rows, width)),
-            pl.BlockSpec((1, PAIR, count), lambda b, g: (b, g, 0)),
+            pl.BlockSpec((1, GROUPS * PAIR, count), lambda b, g: (b, g, 0)),
             whole((1, width)),
             whole((1, width)),
         ]
@@ -535,11 +555,11 @@
             struct((seqs * KVH, 2 * length, count), bf16),
         ),
         [whole((rows, width))] * 5
-        + [pl.BlockSpec((1, 2 * length, count), lambda b, g: (b * KVH + g, 0, 0))],
+        + [pl.BlockSpec((GROUPS, 2 * length, count), lambda b, g: (b * steps + g, 0, 0))],
         "cross_forward",
         micros=34,
         after=after,
-        grid=(seqs, KVH),
+        grid=(seqs, steps),
         scratch=[pltpu.VMEM((width, width), bf16)] * 2,
     )
 
@@ -550,26 +570,50 @@
         out[i * rows : (i + 1) * rows] = ref[...]
 
 
-def feed_through(links, n3s, cots, blocks, w_down, after):
-    rows, width = n3s[0].shape
+def feed_prepare(links, cots, blocks, w_down, after):
+    rows, width = cots[0].shape
     units = w_down.shape[0]
     n = blocks.count
+
+    def kernel(spot, *refs):
+        wd_ref = refs[4]
+        wg_ref, wu_ref, dh_ref, cot_all = refs[5 + n :]
+        blocks.put(spot, refs[5 : 5 + n], wg_ref, wu_ref)
+        stack_rows(refs[:4], cot_all)
+        dh_ref[...] = dot(cot_all[...], wd_ref[...], 1, 1)
+
+    return call(
+        kernel,
+        [links.spot, *cots, w_down] + blocks.arrays,
+        [smem()] + [whole((rows, width))] * 4 + [whole(w_down.shape)] + blocks.specs(),
+        (
+            struct((width, units), bf16),
+            struct((width, units), bf16),
+            struct((4 * rows, units), f32),
+        ),
+        [whole((width, units))] * 2 + [whole((4 * rows, units))],
+        "feed_prepare",
+        micros=6,
+        after=after,
+        scratch=[pltpu.VMEM((4 * rows, width), bf16)],
+    )
+
+
+def feed_through(n3s, w_gate, w_up, dh, after):
+    rows, width = n3s[0].shape
+    units = w_gate.shape[1]
     c0 = np.float32(np.sqrt(2.0 / np.pi))
     c1 = np.float32(0.044715)
     cuts = [slice(i, min(i + 256, units)) for i in range(0, units, 256)]
 
-    def kernel(spot, *refs):
-        wd_ref = refs[8]
-        held = refs[9 : 9 + n]
-        hid_ref, dgate_ref, dup_ref, dn_ref, dn_hi_ref, dn_away_ref = refs[9 + n : 15 + n]
-        wg_ref, wu_ref, n3_all, cot_all = refs[15 + n :]
-        blocks.put(spot, held, wg_ref, wu_ref)
+    def kernel(*refs):
+        wg_ref, wu_ref, dh_ref = refs[4:7]
+        hid_ref, dgate_ref, dup_ref, dn_ref, dn_hi_ref, dn_away_ref, n3_all = refs[7:]
         stack_rows(refs[:4], n3_all)
-        stack_rows(refs[4:8], cot_all)
         for cut in cuts:
             gate = dot(n3_all[...], wg_ref[:, cut])
             up = dot(n3_all[...], wu_ref[:, cut])
-            dh = dot(cot_all[...], wd_ref[cut, :], 1, 1)
+            dh = dh_ref[:, cut]
             square = gate * gate
             t = jnp.tanh(c0 * (gate + c1 * (square * gate)))
             cdf = 0.5 * (1.0 + t)
@@ -588,8 +632,8 @@
 
     return call(
         kernel,
-        [links.spot, *n3s, *cots, w_down] + blocks.arrays,
-        [smem()] + [whole((rows, width))] * 8 + [whole(w_down.shape)] + blocks.specs(),
+        [*n3s, w_gate, w_up, dh],
+        [whole((rows, width))] * 4 + [whole((width, units))] * 2 + [whole((4 * rows, units))],
         (
             struct((4 * rows, units), bf16),
             struct((4 * rows, units), bf16),
@@ -602,43 +646,42 @@
         "feed_through",
         micros=14,
         after=after,
-        scratch=[
-            pltpu.VMEM((width, units), bf16),
-            pltpu.VMEM((width, units), bf16),
-            pltpu.VMEM((4 * rows, width), bf16),
-            pltpu.VMEM((4 * rows, width), bf16),
-        ],
+        scratch=[pltpu.VMEM((4 * rows, width), bf16)],
     )
 
 
 def feed_weight_grads(n3s, cots, hidden, dgate, dup, w_down, after):
     rows, width = n3s[0].shape
     units = hidden.shape[1]
+    tile = 256
 
     def kernel(*refs):
         hid_ref, dgate_ref, dup_ref, wd_ref = refs[8:12]
         y_ref, y_hi_ref, y_away_ref, gu_ref, gd_ref, n3t_ref, cot_all, hid_t = refs[12:]
+
+        @pl.when(pl.program_id(0) == 0)
+        def _():
+            hid_t[...] = hid_ref[...].T
+
         for i in range(4):
             n3t_ref[:, i * rows : (i + 1) * rows] = refs[i][...].T
         stack_rows(refs[4:8], cot_all)
-        hid_t[...] = hid_ref[...].T
-        for i in range(0, width, 256):
-            gu_ref[i : i + 256, :units] = dot(n3t_ref[i : i + 256], dgate_ref[...]).astype(bf16)
-            gu_ref[i : i + 256, units:] = dot(n3t_ref[i : i + 256], dup_ref[...]).astype(bf16)
-        for i in range(0, units, 352):
-            gd_ref[i : i + 352] = dot(hid_t[i : i + 352], cot_all[...]).astype(bf16)
-        for i in range(0, width, 256):
-            at = slice(i, i + 256)
-            y = dot(hid_ref[...], wd_ref[:, at])
-            y_ref[:, at] = y[:rows]
-            y_away_ref[:rows, at] = y[rows : 2 * rows].astype(bf16)
-            y_hi_ref[:, at] = y[2 * rows : 3 * rows]
-            y_away_ref[rows:, at] = y[3 * rows :].astype(bf16)
+        gu_ref[:, :units] = dot(n3t_ref[...], dgate_ref[...]).astype(bf16)
+        gu_ref[:, units:] = dot(n3t_ref[...], dup_ref[...]).astype(bf16)
+        gd_ref[...] = dot(hid_t[...], cot_all[...]).astype(bf16)
+        y = dot(hid_ref[...], wd_ref[...])
+        y_ref[...] = y[:rows]
+        y_away_ref[:rows] = y[rows : 2 * rows].astype(bf16)
+        y_hi_ref[...] = y[2 * rows : 3 * rows]
+        y_away_ref[rows:] = y[3 * rows :].astype(bf16)
+
+    def columns(count):
+        return pl.BlockSpec((count, tile), lambda t: (0, t))
 
     return call(
         kernel,
         [*n3s, *cots, hidden, dgate, dup, w_down],
-        [whole((rows, width))] * 8 + [whole((4 * rows, units))] * 3 + [whole(w_down.shape)],
+        [columns(rows)] * 8 + [whole((4 * rows, units))] * 3 + [columns(units)],
         (
             struct((rows, width), f32),
             struct((rows, width), f32),
@@ -646,14 +689,15 @@
             struct((width, 2 * units), bf16),
             struct((units, width), bf16),
         ),
-        [whole((rows, width))] * 2
-        + [whole((2 * rows, width)), whole((width, 2 * units)), whole((units, width))],
+        [columns(rows)] * 2
+        + [columns(2 * rows), pl.BlockSpec((tile, 2 * units), lambda t: (t, 0)), columns(units)],
         "feed_weight_grads",
         micros=12,
         after=after,
+        grid=(width // tile,),
         scratch=[
-            pltpu.VMEM((width, 4 * rows), bf16),
-            pltpu.VMEM((4 * rows, width), bf16),
+            pltpu.VMEM((tile, 4 * rows), bf16),
+            pltpu.VMEM((4 * rows, tile), bf16),
             pltpu.VMEM((units, 4 * rows), bf16),
         ],
     )
@@ -702,34 +746,30 @@
     rows, width = q2.shape
     seqs, cols, count = keyval.shape
     length = rows // seqs
-    chunk = 512
+    steps = KVH // GROUPS
 
     def kernel(q_ref, do_ref, o_ref, kv_ref, p_ref, dq_ref, dkv_ref):
-        q, do = q_ref[...], do_ref[...]
-        low, high = heads_low(q), heads_high(do)
-        low_t, high_t = low.T, high.T
-        product = do.astype(f32) * o_ref[...].astype(f32)
-        keep = low_lanes(product.shape)
-        inner = jnp.concatenate(
-            [
-                jnp.sum(jnp.where(keep, product, 0.0), axis=-1, keepdims=True),
-                jnp.sum(jnp.where(keep, 0.0, product), axis=-1, keepdims=True),
-            ],
-            axis=0,
-        )
-        dq = jnp.zeros((2 * length, PAIR), f32)
-        for c in range(count // chunk):
-            cut = slice(c * chunk, (c + 1) * chunk)
-            kv = kv_ref[0, :, cut]
-            p = p_ref[0, :, cut]
-            dp = dot(high, kv)
-            ds = (p.astype(f32) * (dp - inner)).astype(bf16)
-            dq += dot(ds, kv, 1, 1)
-            dkv_ref[0, :, cut] = (dot(low_t, ds) + dot(high_t, p)).astype(bf16)
-        dq_ref[...] = merge_low(dq).astype(bf16)
-
-    heads_block = pl.BlockSpec((length, PAIR), lambda b, g: (b, g))
-    kv_block = pl.BlockSpec((1, PAIR, count), lambda b, g: (b, g, 0))
+        for i in range(GROUPS):
+            lanes = slice(i * PAIR, (i + 1) * PAIR)
+            q, do = q_ref[:, lanes], do_ref[:, lanes]
+            low, high = heads_low(q), heads_high(do)
+            product = do.astype(f32) * o_ref[:, lanes].astype(f32)
+            keep = low_lanes(product.shape)
+            inner = jnp.concatenate(
+                [
+                    jnp.sum(jnp.where(keep, product, 0.0), axis=-1, keepdims=True),
+                    jnp.sum(jnp.where(keep, 0.0, product), axis=-1, keepdims=True),
+                ],
+                axis=0,
+            )
+            kv = kv_ref[0, lanes]
+            p = p_ref[i]
+            ds = (p.astype(f32) * (dot(high, kv) - inner)).astype(bf16)
+            dq_ref[:, lanes] = merge_low(dot(ds, kv, 1, 1)).astype(bf16)
+            dkv_ref[0, lanes] = (dot(low.T, ds) + dot(high.T, p)).astype(bf16)
+
+    heads_block = pl.BlockSpec((length, GROUPS * PAIR), lambda b, g: (b, g))
+    kv_block = pl.BlockSpec((1, GROUPS * PAIR, count), lambda b, g: (b, g, 0))
     return call(
         kernel,
         [q2, do2, o2, keyval, probs],
@@ -738,21 +778,21 @@
             heads_block,
             heads_block,
             kv_block,
-            pl.BlockSpec((1, 2 * length, count), lambda b, g: (b * KVH + g, 0, 0)),
+            pl.BlockSpec((GROUPS, 2 * length, count), lambda b, g: (b * steps + g, 0, 0)),
         ],
         (struct((rows, width), bf16), struct((seqs, cols, count), bf16)),
         [heads_block, kv_block],
         "cross_backward",
         micros=25,
         after=after,
-        grid=(seqs, KVH),
+        grid=(seqs, steps),
     )
 
 
 def keyval_weight_grad(links, memory, grad_keyval, small, after):
     seqs, count, width = memory.shape
     cols = grad_keyval.shape[1]
-    tile = 512
+    tile = 1024
     steps = count // tile
     wide = cols + EXTRA
     split = (2, width // 4, wide)
@@ -802,16 +842,17 @@
     )
 
 
-def memory_gradient(links, grad_keyval, blocks, after):
+def memory_gradient(links, grad_keyval, blocks, b, before, after):
     seqs, cols, count = grad_keyval.shape
     width = cols
-    tile = 512
+    tile = 1024
     n = blocks.count
+    given = () if before is None else (before,)
 
     def kernel(spot, dkv_ref, *refs):
-        out_ref, w_ref = refs[n:]
-
-        @pl.when((pl.program_id(0) == 0) & (pl.program_id(1) == 0))
+        out_ref, w_ref = refs[n + len(given) :]
+
+        @pl.when(pl.program_id(0) == 0)
         def _():
             blocks.put(spot, refs[:n], w_ref)
 
@@ -819,15 +860,18 @@
 
     return call(
         kernel,
-        [links.spot, grad_keyval] + blocks.arrays,
-        [smem(), pl.BlockSpec((1, cols, tile), lambda b, t: (b, 0, t))] + blocks.specs(cols, 0),
+        [links.spot, grad_keyval] + blocks.arrays + list(given),
+        [smem(), pl.BlockSpec((1, cols, tile), lambda t: (b, 0, t))]
+        + blocks.specs(cols, 0)
+        + [pl.BlockSpec(memory_space=pl.ANY)] * len(given),
         struct((seqs, count, width), bf16),
-        pl.BlockSpec((1, tile, width), lambda b, t: (b, t, 0)),
+        pl.BlockSpec((1, tile, width), lambda t: (b, t, 0)),
         "memory_gradient",
-        micros=15,
+        micros=8,
         after=after,
-        grid=(seqs, count // tile),
+        grid=(count // tile,),
         scratch=[pltpu.VMEM((width, cols), bf16)],
+        aliases={2 + n: 0} if given else {},
     )
 
 
@@ -894,27 +938,36 @@
         i = lax.broadcasted_iota(jnp.int32, (length, length), 0)
         j = lax.broadcasted_iota(jnp.int32, (length, length), 1)
         flip = jnp.where(i + j == length - 1, 1.0, 0.0).astype(bf16)
-        for g in range(KVH):
-            lanes = slice(g * PAIR, (g + 1) * PAIR)
-            kv_lanes = slice(width + g * PAIR, width + (g + 1) * PAIR)
-            even_sum = jnp.zeros((length, length), f32)
-            odd_sum = jnp.zeros((length, length), f32)
-            for b in range(seqs):
-                part = slice(b * length, (b + 1) * length)
-                keyval = qkv_ref[part, kv_lanes]
-                low = heads_low(qkv_ref[part, lanes])
-                high = heads_high(do_ref[part, lanes])
-                p = causal_probs(low, keyval, tab, g, length, len_ref[b])
-                dp = dot(high, keyval, 1, 1)
-                ds = (p * (dp - jnp.sum(p * dp, axis=-1, keepdims=True))).astype(bf16)
-                even_sum += dot(flip, ds[:length])
-                odd_sum += dot(flip, ds[length:])
-                dqkv_ref[part, lanes] = merge_low(dot(ds, keyval)).astype(bf16)
-                dqkv_ref[part, kv_lanes] = (
+        for spots in batches(seqs):
+            held = [
+                (
+                    heads_low(qkv_ref[rows_of(b, length), lanes_of(g)]),
+                    heads_high(do_ref[rows_of(b, length), lanes_of(g)]),
+                    qkv_ref[rows_of(b, length), lanes_of(g, width)],
+                )
+                for b, g in spots
+            ]
+            scores = [dot(low, keyval, 1, 1) for low, _, keyval in held]
+            dps = [dot(high, keyval, 1, 1) for _, high, keyval in held]
+            probs = [causal_probs(s, tab, g, length, len_ref[b]) for s, (b, g) in zip(scores, spots)]
+            dss = [
+                (p * (dp - jnp.sum(p * dp, axis=-1, keepdims=True))).astype(bf16)
+                for p, dp in zip(probs, dps)
+            ]
+            for ds, p, (low, high, keyval), (b, g) in zip(dss, probs, held, spots):
+                part = rows_of(b, length)
+                dqkv_ref[part, lanes_of(g)] = merge_low(dot(ds, keyval)).astype(bf16)
+                dqkv_ref[part, lanes_of(g, width)] = (
                     dot(ds.T, low) + dot(p.astype(bf16).T, high)
                 ).astype(bf16)
-            bias_ref[2 * g : 2 * g + 1] = diagonal_sums(even_sum)
-            bias_ref[2 * g + 1 : 2 * g + 2] = diagonal_sums(odd_sum)
+            for i in range(0, len(spots), seqs):
+                g = spots[i][1]
+                for side in range(2):
+                    total = None
+                    for ds in dss[i : i + seqs]:
+                        term = dot(flip, ds[side * length : (side + 1) * length])
+                        total = term if total is None else total + term
+                    bias_ref[2 * g + side : 2 * g + side + 1] = diagonal_sums(total)
         dqkv = dqkv_ref[...]
         n1t_ref[...] = n1_ref[...].T
         grad_rows, grad_gain = norm_back(
@@ -1044,12 +1097,11 @@
     keyval, small_all = project_memory(
         links, tie(memory, stack, first_far[0], feed_near), first_blocks
     )
-    down_one = links.grow((feed_down[None], near), bits[:1], stack, feed_near, then=(keyval,))
     feed_one = links.grow((feed_near[None], near), bits[:1], stack, then=(keyval,))
-    left_two = links.send(left_one[0], "hi", keyval, down_one[0], feed_one[0])
-    right_two = links.send(right_one[0], "lo", keyval, down_one[0], feed_one[0])
-    down_ring = links.grow(down_one, bits[1:], keyval)
-    feed_ring = links.grow(feed_one, bits[1:], keyval)
+    left_two = links.send(left_one[0], "hi", keyval, feed_one[0])
+    right_two = links.send(right_one[0], "lo", keyval, feed_one[0])
+    feed_ring = links.grow(feed_one, bits[1:], keyval, then=(left_two, right_two))
+    down_one = links.grow((feed_down[None], near), bits[:1], feed_one[0], left_one[0])
     n = len(fars)
     second_near = jnp.concatenate(
         [
@@ -1060,11 +1112,14 @@
         ],
         axis=2,
     )
-    second_near = tie(second_near, down_ring[0], feed_ring[0])
+    down_ring = links.grow(down_one, bits[1:], then=(left_two, right_two))
+    second_near = tie(second_near, feed_ring[0], down_ring[0])
     cot_both = links.send(cot_hi, "core", second_near)
     second_fars = left_one[1] + [f | {"hi"} for f in left_one[1]]
     second_far = links.send(second_near, "core"), [f | {"core"} for f in second_fars]
     second_blocks = Blocks(links, (second_near, second_fars), second_far)
+    feed_far = links.send(feed_ring[0], "lo", right_two), [f | {"lo"} for f in feed_ring[1]]
+    feed_blocks = Blocks(links, feed_ring, feed_far, quads=True)
     down_far = links.send(down_ring[0], "lo", right_two), [f | {"lo"} for f in down_ring[1]]
     cots = (cot, cot_core, cot_hi, cot_both)
 
@@ -1074,21 +1129,18 @@
     table = jnp.dot(bias_all.astype(bf16), onehot.astype(bf16), preferred_element_type=f32)
 
     x1, n1, qkv1, o1 = causal_forward(
-        links, inputs, second_blocks, gain_one, table, lengths, (keyval, feed_ring[0], down_ring[0])
-    )
-    w_down = assemble(links, (down_ring, down_far), (x1,))
-    feed_far = links.send(feed_ring[0], "lo", x1), [f | {"lo"} for f in feed_ring[1]]
-    feed_blocks = Blocks(links, feed_ring, feed_far, quads=True)
+        links, inputs, second_blocks, gain_one, table, lengths, (keyval,)
+    )
     n2, q2, o2, x2, n3, probs = cross_forward(
-        links, x1, keyval, second_blocks, gain_two, gain_three, (w_down,)
+        links, x1, keyval, second_blocks, gain_two, gain_three, ()
     )
     n3_hi = links.send(n3, "hi")
     n3_core = links.send(n3, "core")
-    n3_both = links.send(n3_hi, "core")
+    w_down = assemble(links, (down_ring, down_far), (n3,))
+    w_gate, w_up, dh = feed_prepare(links, cots, feed_blocks, w_down, (n3,))
+    n3_both = links.send(n3_hi, "core", dh)
     n3s = (n3, n3_core, n3_hi, n3_both)
-    hidden, dgate, dup, dn3, dn3_hi, dn3_away = feed_through(
-        links, n3s, cots, feed_blocks, w_down, ()
-    )
+    hidden, dgate, dup, dn3, dn3_hi, dn3_away = feed_through(n3s, w_gate, w_up, dh, ())
 
     dn3_got = links.send(dn3_away, "core")
     dn3_passed = (dn3_hi + dn3_got[rows:].astype(f32)).astype(bf16)
@@ -1127,18 +1179,17 @@
     dx1, do1, keep, away, grad_gain_two = causal_enter(
         links, dx2, x1, gain_two, n2, dq2, o1, second_blocks, ()
     )
-    early_sums += halves(keep, away, lo_hi, (0, 2 * width))
+    done = advance(links, early_sums, (dx1,))
+    o1q2_sums = halves(keep, away, hi_lo, (0, 2 * width))
     y_passed = (tie(y_hi, dx1) + y_got[rows:].astype(f32)).astype(bf16)
     y_terms = (y, y_got[:rows], links.send(y_passed, "hi"))
     keep, away, grad_gain_one, grad_bias, input_grad = causal_backward(
-        links, lengths, dx1, do1, qkv1, n1, x, gain_one, table, second_blocks, ()
-    )
-    middle_sums = halves(keep, away, lo_hi, (0, width))
-    middle_sums += [
-        Sum([Leaf(leaf.array, leaf.axes, width, width) for leaf in middle_sums[0].leaves], hi_lo + back)
-    ]
+        links, lengths, dx1, do1, qkv1, n1, x, gain_one, table, second_blocks, done
+    )
+    middle_sums = halves(keep, away, hi_lo, (0, 2 * width))
     done = advance(links, feed_sums, (input_grad,))
-    done = advance(links, early_sums, done)
+    done = advance(links, o1q2_sums, (*done, early_sums[0].leaves[-1].array, y_terms[2]))
+    early_sums += o1q2_sums
 
     grad_table = lax.dot_general(
         grad_bias, onehot, (((1,), (1,)), ((), ())), precision=lax.Precision.HIGHEST
@@ -1151,12 +1202,13 @@
         axis=0,
     )
     keep, away = keyval_weight_grad(links, memory, grad_keyval, small_rows, done)
-    late_sums = halves(keep, away, hi_lo, (0, KVH * PAIR + EXTRA))
-    done = advance(links, early_sums + middle_sums, (keep,))
-    memory_grad = memory_gradient(links, grad_keyval, first_blocks, done)
-    done = advance(links, early_sums + middle_sums + late_sums, (memory_grad,))
-    done = advance(links, feed_sums + early_sums + middle_sums + late_sums, done)
-    done = advance(links, middle_sums + late_sums, done)
+    late_sums = halves(keep, away, lo_hi, (0, KVH * PAIR + EXTRA))
+    memory_grad = memory_gradient(links, grad_keyval, first_blocks, 0, None, (keep,))
+    done = advance(links, feed_sums + early_sums + middle_sums + late_sums, (memory_grad,))
+    for b in range(1, seqs):
+        memory_grad = memory_gradient(links, grad_keyval, first_blocks, b, memory_grad, done)
+    done = (memory_grad,)
+    done = advance(links, early_sums + middle_sums + late_sums, done)
     half = width // 2
     while feed_sums[0].ways:
         done = advance(links, feed_sums, done)
@@ -1165,12 +1217,14 @@
     while late_sums[0].ways:
         done = advance(links, [one for one in early_sums + middle_sums + late_sums if one.ways], done)
     wide = links.unquarter(sum_gu, done)
-    sum_o2, sum_o1, sum_q2, sum_q1, sum_k1, sum_v1 = finish(
-        links, early_sums + middle_sums, [(width,), (width, width), (width,), (half, half)], done
-    )
-    sum_k2, sum_v2, sum_small = finish(links, late_sums, [(half, half, EXTRA)], (sum_o2,))
-
-    layer_out = (x2 + sum(t.astype(f32) for t in y_terms)).astype(bf16)
+    sum_o2, sum_o1, sum_q2, sum_q1, sum_k1, sum_v1, sum_k2, sum_v2, sum_small = finish(
+        links,
+        early_sums + middle_sums + late_sums,
+        [(width,), (width, width), (width, half, half), (half, half, EXTRA)],
+        done,
+    )
+
+    layer_out = (x2 + sum(tie(t, memory_grad).astype(f32) for t in y_terms)).astype(bf16)
     sum_gate, sum_up = (
         jnp.concatenate([part[:, i * units : (i + 1) * units] for part in wide], axis=1)
         for i in range(2)

time: 472 us -> 417 us (0.88)
  waiting for transfers between devices: 151 us -> 98.7 us
  Pallas kernels: 214 us -> 207 us
    ppermute x60 -> x55, waiting for transfers between devices: 151 us -> 98.7 us  [send(): return lax.ppermute(tie(a, *after), AXES, self.pairs[way])]
    pallas_call x23 -> x24, Pallas kernels: 214 us -> 207 us  [call(): pl.pallas_call(body, grid_spec=spec, out_shape=out_shape, input_output_al...]
    unnamed x123 -> x112, local copies, waits for them, and re-layouts: 15.9 us -> 18.6 us
    ppermute x60 -> x55, starting transfers between devices: 56.2 us -> 57 us  [send(): return lax.ppermute(tie(a, *after), AXES, self.pairs[way])]
  transfers between devices with their start and end apart: 60 -> 55, of which waited for: 24 -> 21; matrix products, arithmetic and copies ran while one was open for 3% -> 5% of each run, Pallas kernels for 42% -> 44%
where the time goes in v3:
time: 417 us; the launch traced here: 411 us
  Pallas kernels  207 us (50%)
  waiting for transfers between devices  98.7 us (24%)
  starting transfers between devices  57 us (14%)
  local copies, waits for them, and re-layouts  35.8 us (9%)
  other arithmetic  8.52 us (2%)
    pallas_call x24, Pallas kernels, call(): pl.pallas_call(body, grid_spec=spec, out_shape=out_shape, input_output_al...  207 us
    ppermute x55, waiting for transfers between devices, send(): return lax.ppermute(tie(a, *after), AXES, self.pairs[way])  98.7 us
    ppermute x55, starting transfers between devices, send(): return lax.ppermute(tie(a, *after), AXES, self.pairs[way])  57 us
    unnamed x112, local copies, waits for them, and re-layouts  18.6 us
  transfers between devices with their start and end apart: 55, of which 21 were waited for; matrix products, arithmetic and copies ran while one was open for 5% of the time, Pallas kernels for 44%

profile of v3, /device:TPU:0, one launch (start us, length us, event | category | flops | bytes accessed | tf_op | source)
XLA Modules:
  0.0 410.6 jit_solution(1426269387817027851)
XLA Ops:
  5.7 4.1 collective-permute-start
  15.6 3.7 collective-permute-done.1
  23.3 3.6 collective-permute-done.3
  30.2 6.9 %collective-permute-done.2 = bf16[1,32,5120]{2,1,0:T(8,128)(2,1)S(1)} collective-permute-done((bf16[1,32,5120]{2,1,0:T(8,128)(2,1)S(1)}, bf16[1,32,5120]{2,1,0:T(8,128)(2,1)S(1)}, u32[]{:S(2)}, u32[]{:S(2)}) %collective-permute-start.2) | collective-permute-done | bytes 327712 | tf_op jit(solution)/shard_map/ppermute | solution.py:108
  37.2 6.1 %collective-permute-done.4 = bf16[8,32,1152]{2,1,0:T(8,128)(2,1)S(1)} collective-permute-done((bf16[8,32,1152]{2,1,0:T(8,128)(2,1)S(1)}, bf16[8,32,1152]{2,1,0:T(8,128)(2,1)S(1)}, u32[]{:S(2)}, u32[]{:S(2)}) %collective-permute-start.4) | collective-permute-done | bytes 589856 | tf_op jit(solution)/shard_map/ppermute | solution.py:108
  46.0 5.4 %collective-permute-done.8.refs_3_.refs_6_ = bf16[256,1024]{1,0:T(8,128)(2,1)} collective-permute-done((bf16[256,1024]{1,0:T(8,128)(2,1)S(1)}, bf16[256,1024]{1,0:T(8,128)(2,1)}, u32[]{:S(2)}, u32[]{:S(2)}) %collective-permute-start.8) | collective-permute-done | bytes 524320 | tf_op jit(solution)/shard_map/ppermute | solution.py:108
  58.6 3.6 collective-permute-start.13
  64.7 14.1 %project_memory.1 = (bf16[2,1024,2048]{2,1,0:T(8,128)(2,1)}, f32[8,1024]{1,0:T(8,128)}) custom-call(s32[6]{0:T(128)} %stack.66.refs_0_, bf16[2,2048,1024]{2,1,0:T(8,128)(2,1)} %refs_1_.6, bf16[16,32,1152]{2,1,0:T(8,128)(2,1)} %constant_dynamic-update-slice_fusion.4.refs_2_, bf16[16,32,1152]{2,1,0:T(8,128)(2,1)} %copy-done.32), custom_call_target="tpu_custom_call" | custom-call | flops 30000001024 | bytes 1000 | tf_op jit(solution)/shard_map/project_memory/pallas_call | solution.py:59
  82.1 3.7 collective-permute-start.17
  85.8 6.5 %collective-permute-done.18 = bf16[1,88,1024]{2,1,0:T(8,128)(2,1)S(1)} collective-permute-done((bf16[1,88,1024]{2,1,0:T(8,128)(2,1)S(1)}, bf16[1,88,1024]{2,1,0:T(8,128)(2,1)S(1)}, u32[]{:S(2)}, u32[]{:S(2)}) %collective-permute-start.18) | collective-permute-done | bytes 180256 | tf_op jit(solution)/shard_map/ppermute | solution.py:108
  92.5 16.7 %collective-permute-done.16 = bf16[8,32,2560]{2,1,0:T(8,128)(2,1)S(1)} collective-permute-done((bf16[8,32,2560]{2,1,0:T(8,128)(2,1)S(1)}, bf16[8,32,2560]{2,1,0:T(8,128)(2,1)S(1)}, u32[]{:S(2)}, u32[]{:S(2)}) %collective-permute-start.16) | collective-permute-done | bytes 1310752 | tf_op jit(solution)/shard_map/ppermute | solution.py:108
  117.6 4.9 %collective-permute-done.20.refs_6_.refs_8_.refs_9_.refs_10_ = bf16[16,32,5120]{2,1,0:T(8,128)(2,1)} collective-permute-done((bf16[16,32,5120]{2,1,0:T(8,128)(2,1)}, bf16[16,32,5120]{2,1,0:T(8,128)(2,1)}, u32[]{:S(2)}, u32[]{:S(2)}) %collective-permute-start.20) | collective-permute-done | bytes 5242912 | tf_op jit(solution)/shard_map/ppermute | solution.py:108
  122.6 8.1 %causal_forward.1 = (f32[256,1024]{1,0:T(8,128)}, bf16[256,1024]{1,0:T(8,128)(2,1)}, bf16[256,2048]{1,0:T(8,128)(2,1)}, bf16[256,1024]{1,0:T(8,128)(2,1)}) custom-call(s32[6]{0:T(128)} %stack.66.refs_0_, s32[2]{0:T(128)} %refs_1_.5, bf16[256,1024]{1,0:T(8,128)(2,1)} %bitcast.160, f32[1,1024]{1,0:T(1,128)} %get-tuple-element.252.refs_3_.refs_7_, ...), custom_call_target="tpu_custom_call" | custom-call | flops 17999998976 | bytes 1000 | tf_op jit(solution)/shard_map/causal_forward/pallas_call | solution.py:59
  130.7 33.6 %cross_forward.1 = (bf16[256,1024]{1,0:T(8,128)(2,1)}, bf16[256,1024]{1,0:T(8,128)(2,1)}, bf16[256,1024]{1,0:T(8,128)(2,1)}, f32[256,1024]{1,0:T(8,128)}, bf16[2...) custom-call(s32[6]{0:T(128)} %stack.66.refs_0_, f32[256,1024]{1,0:T(8,128)} %get-tuple-element.135.refs_1_.refs_2_, ...), custom_call_target="tpu_custom_call" | custom-call | flops 67999997952 | bytes 1000 | tf_op jit(solution)/shard_map/cross_forward/pallas_call | solution.py:59
  171.2 7.4 %feed_prepare.1 = (bf16[1024,704]{1,0:T(8,128)(2,1)}, bf16[1024,704]{1,0:T(8,128)(2,1)}, f32[1024,704]{1,0:T(8,128)}) custom-call(s32[6]{0:T(128)} %stack.66.refs_0_, bf16[256,1024]{1,0:T(8,128)(2,1)} %bitcast.155, bf16[256,1024]{1,0:T(8,128)(2,1)} %collective-permute-done.7.refs_2_.refs_5_, bf16[256,1024]{1,0:T(8,128)(2,1)} %collective-permute-done.8.refs_3_.refs_6_, ...), custom_call_target="tpu_custom_call" | custom-call | flops 12000000000 | bytes 1000 | tf_op jit(solution)/shard_map/feed_prepare/pallas_call | solution.py:59
  181.6 12.9 %feed_through.1 = (bf16[1024,704]{1,0:T(8,128)(2,1)}, bf16[1024,704]{1,0:T(8,128)(2,1)}, bf16[1024,704]{1,0:T(8,128)(2,1)}, f32[256,1024]{1,0:T(8,128)}, f32[256,1024]{1,0:T(8,128)}, /*index=5*/bf16[512,1024]{1,0:T(8,128)(2,1)}) custom-call(bf16[256,1024]{1,0:T(8,128)(2,1)} %get-tuple-element.137.refs_3_.refs_8_.refs_0_, bf16[256,1024]{1,0:T(8,128)(2,1)} %copy-done.38, ...), custom_call_target="tpu_custom_call" | custom-call | flops 28000000000 | bytes 1000 | tf_op jit(solution)/shard_map/feed_through/pallas_call | solution.py:59
  200.4 12.5 %feed_weight_grads.1 = (f32[256,1024]{1,0:T(8,128)}, f32[256,1024]{1,0:T(8,128)}, bf16[512,1024]{1,0:T(8,128)(2,1)}, bf16[1024,1408]{1,0:T(8,128)(2,1)}, bf16[704,1024]{1,0:T(8,128)(2,1)}) custom-call(bf16[256,1024]{1,0:T(8,128)(2,1)} %get-tuple-element.137.refs_3_.refs_8_.refs_0_, bf16[256,1024]{1,0:T(8,128)(2,1)} %copy-done.38, ...), custom_call_target="tpu_custom_call" | custom-call | flops 24000000000 | bytes 1000 | tf_op jit(solution)/shard_map/feed_weight_grads/pallas_call | solution.py:59
  213.0 3.6 combine.8
  220.3 6.2 %cross_enter.1 = (f32[256,1024]{1,0:T(8,128)}, bf16[256,1024]{1,0:T(8,128)(2,1)}, bf16[2,256,1024]{2,1,0:T(8,128)(2,1)}, bf16[2,256,1024]{2,1,0:T(8,128)(2,1)}, f32[1,1024]{1,0:T(1,128)}) custom-call(s32[6]{0:T(128)} %stack.66.refs_0_, f32[256,1024]{1,0:T(8,128)} %get-tuple-element.136.refs_1_, f32[1,1024]{1,0:T(1,128)} %get-tuple-element.250.refs_4_.refs_2_, ...), custom_call_target="tpu_custom_call" | custom-call | flops 12000000000 | bytes 1000 | tf_op jit(solution)/shard_map/cross_enter/pallas_call | solution.py:59
  227.0 19.7 %cross_backward.1 = (bf16[256,1024]{1,0:T(8,128)(2,1)}, bf16[2,1024,2048]{2,1,0:T(8,128)(2,1)}) custom-call(bf16[256,1024]{1,0:T(8,128)(2,1)} %get-tuple-element.151.refs_0_, bf16[256,1024]{1,0:T(8,128)(2,1)} %get-tuple-element.157.refs_1_, bf16[256,1024]{1,0:T(8,128)(2,1)} %get-tuple-element.153.refs_7_.refs_2_, ...), custom_call_target="tpu_custom_call" | custom-call | flops 49999998976 | bytes 1000 | tf_op jit(solution)/shard_map/cross_backward/pallas_call | solution.py:59
  246.7 8.5 %causal_enter.1 = (f32[256,1024]{1,0:T(8,128)}, bf16[256,1024]{1,0:T(8,128)(2,1)}, bf16[2,256,2048]{2,1,0:T(8,128)(2,1)}, bf16[2,256,2048]{2,1,0:T(8,128)(2,1)}, f32[1,1024]{1,0:T(1,128)}) custom-call(s32[6]{0:T(128)} %stack.66.refs_0_, f32[256,1024]{1,0:T(8,128)} %get-tuple-element.159.refs_5_.refs_1_, f32[256,1024]{1,0:T(8,128)} %get-tuple-element.135.refs_1_.refs_2_, ...), custom_call_target="tpu_custom_call" | custom-call | flops 16000000000 | bytes 1000 | tf_op jit(solution)/shard_map/causal_enter/pallas_call | solution.py:59
  262.1 13.3 %causal_backward.1 = (bf16[2,256,2048]{2,1,0:T(8,128)(2,1)}, bf16[2,256,2048]{2,1,0:T(8,128)(2,1)}, f32[1,1024]{1,0:T(1,128)}, f32[16,128]{1,0:T(8,128)}, bf16[256,1024]{1,0:T(8,128)(2,1)}) custom-call(s32[6]{0:T(128)} %stack.66.refs_0_, s32[2]{0:T(128)} %refs_1_.5, f32[256,1024]{1,0:T(8,128)} %get-tuple-element.164.refs_3_.refs_2_, ...), custom_call_target="tpu_custom_call" | custom-call | flops 30000001024 | bytes 1000 | tf_op jit(solution)/shard_map/causal_backward/pallas_call | solution.py:59
  289.4 14.2 %keyval_weight_grad.1 = (bf16[2,256,1152]{2,1,0:T(8,128)(2,1)}, bf16[2,256,1152]{2,1,0:T(8,128)(2,1)}) custom-call(s32[6]{0:T(128)} %stack.66.refs_0_, bf16[2,2048,1024]{2,1,0:T(8,128)(2,1)} %refs_1_.6, bf16[2,1024,2048]{2,1,0:T(8,128)(2,1)} %get-tuple-element.160.refs_2_.refs_1_, f32[8,1024]{1,0:T(8,128)} %concatenate.110.refs_3_, ...), custom_call_target="tpu_custom_call" | custom-call | flops 30000001024 | bytes 1000 | tf_op jit(solution)/shard_map/keyval_weight_grad/pallas_call | solution.py:59
  303.8 8.4 %memory_gradient.2.refs_17_.refs_4_ = bf16[2,2048,1024]{2,1,0:T(8,128)(2,1)} custom-call(s32[6]{0:T(128)} %stack.66.refs_0_, bf16[2,1024,2048]{2,1,0:T(8,128)(2,1)} %get-tuple-element.160.refs_2_.refs_1_, bf16[16,32,1152]{2,1,0:T(8,128)(2,1)} %constant_dynamic-update-slice_fusion.4.refs_2_, bf16[16,32,1152]{2,1,0:T(8,128)(2,1)} %copy-done.32, ...), custom_call_target="tpu_custom_call" | custom-call | flops 16000000000 | bytes 1000 | tf_op jit(solution)/shard_map/memory_gradient/pallas_call | solution.py:59
  316.5 5.6 %combine.12 = (bf16[2,2,32,1408]{3,2,1,0:T(8,128)(2,1)}, bf16[88,1024]{1,0:T(8,128)(2,1)}, bf16[2,2,32,3072]{3,2,1,0:T(8,128)(2,1)}, bf16[2,2,2,32,2048]{4,3,2,1,0:T(8,128)(2,1)}, bf16[2,2,2,32,1152]{4,3,2,1,0:T(8,128)(2,1)}) custom-call(s32[6]{0:T(128)} %stack.66.refs_0_, bf16[2,2,2,2,2,32,1408]{6,5,4,3,2,1,0:T(8,128)(2,1)} %bitcast.128, ...), custom_call_target="tpu_custom_call" | custom-call | flops 6000000000 | bytes 1000 | tf_op jit(solution)/shard_map/combine/pallas_call | solution.py:59
  326.9 8.6 %memory_gradient.3.refs_15_ = bf16[2,2048,1024]{2,1,0:T(8,128)(2,1)} custom-call(s32[6]{0:T(128)} %stack.66.refs_0_, bf16[2,1024,2048]{2,1,0:T(8,128)(2,1)} %get-tuple-element.160.refs_2_.refs_1_, bf16[16,32,1152]{2,1,0:T(8,128)(2,1)} %constant_dynamic-update-slice_fusion.4.refs_2_, ...), custom_call_target="tpu_custom_call", output_to_operand_aliasing={{}: (4, {})} | custom-call | flops 16000000000 | bytes 1000 | tf_op jit(solution)/shard_map/memory_gradient/pallas_call | solution.py:59
  338.7 15.4 %collective-permute-done.43.refs_14_.refs_17_.refs_8_.refs_21_ = bf16[2,2,2,32,1152]{4,3,2,1,0:T(8,128)(2,1)S(1)} collective-permute-done((bf16[2,2,2,32,1152]{4,3,2,1,0:T(8,128)(2,1)}, bf16[2,2,2,32,1152]{4,3,2,1,0:T(8,128)(2,1)S(1)}, u32[]{:S(2)}, u32[]{:S(2)}) %collective-permute-start.43) | collective-permute-done | bytes 589856 | tf_op jit(solution)/shard_map/ppermute | solution.py:108
  356.2 4.2 %combine.13 = (bf16[2,32,3072]{2,1,0:T(8,128)(2,1)}, bf16[2,2,32,2048]{3,2,1,0:T(8,128)(2,1)}, bf16[2,2,32,1152]{3,2,1,0:T(8,128)(2,1)}) custom-call(s32[6]{0:T(128)} %stack.66.refs_0_, bf16[2,2,2,2,32,1024]{5,4,3,2,1,0:T(8,128)(2,1)} %bitcast.118, bf16[2,2,2,2,32,1024]{5,4,3,2,1,0:T(8,128)(2,1)} %bitcast.123, bf16[2,2,2,32,1024]{4,3,2,1,0:T(8,128)(2,1)} %copy-done.6, ...), custom_call_target="tpu_custom_call" | custom-call | flops 6000000000 | bytes 1000 | tf_op jit(solution)/shard_map/combine/pallas_call | solution.py:59
  374.4 3.8 combine.14
  383.9 6.8 %collective-permute-done.50.refs_5_.refs_10_.refs_17_.refs_23_ = bf16[2,32,3200]{2,1,0:T(8,128)(2,1)S(1)} collective-permute-done((bf16[2,32,3200]{2,1,0:T(8,128)(2,1)}, bf16[2,32,3200]{2,1,0:T(8,128)(2,1)S(1)}, u32[]{:S(2)}, u32[]{:S(2)}) %collective-permute-start.50) | collective-permute-done | bytes 409632 | tf_op jit(solution)/shard_map/ppermute | solution.py:108
  398.8 4.3 %collective-permute-done.51.refs_18_.refs_24_ = bf16[32,3200]{1,0:T(8,128)(2,1)S(1)} collective-permute-done((bf16[32,3200]{1,0:T(8,128)(2,1)}, bf16[32,3200]{1,0:T(8,128)(2,1)S(1)}, u32[]{:S(2)}, u32[]{:S(2)}) %collective-permute-start.51) | collective-permute-done | bytes 204832 | tf_op jit(solution)/shard_map/ppermute | solution.py:108
  403.8 3.6 finish.3
  (283 shorter events, 128.5 us)
Async XLA Ops:
  28.5 17.4 %collective-permute-start.7 = (bf16[256,1024]{1,0:T(8,128)(2,1)S(1)}, bf16[256,1024]{1,0:T(8,128)(2,1)}, u32[]{:S(2)}, u32[]{:S(2)}) collective-permute-start(bf16[256,1024]{1,0:T(8,128)(2,1)S(1)} %bitcast.158), channel_id=1, source_target_pairs={{0,8},{1,9},{2,10},{3,11},{4,12},{5,13},{6,14},{7,15},{8,0},{9,1},... | collective-permute-start | bytes 1572872 | tf_op jit(solution)/shard_map/ppermute | solution.py:108
  28.5 22.8 %collective-permute-start.8 = (bf16[256,1024]{1,0:T(8,128)(2,1)S(1)}, bf16[256,1024]{1,0:T(8,128)(2,1)}, u32[]{:S(2)}, u32[]{:S(2)}) collective-permute-start(bf16[256,1024]{1,0:T(8,128)(2,1)S(1)} %bitcast.159), channel_id=1, source_target_pairs={{0,16},{1,17},{2,18},{3,19},{4,20},{5,21},{6,22},{7,23},{8,24},{9,... | collective-permute-start | bytes 1572872 | tf_op jit(solution)/shard_map/ppermute | solution.py:108
  58.4 20.5 %collective-permute-start.15 = (bf16[4,32,2560]{2,1,0:T(8,128)(2,1)S(1)}, bf16[4,32,2560]{2,1,0:T(8,128)(2,1)S(1)}, u32[]{:S(2)}, u32[]{:S(2)}) collective-permute-start(bf16[4,32,2560]{2,1,0:T(8,128)(2,1)S(1)} %get-tuple-element.220), channel_id=1, source_target_pairs={{0,16},{1,17},{2,18},{3,19},{4,20},{5,21},{6,22},{7,23},{8,24},{9,... | collective-permute-start | bytes 1966088 | tf_op jit(solution)/shard_map/ppermute | solution.py:108
  58.6 20.3 %collective-permute-start.13 = (bf16[1,128,1408]{2,1,0:T(8,128)(2,1)S(1)}, bf16[1,128,1408]{2,1,0:T(8,128)(2,1)S(1)}, u32[]{:S(2)}, u32[]{:S(2)}) collective-permute-start(bf16[1,128,1408]{2,1,0:T(8,128)(2,1)S(1)} %fusion.4), channel_id=1, source_target_pairs={{0,4},{1,5},{2,6},{3,7},{4,0},{5,1},{6,2},{7,3},{8,12},{9,13},{10,... | collective-permute-start | bytes 1081352 | tf_op jit(solution)/shard_map/ppermute | solution.py:108
  62.2 18.0 %collective-permute-start.12 = (bf16[4,32,2560]{2,1,0:T(8,128)(2,1)S(1)}, bf16[4,32,2560]{2,1,0:T(8,128)(2,1)S(1)}, u32[]{:S(2)}, u32[]{:S(2)}) collective-permute-start(bf16[4,32,2560]{2,1,0:T(8,128)(2,1)S(1)} %get-tuple-element.219), channel_id=1, source_target_pairs={{0,1},{1,0},{2,3},{3,2},{4,5},{5,4},{6,7},{7,6},{8,9},{9,8},{10,11... | collective-permute-start | bytes 1966088 | tf_op jit(solution)/shard_map/ppermute | solution.py:108
  79.0 30.2 %collective-permute-start.16 = (bf16[8,32,2560]{2,1,0:T(8,128)(2,1)S(1)}, bf16[8,32,2560]{2,1,0:T(8,128)(2,1)S(1)}, u32[]{:S(2)}, u32[]{:S(2)}) collective-permute-start(bf16[8,32,2560]{2,1,0:T(8,128)(2,1)S(1)} %pad_maximum_fusion.2), channel_id=1, source_target_pairs={{0,1},{1,0},{2,3},{3,2},{4,5},{5,4},{6,7},{7,6},{8,9},{9,8},{10,11... | collective-permute-start | bytes 3932168 | tf_op jit(solution)/shard_map/ppermute | solution.py:108
  80.4 30.0 %collective-permute-start.14 = (bf16[8,32,2560]{2,1,0:T(8,128)(2,1)S(1)}, bf16[8,32,2560]{2,1,0:T(8,128)(2,1)S(1)}, u32[]{:S(2)}, u32[]{:S(2)}) collective-permute-start(bf16[8,32,2560]{2,1,0:T(8,128)(2,1)S(1)} %pad_maximum_fusion.1), channel_id=1, source_target_pairs={{0,16},{1,17},{2,18},{3,19},{4,20},{5,21},{6,22},{7,23},{8,24},{9,... | collective-permute-start | bytes 3932168 | tf_op jit(solution)/shard_map/ppermute | solution.py:108
  82.1 31.2 %collective-permute-start.17 = (bf16[2,128,1408]{2,1,0:T(8,128)(2,1)S(1)}, bf16[2,128,1408]{2,1,0:T(8,128)(2,1)S(1)}, u32[]{:S(2)}, u32[]{:S(2)}) collective-permute-start(bf16[2,128,1408]{2,1,0:T(8,128)(2,1)S(1)} %constant_dynamic-update-slice_fusion.9), channel_id=1, source_target_pairs={{0,2},{1,3},{2,0},{3,1},{4,6},{5,7},{6,4},{7,5},{8,10},{9,11},{10,... | collective-permute-start | bytes 2162696 | tf_op jit(solution)/shard_map/ppermute | solution.py:108
  92.4 21.1 %collective-permute-start.19 = (bf16[2,88,1024]{2,1,0:T(8,128)(2,1)S(1)}, bf16[2,88,1024]{2,1,0:T(8,128)(2,1)S(1)}, u32[]{:S(2)}, u32[]{:S(2)}) collective-permute-start(bf16[2,88,1024]{2,1,0:T(8,128)(2,1)S(1)} %pad_maximum_fusion.8), channel_id=1, source_target_pairs={{0,2},{1,3},{2,0},{3,1},{4,6},{5,7},{6,4},{7,5},{8,10},{9,11},{10,... | collective-permute-start | bytes 1081352 | tf_op jit(solution)/shard_map/ppermute | solution.py:108
  115.6 54.3 %collective-permute-start.23 = (bf16[256,1024]{1,0:T(8,128)(2,1)}, bf16[256,1024]{1,0:T(8,128)(2,1)S(1)}, u32[]{:S(2)}, u32[]{:S(2)}) collective-permute-start(bf16[256,1024]{1,0:T(8,128)(2,1)} %collective-permute-done.8.refs_3_.refs_6_), channel_id=1, source_target_pairs={{0,8},{1,9},{2,10},{3,11},{4,12},{5,13},{6,14},{7,15},{8,0},{9,1},... | collective-permute-start | bytes 1572872 | tf_op jit(solution)/shard_map/ppermute | solution.py:108
  115.6 50.5 %collective-permute-start.24 = (bf16[4,88,1024]{2,1,0:T(8,128)(2,1)S(1)}, bf16[4,88,1024]{2,1,0:T(8,128)(2,1)S(1)}, u32[]{:S(2)}, u32[]{:S(2)}) collective-permute-start(bf16[4,88,1024]{2,1,0:T(8,128)(2,1)S(1)} %constant_dynamic-update-slice_fusion.13.refs_1_), channel_id=1, source_target_pairs={{0,1},{1,0},{2,3},{3,2},{4,5},{5,4},{6,7},{7,6},{8,9},{9,8},{10,11... | collective-permute-start | bytes 2162696 | tf_op jit(solution)/shard_map/ppermute | solution.py:108
  116.4 53.6 %collective-permute-start.25 = (bf16[4,128,1408]{2,1,0:T(8,128)(2,1)S(1)}, bf16[4,128,1408]{2,1,0:T(8,128)(2,1)S(1)}, u32[]{:S(2)}, u32[]{:S(2)}) collective-permute-start(bf16[4,128,1408]{2,1,0:T(8,128)(2,1)S(1)} %constant_dynamic-update-slice_fusion.11.refs_6_), channel_id=1, source_target_pairs={{0,1},{1,0},{2,3},{3,2},{4,5},{5,4},{6,7},{7,6},{8,9},{9,8},{10,11... | collective-permute-start | bytes 4325384 | tf_op jit(solution)/shard_map/ppermute | solution.py:108
  198.7 20.8 %collective-permute-start.28 = (bf16[256,1024]{1,0:T(8,128)(2,1)S(1)}, bf16[256,1024]{1,0:T(8,128)(2,1)S(1)}, u32[]{:S(2)}, u32[]{:S(2)}) collective-permute-start(bf16[256,1024]{1,0:T(8,128)(2,1)S(1)} %add_convert_fusion.2.refs_12_), channel_id=1, source_target_pairs={{0,16},{1,17},{2,18},{3,19},{4,20},{5,21},{6,22},{7,23},{8,24},{9,... | collective-permute-start | bytes 1572872 | tf_op jit(solution)/shard_map/ppermute | solution.py:108
  216.6 59.9 %collective-permute-start.31 = (bf16[2,2,2,2,32,1408]{5,4,3,2,1,0:T(8,128)(2,1)}, bf16[2,2,2,2,32,1408]{5,4,3,2,1,0:T(8,128)(2,1)}, u32[]{:S(2)}, u32[]{:S(2)}) collective-permute-start(bf16[2,2,2,2,32,1408]{5,4,3,2,1,0:T(8,128)(2,1)} %get-tuple-element.156.refs_10_), channel_id=1, source_target_pairs={{0,1},{1,0},{2,3},{3,2},{4,5},{5,4},{6,7},{7,6},{8,9},{9,8},{10,11... | collective-permute-start | bytes 4325384 | tf_op jit(solution)/shard_map/ppermute | solution.py:108
  217.4 59.0 %collective-permute-start.32 = (bf16[2,2,88,1024]{3,2,1,0:T(8,128)(2,1)}, bf16[2,2,88,1024]{3,2,1,0:T(8,128)(2,1)S(1)}, u32[]{:S(2)}, u32[]{:S(2)}) collective-permute-start(bf16[2,2,88,1024]{3,2,1,0:T(8,128)(2,1)} %get-tuple-element.176), channel_id=1, source_target_pairs={{0,1},{1,0},{2,3},{3,2},{4,5},{5,4},{6,7},{7,6},{8,9},{9,8},{10,11... | collective-permute-start | bytes 2162696 | tf_op jit(solution)/shard_map/ppermute | solution.py:108
  226.5 28.7 %collective-permute-start.34 = (bf16[512,1024]{1,0:T(8,128)(2,1)S(1)}, bf16[512,1024]{1,0:T(8,128)(2,1)S(1)}, u32[]{:S(2)}, u32[]{:S(2)}) collective-permute-start(bf16[512,1024]{1,0:T(8,128)(2,1)S(1)} %copy-done.33), channel_id=1, source_target_pairs={{0,8},{1,9},{2,10},{3,11},{4,12},{5,13},{6,14},{7,15},{8,0},{9,1},... | collective-permute-start | bytes 3145736 | tf_op jit(solution)/shard_map/ppermute | solution.py:108
  226.5 30.5 %collective-permute-start.29 = (bf16[2,256,1024]{2,1,0:T(8,128)(2,1)}, bf16[2,256,1024]{2,1,0:T(8,128)(2,1)S(1)}, u32[]{:S(2)}, u32[]{:S(2)}) collective-permute-start(bf16[2,256,1024]{2,1,0:T(8,128)(2,1)} %get-tuple-element.169), channel_id=1, source_target_pairs={{0,8},{1,9},{2,10},{3,11},{4,12},{5,13},{6,14},{7,15},{8,0},{9,1},... | collective-permute-start | bytes 3145736 | tf_op jit(solution)/shard_map/ppermute | solution.py:108
  255.2 28.4 %collective-permute-start.30 = (bf16[2,256,2048]{2,1,0:T(8,128)(2,1)}, bf16[2,256,2048]{2,1,0:T(8,128)(2,1)S(1)}, u32[]{:S(2)}, u32[]{:S(2)}) collective-permute-start(bf16[2,256,2048]{2,1,0:T(8,128)(2,1)} %get-tuple-element.175), channel_id=1, source_target_pairs={{0,8},{1,9},{2,10},{3,11},{4,12},{5,13},{6,14},{7,15},{8,0},{9,1},... | collective-permute-start | bytes 6291464 | tf_op jit(solution)/shard_map/ppermute | solution.py:108
  256.3 27.2 %collective-permute-start.35 = (bf16[256,1024]{1,0:T(8,128)(2,1)}, bf16[256,1024]{1,0:T(8,128)(2,1)}, u32[]{:S(2)}, u32[]{:S(2)}) collective-permute-start(bf16[256,1024]{1,0:T(8,128)(2,1)} %add_convert_fusion.1), channel_id=1, source_target_pairs={{0,16},{1,17},{2,18},{3,19},{4,20},{5,21},{6,22},{7,23},{8,24},{9,... | collective-permute-start | bytes 1572872 | tf_op jit(solution)/shard_map/ppermute | solution.py:108
  260.8 22.7 %collective-permute-start.33 = (bf16[2,2,2,32,1024]{4,3,2,1,0:T(8,128)(2,1)}, bf16[2,2,2,32,1024]{4,3,2,1,0:T(8,128)(2,1)S(1)}, u32[]{:S(2)}, u32[]{:S(2)}) collective-permute-start(bf16[2,2,2,32,1024]{4,3,2,1,0:T(8,128)(2,1)} %combine.9.refs_11_), channel_id=1, source_target_pairs={{0,16},{1,17},{2,18},{3,19},{4,20},{5,21},{6,22},{7,23},{8,24},{9,... | collective-permute-start | bytes 1572872 | tf_op jit(solution)/shard_map/ppermute | solution.py:108
  280.8 31.4 %collective-permute-start.36 = (bf16[2,2,2,32,1408]{4,3,2,1,0:T(8,128)(2,1)}, bf16[2,2,2,32,1408]{4,3,2,1,0:T(8,128)(2,1)S(1)}, u32[]{:S(2)}, u32[]{:S(2)}) collective-permute-start(bf16[2,2,2,32,1408]{4,3,2,1,0:T(8,128)(2,1)} %get-tuple-element.178.refs_3_), channel_id=1, source_target_pairs={{0,2},{1,3},{2,0},{3,1},{4,6},{5,7},{6,4},{7,5},{8,10},{9,11},{10,... | collective-permute-start | bytes 2162696 | tf_op jit(solution)/shard_map/ppermute | solution.py:108
  281.4 30.9 %collective-permute-start.37 = (bf16[2,88,1024]{2,1,0:T(8,128)(2,1)}, bf16[2,88,1024]{2,1,0:T(8,128)(2,1)}, u32[]{:S(2)}, u32[]{:S(2)}) collective-permute-start(bf16[2,88,1024]{2,1,0:T(8,128)(2,1)} %get-tuple-element.184), channel_id=1, source_target_pairs={{0,2},{1,3},{2,0},{3,1},{4,6},{5,7},{6,4},{7,5},{8,10},{9,11},{10,... | collective-permute-start | bytes 1081352 | tf_op jit(solution)/shard_map/ppermute | solution.py:108
  283.5 30.9 %collective-permute-start.39 = (bf16[2,256,2048]{2,1,0:T(8,128)(2,1)}, bf16[2,256,2048]{2,1,0:T(8,128)(2,1)S(1)}, u32[]{:S(2)}, u32[]{:S(2)}) collective-permute-start(bf16[2,256,2048]{2,1,0:T(8,128)(2,1)} %get-tuple-element.186), channel_id=1, source_target_pairs={{0,8},{1,9},{2,10},{3,11},{4,12},{5,13},{6,14},{7,15},{8,0},{9,1},... | collective-permute-start | bytes 6291464 | tf_op jit(solution)/shard_map/ppermute | solution.py:108
  288.7 25.8 %collective-permute-start.38 = (bf16[2,2,2,32,2048]{4,3,2,1,0:T(8,128)(2,1)}, bf16[2,2,2,32,2048]{4,3,2,1,0:T(8,128)(2,1)S(1)}, u32[]{:S(2)}, u32[]{:S(2)}) collective-permute-start(bf16[2,2,2,32,2048]{4,3,2,1,0:T(8,128)(2,1)} %combine.11.refs_4_), channel_id=1, source_target_pairs={{0,16},{1,17},{2,18},{3,19},{4,20},{5,21},{6,22},{7,23},{8,24},{9,... | collective-permute-start | bytes 3145736 | tf_op jit(solution)/shard_map/ppermute | solution.py:108
  322.1 32.0 %collective-permute-start.41 = (bf16[2,2,32,3072]{3,2,1,0:T(8,128)(2,1)}, bf16[2,2,32,3072]{3,2,1,0:T(8,128)(2,1)S(1)}, u32[]{:S(2)}, u32[]{:S(2)}) collective-permute-start(bf16[2,2,32,3072]{3,2,1,0:T(8,128)(2,1)} %get-tuple-element.192), channel_id=1, source_target_pairs={{0,1},{1,0},{2,3},{3,2},{4,5},{5,4},{6,7},{7,6},{8,9},{9,8},{10,11... | collective-permute-start | bytes 2359304 | tf_op jit(solution)/shard_map/ppermute | solution.py:108
  322.9 31.2 %collective-permute-start.42 = (bf16[2,2,2,32,2048]{4,3,2,1,0:T(8,128)(2,1)}, bf16[2,2,2,32,2048]{4,3,2,1,0:T(8,128)(2,1)S(1)}, u32[]{:S(2)}, u32[]{:S(2)}) collective-permute-start(bf16[2,2,2,32,2048]{4,3,2,1,0:T(8,128)(2,1)} %get-tuple-element.193), channel_id=1, source_target_pairs={{0,16},{1,17},{2,18},{3,19},{4,20},{5,21},{6,22},{7,23},{8,24},{9,... | collective-permute-start | bytes 3145736 | tf_op jit(solution)/shard_map/ppermute | solution.py:108
  323.6 30.5 %collective-permute-start.43 = (bf16[2,2,2,32,1152]{4,3,2,1,0:T(8,128)(2,1)}, bf16[2,2,2,32,1152]{4,3,2,1,0:T(8,128)(2,1)S(1)}, u32[]{:S(2)}, u32[]{:S(2)}) collective-permute-start(bf16[2,2,2,32,1152]{4,3,2,1,0:T(8,128)(2,1)} %get-tuple-element.194), channel_id=1, source_target_pairs={{0,1},{1,0},{2,3},{3,2},{4,5},{5,4},{6,7},{7,6},{8,9},{9,8},{10,11... | collective-permute-start | bytes 1769480 | tf_op jit(solution)/shard_map/ppermute | solution.py:108
  324.9 38.2 %collective-permute-start.47 = (bf16[2,2,32,1408]{3,2,1,0:T(8,128)(2,1)}, bf16[2,2,32,1408]{3,2,1,0:T(8,128)(2,1)S(1)}, u32[]{:S(2)}, u32[]{:S(2)}) collective-permute-start(bf16[2,2,32,1408]{3,2,1,0:T(8,128)(2,1)} %get-tuple-element.188.refs_5_), channel_id=1, source_target_pairs={{0,4},{1,5},{2,6},{3,7},{4,0},{5,1},{6,2},{7,3},{8,12},{9,13},{10,... | collective-permute-start | bytes 1081352 | tf_op jit(solution)/shard_map/ppermute | solution.py:108
  335.5 27.6 %collective-permute-start.48 = (bf16[88,1024]{1,0:T(8,128)(2,1)S(1)}, bf16[88,1024]{1,0:T(8,128)(2,1)S(1)}, u32[]{:S(2)}, u32[]{:S(2)}) collective-permute-start(bf16[88,1024]{1,0:T(8,128)(2,1)S(1)} %copy-done.48), channel_id=1, source_target_pairs={{0,4},{1,5},{2,6},{3,7},{4,0},{5,1},{6,2},{7,3},{8,12},{9,13},{10,... | collective-permute-start | bytes 540680 | tf_op jit(solution)/shard_map/ppermute | solution.py:108
  379.7 16.8 %collective-permute-start.54 = (bf16[32,1408]{1,0:T(8,128)(2,1)S(1)}, bf16[32,1408]{1,0:T(8,128)(2,1)S(1)}, u32[]{:S(2)}, u32[]{:S(2)}) collective-permute-start(bf16[32,1408]{1,0:T(8,128)(2,1)S(1)} %get-tuple-element.228), channel_id=1, source_target_pairs={{0,24},{1,25},{2,26},{3,27},{4,28},{5,29},{6,30},{7,31},{8,16},{9,... | collective-permute-start | bytes 270344 | tf_op jit(solution)/shard_map/ppermute | solution.py:108
  379.8 16.7 %collective-permute-start.53 = (bf16[32,1408]{1,0:T(8,128)(2,1)S(1)}, bf16[32,1408]{1,0:T(8,128)(2,1)S(1)}, u32[]{:S(2)}, u32[]{:S(2)}) collective-permute-start(bf16[32,1408]{1,0:T(8,128)(2,1)S(1)} %get-tuple-element.229), channel_id=1, source_target_pairs={{0,16},{1,17},{2,18},{3,19},{4,20},{5,21},{6,22},{7,23},{8,24},{9,... | collective-permute-start | bytes 270344 | tf_op jit(solution)/shard_map/ppermute | solution.py:108
  381.7 17.1 %collective-permute-start.49 = (bf16[32,3072]{1,0:T(8,128)(2,1)}, bf16[32,3072]{1,0:T(8,128)(2,1)S(1)}, u32[]{:S(2)}, u32[]{:S(2)}) collective-permute-start(bf16[32,3072]{1,0:T(8,128)(2,1)} %get-tuple-element.200.refs_11_), channel_id=1, source_target_pairs={{0,4},{1,5},{2,6},{3,7},{4,0},{5,1},{6,2},{7,3},{8,12},{9,13},{10,... | collective-permute-start | bytes 589832 | tf_op jit(solution)/shard_map/ppermute | solution.py:108
  (74 other events, 465.8 us)

commit v4 on v3

--- a/solution.py
+++ b/solution.py
@@ -650,14 +650,16 @@
     )
 
 
-def feed_weight_grads(n3s, cots, hidden, dgate, dup, w_down, after):
+def feed_weight_grads(links, n3s, cots, hidden, dgate, dup, w_down, after):
     rows, width = n3s[0].shape
     units = hidden.shape[1]
-    tile = 256
-
-    def kernel(*refs):
+    tile = width // links.nf
+    r, d = tile // links.nd, units // links.nd
+
+    def kernel(spot, *refs):
         hid_ref, dgate_ref, dup_ref, wd_ref = refs[8:12]
-        y_ref, y_hi_ref, y_away_ref, gu_ref, gd_ref, n3t_ref, cot_all, hid_t = refs[12:]
+        y_ref, y_hi_ref, y_away_ref = refs[12:15]
+        gu_keep, gu_away, gd_keep, gd_away, n3t_ref, cot_all, hid_t, gu_ref, gd_ref = refs[15:]
 
         @pl.when(pl.program_id(0) == 0)
         def _():
@@ -666,9 +668,16 @@
         for i in range(4):
             n3t_ref[:, i * rows : (i + 1) * rows] = refs[i][...].T
         stack_rows(refs[4:8], cot_all)
-        gu_ref[:, :units] = dot(n3t_ref[...], dgate_ref[...]).astype(bf16)
-        gu_ref[:, units:] = dot(n3t_ref[...], dup_ref[...]).astype(bf16)
-        gd_ref[...] = dot(hid_t[...], cot_all[...]).astype(bf16)
+        gu_ref[:, :units] = dot(n3t_ref[...], dgate_ref[...])
+        gu_ref[:, units:] = dot(n3t_ref[...], dup_ref[...])
+        down = dot(hid_t[...], cot_all[...])
+        for place in range(links.nd):
+            gd_ref[place] = down[place * d : (place + 1) * d]
+        for ring in range(links.size):
+            for at, gu, gd in ((spot[3], gu_keep, gd_keep), (1 - spot[3], gu_away, gd_away)):
+                place = ring * 2 + at
+                gu[0, ring] = gu_ref[pl.ds(pl.multiple_of(place * r, 8), r), :].astype(bf16)
+                gd[ring] = gd_ref[place].astype(bf16)
         y = dot(hid_ref[...], wd_ref[...])
         y_ref[...] = y[:rows]
         y_away_ref[:rows] = y[rows : 2 * rows].astype(bf16)
@@ -680,17 +689,19 @@
 
     return call(
         kernel,
-        [*n3s, *cots, hidden, dgate, dup, w_down],
-        [columns(rows)] * 8 + [whole((4 * rows, units))] * 3 + [columns(units)],
+        [links.spot, *n3s, *cots, hidden, dgate, dup, w_down],
+        [smem()] + [columns(rows)] * 8 + [whole((4 * rows, units))] * 3 + [columns(units)],
         (
             struct((rows, width), f32),
             struct((rows, width), f32),
             struct((2 * rows, width), bf16),
-            struct((width, 2 * units), bf16),
-            struct((units, width), bf16),
+            *[struct((links.nf, links.size, r, 2 * units), bf16)] * 2,
+            *[struct((links.size, d, width), bf16)] * 2,
         ),
         [columns(rows)] * 2
-        + [columns(2 * rows), pl.BlockSpec((tile, 2 * units), lambda t: (t, 0)), columns(units)],
+        + [columns(2 * rows)]
+        + [pl.BlockSpec((1, links.size, r, 2 * units), lambda t: (t, 0, 0, 0))] * 2
+        + [pl.BlockSpec((links.size, d, tile), lambda t: (0, 0, t))] * 2,
         "feed_weight_grads",
         micros=12,
         after=after,
@@ -699,6 +710,8 @@
             pltpu.VMEM((tile, 4 * rows), bf16),
             pltpu.VMEM((4 * rows, tile), bf16),
             pltpu.VMEM((units, 4 * rows), bf16),
+            pltpu.VMEM((tile, 2 * units), f32),
+            pltpu.VMEM((links.nd, d, tile), f32),
         ],
     )
 
@@ -1145,8 +1158,8 @@
     dn3_got = links.send(dn3_away, "core")
     dn3_passed = (dn3_hi + dn3_got[rows:].astype(f32)).astype(bf16)
     dn3_terms = (dn3, dn3_got[:rows], links.send(dn3_passed, "hi"))
-    y, y_hi, y_away, grad_gu, grad_down = feed_weight_grads(
-        n3s, cots, hidden, dgate, dup, w_down, (dn3_passed,)
+    y, y_hi, y_away, gu_keep, gu_away, down_keep, down_away = feed_weight_grads(
+        links, n3s, cots, hidden, dgate, dup, w_down, (dn3_passed,)
     )
 
     def split(a, axes):
@@ -1164,12 +1177,15 @@
             for left, width in windows
         ]
 
-    gu_axes = ("hi", "core") + dp_axes
-    feed_sums = [
-        Sum([Leaf(split(grad_gu, gu_axes), gu_axes)], ("lo",) + back),
-        Sum([Leaf(split(grad_down, dp_axes), dp_axes)], ("lo",) + back),
-    ]
-    done = advance(links, feed_sums, (y,))
+    feed_sums = []
+    for keep, away, axes in (
+        (gu_keep, gu_away, ("hi", "core") + bits),
+        (down_keep, down_away, bits),
+    ):
+        got = links.send(away, "lo").reshape((2,) * len(axes) + away.shape[-2:])
+        keep = keep.reshape(got.shape)
+        feed_sums.append(Sum([Leaf(keep, axes), Leaf(got, axes)], back))
+    done = (y,)
     dx2, do2, keep, away, grad_gain_three = cross_enter(
         links, x2, gain_three, *dn3_terms, cot, o2, second_blocks, done
     )
@@ -1188,8 +1204,7 @@
     )
     middle_sums = halves(keep, away, hi_lo, (0, 2 * width))
     done = advance(links, feed_sums, (input_grad,))
-    done = advance(links, o1q2_sums, (*done, early_sums[0].leaves[-1].array, y_terms[2]))
-    early_sums += o1q2_sums
+    done = advance(links, o1q2_sums + early_sums, (*done, y_terms[2]))
 
     grad_table = lax.dot_general(
         grad_bias, onehot, (((1,), (1,)), ((), ())), precision=lax.Precision.HIGHEST
@@ -1204,7 +1219,8 @@
     keep, away = keyval_weight_grad(links, memory, grad_keyval, small_rows, done)
     late_sums = halves(keep, away, lo_hi, (0, KVH * PAIR + EXTRA))
     memory_grad = memory_gradient(links, grad_keyval, first_blocks, 0, None, (keep,))
-    done = advance(links, feed_sums + early_sums + middle_sums + late_sums, (memory_grad,))
+    done = advance(links, feed_sums + o1q2_sums + middle_sums + late_sums, (memory_grad,))
+    early_sums += o1q2_sums
     for b in range(1, seqs):
         memory_grad = memory_gradient(links, grad_keyval, first_blocks, b, memory_grad, done)
     done = (memory_grad,)

time: 417 us -> 406 us (0.974)
  waiting for transfers between devices: 98.7 us -> 91.7 us
    ppermute x55 -> x56, waiting for transfers between devices: 98.7 us -> 91.7 us  [send(): return lax.ppermute(tie(a, *after), AXES, self.pairs[way])]
    pallas_call x24 -> x23, Pallas kernels: 207 us -> 203 us  [call(): pl.pallas_call(body, grid_spec=spec, out_shape=out_shape, input_output_al...]
    unnamed x112 -> x110, local copies, waits for them, and re-layouts: 18.6 us -> 17.3 us
    ppermute x55 -> x56, starting transfers between devices: 57 us -> 58.2 us  [send(): return lax.ppermute(tie(a, *after), AXES, self.pairs[way])]
  transfers between devices with their start and end apart: 55 -> 56, of which waited for: 21 -> 21; matrix products, arithmetic and copies ran while one was open for 5% -> 5% of each run, Pallas kernels for 44% -> 46%
where the time goes in v4:
time: 406 us; the launch traced here: 400 us
  Pallas kernels  203 us (50%)
  waiting for transfers between devices  91.7 us (23%)
  starting transfers between devices  58.2 us (14%)
  local copies, waits for them, and re-layouts  34.5 us (8%)
  other arithmetic  8.77 us (2%)
    pallas_call x23, Pallas kernels, call(): pl.pallas_call(body, grid_spec=spec, out_shape=out_shape, input_output_al...  203 us
    ppermute x56, waiting for transfers between devices, send(): return lax.ppermute(tie(a, *after), AXES, self.pairs[way])  91.7 us
    ppermute x56, starting transfers between devices, send(): return lax.ppermute(tie(a, *after), AXES, self.pairs[way])  58.2 us
    unnamed x110, local copies, waits for them, and re-layouts  17.3 us
  transfers between devices with their start and end apart: 56, of which 21 were waited for; matrix products, arithmetic and copies ran while one was open for 5% of the time, Pallas kernels for 46%

profile of v4, /device:TPU:0, one launch (start us, length us, event | category | flops | bytes accessed | tf_op | source)
XLA Modules:
  0.0 399.9 jit_solution(16490150971163779984)
XLA Ops:
  5.7 4.1 %collective-permute-start = (bf16[1,32,1152]{2,1,0:T(8,128)(2,1)S(1)}, bf16[1,32,1152]{2,1,0:T(8,128)(2,1)S(1)}, u32[]{:S(2)}, u32[]{:S(2)}) collective-permute-start(bf16[1,32,1152]{2,1,0:T(8,128)(2,1)S(1)} %bitcast.118), channel_id=1, source_target_pairs={{0,4},{1,5},{2,6},{3,7},{4,0},{5,1},{6,2},{7,3},{8,12},{9,13},{10,... | collective-permute-start | bytes 221192 | tf_op jit(solution)/shard_map/ppermute | solution.py:108
  15.6 3.7 collective-permute-done.1
  23.3 3.6 collective-permute-done.3
  30.2 6.9 %collective-permute-done.2 = bf16[1,32,5120]{2,1,0:T(8,128)(2,1)S(1)} collective-permute-done((bf16[1,32,5120]{2,1,0:T(8,128)(2,1)S(1)}, bf16[1,32,5120]{2,1,0:T(8,128)(2,1)S(1)}, u32[]{:S(2)}, u32[]{:S(2)}) %collective-permute-start.2) | collective-permute-done | bytes 327712 | tf_op jit(solution)/shard_map/ppermute | solution.py:108
  37.2 6.1 %collective-permute-done.4 = bf16[8,32,1152]{2,1,0:T(8,128)(2,1)S(1)} collective-permute-done((bf16[8,32,1152]{2,1,0:T(8,128)(2,1)S(1)}, bf16[8,32,1152]{2,1,0:T(8,128)(2,1)S(1)}, u32[]{:S(2)}, u32[]{:S(2)}) %collective-permute-start.4) | collective-permute-done | bytes 589856 | tf_op jit(solution)/shard_map/ppermute | solution.py:108
  46.0 5.4 %collective-permute-done.8.refs_3_.refs_7_ = bf16[256,1024]{1,0:T(8,128)(2,1)} collective-permute-done((bf16[256,1024]{1,0:T(8,128)(2,1)S(1)}, bf16[256,1024]{1,0:T(8,128)(2,1)}, u32[]{:S(2)}, u32[]{:S(2)}) %collective-permute-start.8) | collective-permute-done | bytes 524320 | tf_op jit(solution)/shard_map/ppermute | solution.py:108
  58.6 3.6 collective-permute-start.13
  64.7 14.1 %project_memory.1 = (bf16[2,1024,2048]{2,1,0:T(8,128)(2,1)}, f32[8,1024]{1,0:T(8,128)}) custom-call(s32[6]{0:T(128)} %stack.66.refs_0_, bf16[2,2048,1024]{2,1,0:T(8,128)(2,1)} %refs_1_.6, bf16[16,32,1152]{2,1,0:T(8,128)(2,1)} %constant_dynamic-update-slice_fusion.4.refs_2_, bf16[16,32,1152]{2,1,0:T(8,128)(2,1)} %copy-done.30), custom_call_target="tpu_custom_call" | custom-call | flops 30000001024 | bytes 1000 | tf_op jit(solution)/shard_map/project_memory/pallas_call | solution.py:59
  82.1 3.7 collective-permute-start.17
  85.8 6.5 %collective-permute-done.18 = bf16[1,88,1024]{2,1,0:T(8,128)(2,1)S(1)} collective-permute-done((bf16[1,88,1024]{2,1,0:T(8,128)(2,1)S(1)}, bf16[1,88,1024]{2,1,0:T(8,128)(2,1)S(1)}, u32[]{:S(2)}, u32[]{:S(2)}) %collective-permute-start.18) | collective-permute-done | bytes 180256 | tf_op jit(solution)/shard_map/ppermute | solution.py:108
  92.5 16.7 %collective-permute-done.16 = bf16[8,32,2560]{2,1,0:T(8,128)(2,1)S(1)} collective-permute-done((bf16[8,32,2560]{2,1,0:T(8,128)(2,1)S(1)}, bf16[8,32,2560]{2,1,0:T(8,128)(2,1)S(1)}, u32[]{:S(2)}, u32[]{:S(2)}) %collective-permute-start.16) | collective-permute-done | bytes 1310752 | tf_op jit(solution)/shard_map/ppermute | solution.py:108
  117.8 4.9 %collective-permute-done.20.refs_6_.refs_8_.refs_9_.refs_10_ = bf16[16,32,5120]{2,1,0:T(8,128)(2,1)} collective-permute-done((bf16[16,32,5120]{2,1,0:T(8,128)(2,1)}, bf16[16,32,5120]{2,1,0:T(8,128)(2,1)}, u32[]{:S(2)}, u32[]{:S(2)}) %collective-permute-start.20) | collective-permute-done | bytes 5242912 | tf_op jit(solution)/shard_map/ppermute | solution.py:108
  122.7 8.2 %causal_forward.1 = (f32[256,1024]{1,0:T(8,128)}, bf16[256,1024]{1,0:T(8,128)(2,1)}, bf16[256,2048]{1,0:T(8,128)(2,1)}, bf16[256,1024]{1,0:T(8,128)(2,1)}) custom-call(s32[6]{0:T(128)} %stack.66.refs_0_, s32[2]{0:T(128)} %refs_1_.5, bf16[256,1024]{1,0:T(8,128)(2,1)} %bitcast.160, f32[1,1024]{1,0:T(1,128)} %get-tuple-element.256.refs_3_.refs_7_, ...), custom_call_target="tpu_custom_call" | custom-call | flops 17999998976 | bytes 1000 | tf_op jit(solution)/shard_map/causal_forward/pallas_call | solution.py:59
  131.0 33.6 %cross_forward.1 = (bf16[256,1024]{1,0:T(8,128)(2,1)}, bf16[256,1024]{1,0:T(8,128)(2,1)}, bf16[256,1024]{1,0:T(8,128)(2,1)}, f32[256,1024]{1,0:T(8,128)}, bf16[2...) custom-call(s32[6]{0:T(128)} %stack.66.refs_0_, f32[256,1024]{1,0:T(8,128)} %get-tuple-element.137.refs_1_.refs_2_, ...), custom_call_target="tpu_custom_call" | custom-call | flops 67999997952 | bytes 1000 | tf_op jit(solution)/shard_map/cross_forward/pallas_call | solution.py:59
  171.5 7.5 %feed_prepare.1 = (bf16[1024,704]{1,0:T(8,128)(2,1)}, bf16[1024,704]{1,0:T(8,128)(2,1)}, f32[1024,704]{1,0:T(8,128)}) custom-call(s32[6]{0:T(128)} %stack.66.refs_0_, bf16[256,1024]{1,0:T(8,128)(2,1)} %bitcast.155, bf16[256,1024]{1,0:T(8,128)(2,1)} %collective-permute-done.7.refs_2_.refs_6_, bf16[256,1024]{1,0:T(8,128)(2,1)} %collective-permute-done.8.refs_3_.refs_7_, ...), custom_call_target="tpu_custom_call" | custom-call | flops 12000000000 | bytes 1000 | tf_op jit(solution)/shard_map/feed_prepare/pallas_call | solution.py:59
  181.8 12.8 %feed_through.1 = (bf16[1024,704]{1,0:T(8,128)(2,1)}, bf16[1024,704]{1,0:T(8,128)(2,1)}, bf16[1024,704]{1,0:T(8,128)(2,1)}, f32[256,1024]{1,0:T(8,128)}, f32[256,1024]{1,0:T(8,128)}, /*index=5*/bf16[512,1024]{1,0:T(8,128)(2,1)}) custom-call(bf16[256,1024]{1,0:T(8,128)(2,1)} %get-tuple-element.139.refs_3_.refs_8_.refs_0_.refs_1_, ...), custom_call_target="tpu_custom_call" | custom-call | flops 28000000000 | bytes 1000 | tf_op jit(solution)/shard_map/feed_through/pallas_call | solution.py:59
  200.6 12.5 %feed_weight_grads.1 = (f32[256,1024]{1,0:T(8,128)}, f32[256,1024]{1,0:T(8,128)}, bf16[512,1024]{1,0:T(8,128)(2,1)}, bf16[4,4,32,1408]{3,2,1,0:T(8,128)(2,1)}, b...) custom-call(s32[6]{0:T(128)} %stack.66.refs_0_, ...), custom_call_target="tpu_custom_call" | custom-call | flops 24000000000 | bytes 1000 | tf_op jit(solution)/shard_map/feed_weight_grads/pallas_call | solution.py:59
  216.8 6.2 %cross_enter.1 = (f32[256,1024]{1,0:T(8,128)}, bf16[256,1024]{1,0:T(8,128)(2,1)}, bf16[2,256,1024]{2,1,0:T(8,128)(2,1)}, bf16[2,256,1024]{2,1,0:T(8,128)(2,1)}, f32[1,1024]{1,0:T(1,128)}) custom-call(s32[6]{0:T(128)} %stack.66.refs_0_, f32[256,1024]{1,0:T(8,128)} %get-tuple-element.138.refs_1_, f32[1,1024]{1,0:T(1,128)} %get-tuple-element.254.refs_4_.refs_2_, ...), custom_call_target="tpu_custom_call" | custom-call | flops 12000000000 | bytes 1000 | tf_op jit(solution)/shard_map/cross_enter/pallas_call | solution.py:59
  223.5 19.7 %cross_backward.1 = (bf16[256,1024]{1,0:T(8,128)(2,1)}, bf16[2,1024,2048]{2,1,0:T(8,128)(2,1)}) custom-call(bf16[256,1024]{1,0:T(8,128)(2,1)} %get-tuple-element.153.refs_0_, bf16[256,1024]{1,0:T(8,128)(2,1)} %get-tuple-element.156.refs_1_, bf16[256,1024]{1,0:T(8,128)(2,1)} %get-tuple-element.155.refs_7_.refs_2_, ...), custom_call_target="tpu_custom_call" | custom-call | flops 49999998976 | bytes 1000 | tf_op jit(solution)/shard_map/cross_backward/pallas_call | solution.py:59
  243.2 8.5 %causal_enter.1 = (f32[256,1024]{1,0:T(8,128)}, bf16[256,1024]{1,0:T(8,128)(2,1)}, bf16[2,256,2048]{2,1,0:T(8,128)(2,1)}, bf16[2,256,2048]{2,1,0:T(8,128)(2,1)}, f32[1,1024]{1,0:T(1,128)}) custom-call(s32[6]{0:T(128)} %stack.66.refs_0_, f32[256,1024]{1,0:T(8,128)} %get-tuple-element.158.refs_5_.refs_1_, f32[256,1024]{1,0:T(8,128)} %get-tuple-element.137.refs_1_.refs_2_, ...), custom_call_target="tpu_custom_call" | custom-call | flops 16000000000 | bytes 1000 | tf_op jit(solution)/shard_map/causal_enter/pallas_call | solution.py:59
  258.7 13.3 %causal_backward.1 = (bf16[2,256,2048]{2,1,0:T(8,128)(2,1)}, bf16[2,256,2048]{2,1,0:T(8,128)(2,1)}, f32[1,1024]{1,0:T(1,128)}, f32[16,128]{1,0:T(8,128)}, bf16[256,1024]{1,0:T(8,128)(2,1)}) custom-call(s32[6]{0:T(128)} %stack.66.refs_0_, s32[2]{0:T(128)} %refs_1_.5, f32[256,1024]{1,0:T(8,128)} %get-tuple-element.163.refs_3_.refs_2_, ...), custom_call_target="tpu_custom_call" | custom-call | flops 30000001024 | bytes 1000 | tf_op jit(solution)/shard_map/causal_backward/pallas_call | solution.py:59
  280.7 3.9 combine.9
  285.4 14.1 %keyval_weight_grad.1 = (bf16[2,256,1152]{2,1,0:T(8,128)(2,1)}, bf16[2,256,1152]{2,1,0:T(8,128)(2,1)}) custom-call(s32[6]{0:T(128)} %stack.66.refs_0_, bf16[2,2048,1024]{2,1,0:T(8,128)(2,1)} %refs_1_.6, bf16[2,1024,2048]{2,1,0:T(8,128)(2,1)} %get-tuple-element.159.refs_2_.refs_1_, f32[8,1024]{1,0:T(8,128)} %concatenate.110.refs_3_, ...), custom_call_target="tpu_custom_call" | custom-call | flops 30000001024 | bytes 1000 | tf_op jit(solution)/shard_map/keyval_weight_grad/pallas_call | solution.py:59
  299.7 8.5 %memory_gradient.2.refs_14_.refs_4_ = bf16[2,2048,1024]{2,1,0:T(8,128)(2,1)} custom-call(s32[6]{0:T(128)} %stack.66.refs_0_, bf16[2,1024,2048]{2,1,0:T(8,128)(2,1)} %get-tuple-element.159.refs_2_.refs_1_, bf16[16,32,1152]{2,1,0:T(8,128)(2,1)} %constant_dynamic-update-slice_fusion.4.refs_2_, bf16[16,32,1152]{2,1,0:T(8,128)(2,1)} %copy-done.30, ...), custom_call_target="tpu_custom_call" | custom-call | flops 16000000000 | bytes 1000 | tf_op jit(solution)/shard_map/memory_gradient/pallas_call | solution.py:59
  312.3 5.3 %combine.10 = (bf16[2,2,32,1408]{3,2,1,0:T(8,128)(2,1)}, bf16[88,1024]{1,0:T(8,128)(2,1)}, bf16[2,2,32,2048]{3,2,1,0:T(8,128)(2,1)}, bf16[2,2,2,32,2048]{4,3,2,1,0:T(8,128)(2,1)}, bf16[2,2,2,32,1152]{4,3,2,1,0:T(8,128)(2,1)}) custom-call(s32[6]{0:T(128)} %stack.66.refs_0_, bf16[2,2,2,2,32,1408]{5,4,3,2,1,0:T(8,128)(2,1)} %bitcast.126, ...), custom_call_target="tpu_custom_call" | custom-call | flops 6000000000 | bytes 1000 | tf_op jit(solution)/shard_map/combine/pallas_call | solution.py:59
  322.3 8.6 %memory_gradient.3.refs_15_ = bf16[2,2048,1024]{2,1,0:T(8,128)(2,1)} custom-call(s32[6]{0:T(128)} %stack.66.refs_0_, bf16[2,1024,2048]{2,1,0:T(8,128)(2,1)} %get-tuple-element.159.refs_2_.refs_1_, bf16[16,32,1152]{2,1,0:T(8,128)(2,1)} %constant_dynamic-update-slice_fusion.4.refs_2_, ...), custom_call_target="tpu_custom_call", output_to_operand_aliasing={{}: (4, {})} | custom-call | flops 16000000000 | bytes 1000 | tf_op jit(solution)/shard_map/memory_gradient/pallas_call | solution.py:59
  334.3 9.7 %collective-permute-done.44.refs_14_.refs_17_.refs_8_.refs_21_ = bf16[2,2,2,32,1152]{4,3,2,1,0:T(8,128)(2,1)S(1)} collective-permute-done((bf16[2,2,2,32,1152]{4,3,2,1,0:T(8,128)(2,1)}, bf16[2,2,2,32,1152]{4,3,2,1,0:T(8,128)(2,1)S(1)}, u32[]{:S(2)}, u32[]{:S(2)}) %collective-permute-start.44) | collective-permute-done | bytes 589856 | tf_op jit(solution)/shard_map/ppermute | solution.py:108
  345.8 4.1 %combine.11 = (bf16[2,32,3072]{2,1,0:T(8,128)(2,1)}, bf16[2,2,32,2048]{3,2,1,0:T(8,128)(2,1)}, bf16[2,2,32,1152]{3,2,1,0:T(8,128)(2,1)}) custom-call(s32[6]{0:T(128)} %stack.66.refs_0_, bf16[2,2,2,2,32,1024]{5,4,3,2,1,0:T(8,128)(2,1)} %bitcast.130, bf16[2,2,2,2,32,1024]{5,4,3,2,1,0:T(8,128)(2,1)} %bitcast.135, ...), custom_call_target="tpu_custom_call" | custom-call | flops 6000000000 | bytes 1000 | tf_op jit(solution)/shard_map/combine/pallas_call | solution.py:59
  363.8 3.7 combine.12
  373.3 6.7 %collective-permute-done.51.refs_5_.refs_10_.refs_17_.refs_23_ = bf16[2,32,3200]{2,1,0:T(8,128)(2,1)S(1)} collective-permute-done((bf16[2,32,3200]{2,1,0:T(8,128)(2,1)}, bf16[2,32,3200]{2,1,0:T(8,128)(2,1)S(1)}, u32[]{:S(2)}, u32[]{:S(2)}) %collective-permute-start.51) | collective-permute-done | bytes 409632 | tf_op jit(solution)/shard_map/ppermute | solution.py:108
  388.1 4.3 %collective-permute-done.52.refs_18_.refs_24_ = bf16[32,3200]{1,0:T(8,128)(2,1)S(1)} collective-permute-done((bf16[32,3200]{1,0:T(8,128)(2,1)}, bf16[32,3200]{1,0:T(8,128)(2,1)S(1)}, u32[]{:S(2)}, u32[]{:S(2)}) %collective-permute-start.52) | collective-permute-done | bytes 204832 | tf_op jit(solution)/shard_map/ppermute | solution.py:108
  393.1 3.6 finish.3
  (282 shorter events, 124.0 us)
Async XLA Ops:
  28.5 17.4 %collective-permute-start.7 = (bf16[256,1024]{1,0:T(8,128)(2,1)S(1)}, bf16[256,1024]{1,0:T(8,128)(2,1)}, u32[]{:S(2)}, u32[]{:S(2)}) collective-permute-start(bf16[256,1024]{1,0:T(8,128)(2,1)S(1)} %bitcast.158), channel_id=1, source_target_pairs={{0,8},{1,9},{2,10},{3,11},{4,12},{5,13},{6,14},{7,15},{8,0},{9,1},... | collective-permute-start | bytes 1572872 | tf_op jit(solution)/shard_map/ppermute | solution.py:108
  28.5 22.8 %collective-permute-start.8 = (bf16[256,1024]{1,0:T(8,128)(2,1)S(1)}, bf16[256,1024]{1,0:T(8,128)(2,1)}, u32[]{:S(2)}, u32[]{:S(2)}) collective-permute-start(bf16[256,1024]{1,0:T(8,128)(2,1)S(1)} %bitcast.159), channel_id=1, source_target_pairs={{0,16},{1,17},{2,18},{3,19},{4,20},{5,21},{6,22},{7,23},{8,24},{9,... | collective-permute-start | bytes 1572872 | tf_op jit(solution)/shard_map/ppermute | solution.py:108
  58.4 20.5 %collective-permute-start.15 = (bf16[4,32,2560]{2,1,0:T(8,128)(2,1)S(1)}, bf16[4,32,2560]{2,1,0:T(8,128)(2,1)S(1)}, u32[]{:S(2)}, u32[]{:S(2)}) collective-permute-start(bf16[4,32,2560]{2,1,0:T(8,128)(2,1)S(1)} %get-tuple-element.224), channel_id=1, source_target_pairs={{0,16},{1,17},{2,18},{3,19},{4,20},{5,21},{6,22},{7,23},{8,24},{9,... | collective-permute-start | bytes 1966088 | tf_op jit(solution)/shard_map/ppermute | solution.py:108
  58.6 20.3 %collective-permute-start.13 = (bf16[1,128,1408]{2,1,0:T(8,128)(2,1)S(1)}, bf16[1,128,1408]{2,1,0:T(8,128)(2,1)S(1)}, u32[]{:S(2)}, u32[]{:S(2)}) collective-permute-start(bf16[1,128,1408]{2,1,0:T(8,128)(2,1)S(1)} %fusion.4), channel_id=1, source_target_pairs={{0,4},{1,5},{2,6},{3,7},{4,0},{5,1},{6,2},{7,3},{8,12},{9,13},{10,... | collective-permute-start | bytes 1081352 | tf_op jit(solution)/shard_map/ppermute | solution.py:108
  62.2 18.0 %collective-permute-start.12 = (bf16[4,32,2560]{2,1,0:T(8,128)(2,1)S(1)}, bf16[4,32,2560]{2,1,0:T(8,128)(2,1)S(1)}, u32[]{:S(2)}, u32[]{:S(2)}) collective-permute-start(bf16[4,32,2560]{2,1,0:T(8,128)(2,1)S(1)} %get-tuple-element.223), channel_id=1, source_target_pairs={{0,1},{1,0},{2,3},{3,2},{4,5},{5,4},{6,7},{7,6},{8,9},{9,8},{10,11... | collective-permute-start | bytes 1966088 | tf_op jit(solution)/shard_map/ppermute | solution.py:108
  79.0 30.2 %collective-permute-start.16 = (bf16[8,32,2560]{2,1,0:T(8,128)(2,1)S(1)}, bf16[8,32,2560]{2,1,0:T(8,128)(2,1)S(1)}, u32[]{:S(2)}, u32[]{:S(2)}) collective-permute-start(bf16[8,32,2560]{2,1,0:T(8,128)(2,1)S(1)} %pad_maximum_fusion.2), channel_id=1, source_target_pairs={{0,1},{1,0},{2,3},{3,2},{4,5},{5,4},{6,7},{7,6},{8,9},{9,8},{10,11... | collective-permute-start | bytes 3932168 | tf_op jit(solution)/shard_map/ppermute | solution.py:108
  80.4 30.0 %collective-permute-start.14 = (bf16[8,32,2560]{2,1,0:T(8,128)(2,1)S(1)}, bf16[8,32,2560]{2,1,0:T(8,128)(2,1)S(1)}, u32[]{:S(2)}, u32[]{:S(2)}) collective-permute-start(bf16[8,32,2560]{2,1,0:T(8,128)(2,1)S(1)} %pad_maximum_fusion.1), channel_id=1, source_target_pairs={{0,16},{1,17},{2,18},{3,19},{4,20},{5,21},{6,22},{7,23},{8,24},{9,... | collective-permute-start | bytes 3932168 | tf_op jit(solution)/shard_map/ppermute | solution.py:108
  82.1 31.4 %collective-permute-start.17 = (bf16[2,128,1408]{2,1,0:T(8,128)(2,1)S(1)}, bf16[2,128,1408]{2,1,0:T(8,128)(2,1)S(1)}, u32[]{:S(2)}, u32[]{:S(2)}) collective-permute-start(bf16[2,128,1408]{2,1,0:T(8,128)(2,1)S(1)} %constant_dynamic-update-slice_fusion.9), channel_id=1, source_target_pairs={{0,2},{1,3},{2,0},{3,1},{4,6},{5,7},{6,4},{7,5},{8,10},{9,11},{10,... | collective-permute-start | bytes 2162696 | tf_op jit(solution)/shard_map/ppermute | solution.py:108
  92.4 21.2 %collective-permute-start.19 = (bf16[2,88,1024]{2,1,0:T(8,128)(2,1)S(1)}, bf16[2,88,1024]{2,1,0:T(8,128)(2,1)S(1)}, u32[]{:S(2)}, u32[]{:S(2)}) collective-permute-start(bf16[2,88,1024]{2,1,0:T(8,128)(2,1)S(1)} %pad_maximum_fusion.8), channel_id=1, source_target_pairs={{0,2},{1,3},{2,0},{3,1},{4,6},{5,7},{6,4},{7,5},{8,10},{9,11},{10,... | collective-permute-start | bytes 1081352 | tf_op jit(solution)/shard_map/ppermute | solution.py:108
  115.8 54.4 %collective-permute-start.23 = (bf16[256,1024]{1,0:T(8,128)(2,1)}, bf16[256,1024]{1,0:T(8,128)(2,1)S(1)}, u32[]{:S(2)}, u32[]{:S(2)}) collective-permute-start(bf16[256,1024]{1,0:T(8,128)(2,1)} %collective-permute-done.8.refs_3_.refs_7_), channel_id=1, source_target_pairs={{0,8},{1,9},{2,10},{3,11},{4,12},{5,13},{6,14},{7,15},{8,0},{9,1},... | collective-permute-start | bytes 1572872 | tf_op jit(solution)/shard_map/ppermute | solution.py:108
  115.8 50.6 %collective-permute-start.24 = (bf16[4,88,1024]{2,1,0:T(8,128)(2,1)S(1)}, bf16[4,88,1024]{2,1,0:T(8,128)(2,1)S(1)}, u32[]{:S(2)}, u32[]{:S(2)}) collective-permute-start(bf16[4,88,1024]{2,1,0:T(8,128)(2,1)S(1)} %constant_dynamic-update-slice_fusion.13.refs_1_), channel_id=1, source_target_pairs={{0,1},{1,0},{2,3},{3,2},{4,5},{5,4},{6,7},{7,6},{8,9},{9,8},{10,11... | collective-permute-start | bytes 2162696 | tf_op jit(solution)/shard_map/ppermute | solution.py:108
  116.6 53.6 %collective-permute-start.25 = (bf16[4,128,1408]{2,1,0:T(8,128)(2,1)S(1)}, bf16[4,128,1408]{2,1,0:T(8,128)(2,1)S(1)}, u32[]{:S(2)}, u32[]{:S(2)}) collective-permute-start(bf16[4,128,1408]{2,1,0:T(8,128)(2,1)S(1)} %constant_dynamic-update-slice_fusion.11.refs_6_), channel_id=1, source_target_pairs={{0,1},{1,0},{2,3},{3,2},{4,5},{5,4},{6,7},{7,6},{8,9},{9,8},{10,11... | collective-permute-start | bytes 4325384 | tf_op jit(solution)/shard_map/ppermute | solution.py:108
  198.9 17.1 %collective-permute-start.28 = (bf16[256,1024]{1,0:T(8,128)(2,1)S(1)}, bf16[256,1024]{1,0:T(8,128)(2,1)S(1)}, u32[]{:S(2)}, u32[]{:S(2)}) collective-permute-start(bf16[256,1024]{1,0:T(8,128)(2,1)S(1)} %add_convert_fusion.2.refs_13_), channel_id=1, source_target_pairs={{0,16},{1,17},{2,18},{3,19},{4,20},{5,21},{6,22},{7,23},{8,24},{9,... | collective-permute-start | bytes 1572872 | tf_op jit(solution)/shard_map/ppermute | solution.py:108
  213.0 60.0 %collective-permute-start.32 = (bf16[4,4,32,1408]{3,2,1,0:T(8,128)(2,1)}, bf16[4,4,32,1408]{3,2,1,0:T(8,128)(2,1)}, u32[]{:S(2)}, u32[]{:S(2)}) collective-permute-start(bf16[4,4,32,1408]{3,2,1,0:T(8,128)(2,1)} %get-tuple-element.176), channel_id=1, source_target_pairs={{0,1},{1,0},{2,3},{3,2},{4,5},{5,4},{6,7},{7,6},{8,9},{9,8},{10,11... | collective-permute-start | bytes 4325384 | tf_op jit(solution)/shard_map/ppermute | solution.py:108
  213.9 59.1 %collective-permute-start.33 = (bf16[4,88,1024]{2,1,0:T(8,128)(2,1)}, bf16[4,88,1024]{2,1,0:T(8,128)(2,1)}, u32[]{:S(2)}, u32[]{:S(2)}) collective-permute-start(bf16[4,88,1024]{2,1,0:T(8,128)(2,1)} %get-tuple-element.178), channel_id=1, source_target_pairs={{0,1},{1,0},{2,3},{3,2},{4,5},{5,4},{6,7},{7,6},{8,9},{9,8},{10,11... | collective-permute-start | bytes 2162696 | tf_op jit(solution)/shard_map/ppermute | solution.py:108
  222.9 28.8 %collective-permute-start.34 = (bf16[512,1024]{1,0:T(8,128)(2,1)S(1)}, bf16[512,1024]{1,0:T(8,128)(2,1)S(1)}, u32[]{:S(2)}, u32[]{:S(2)}) collective-permute-start(bf16[512,1024]{1,0:T(8,128)(2,1)S(1)} %copy-done.31), channel_id=1, source_target_pairs={{0,8},{1,9},{2,10},{3,11},{4,12},{5,13},{6,14},{7,15},{8,0},{9,1},... | collective-permute-start | bytes 3145736 | tf_op jit(solution)/shard_map/ppermute | solution.py:108
  223.0 30.6 %collective-permute-start.29 = (bf16[2,256,1024]{2,1,0:T(8,128)(2,1)}, bf16[2,256,1024]{2,1,0:T(8,128)(2,1)S(1)}, u32[]{:S(2)}, u32[]{:S(2)}) collective-permute-start(bf16[2,256,1024]{2,1,0:T(8,128)(2,1)} %get-tuple-element.168), channel_id=1, source_target_pairs={{0,8},{1,9},{2,10},{3,11},{4,12},{5,13},{6,14},{7,15},{8,0},{9,1},... | collective-permute-start | bytes 3145736 | tf_op jit(solution)/shard_map/ppermute | solution.py:108
  251.6 27.7 %collective-permute-start.30 = (bf16[2,256,2048]{2,1,0:T(8,128)(2,1)}, bf16[2,256,2048]{2,1,0:T(8,128)(2,1)S(1)}, u32[]{:S(2)}, u32[]{:S(2)}) collective-permute-start(bf16[2,256,2048]{2,1,0:T(8,128)(2,1)} %get-tuple-element.174), channel_id=1, source_target_pairs={{0,8},{1,9},{2,10},{3,11},{4,12},{5,13},{6,14},{7,15},{8,0},{9,1},... | collective-permute-start | bytes 6291464 | tf_op jit(solution)/shard_map/ppermute | solution.py:108
  252.8 26.5 %collective-permute-start.35 = (bf16[256,1024]{1,0:T(8,128)(2,1)}, bf16[256,1024]{1,0:T(8,128)(2,1)}, u32[]{:S(2)}, u32[]{:S(2)}) collective-permute-start(bf16[256,1024]{1,0:T(8,128)(2,1)} %add_convert_fusion.1), channel_id=1, source_target_pairs={{0,16},{1,17},{2,18},{3,19},{4,20},{5,21},{6,22},{7,23},{8,24},{9,... | collective-permute-start | bytes 1572872 | tf_op jit(solution)/shard_map/ppermute | solution.py:108
  257.4 21.8 %collective-permute-start.31 = (bf16[2,2,2,32,1024]{4,3,2,1,0:T(8,128)(2,1)}, bf16[2,2,2,32,1024]{4,3,2,1,0:T(8,128)(2,1)}, u32[]{:S(2)}, u32[]{:S(2)}) collective-permute-start(bf16[2,2,2,32,1024]{4,3,2,1,0:T(8,128)(2,1)} %combine.7.refs_11_), channel_id=1, source_target_pairs={{0,16},{1,17},{2,18},{3,19},{4,20},{5,21},{6,22},{7,23},{8,24},{9,... | collective-permute-start | bytes 1572872 | tf_op jit(solution)/shard_map/ppermute | solution.py:108
  276.6 32.4 %collective-permute-start.36 = (bf16[2,2,2,32,1408]{4,3,2,1,0:T(8,128)(2,1)}, bf16[2,2,2,32,1408]{4,3,2,1,0:T(8,128)(2,1)}, u32[]{:S(2)}, u32[]{:S(2)}) collective-permute-start(bf16[2,2,2,32,1408]{4,3,2,1,0:T(8,128)(2,1)} %get-tuple-element.180.refs_6_), channel_id=1, source_target_pairs={{0,2},{1,3},{2,0},{3,1},{4,6},{5,7},{6,4},{7,5},{8,10},{9,11},{10,... | collective-permute-start | bytes 2162696 | tf_op jit(solution)/shard_map/ppermute | solution.py:108
  277.1 31.1 %collective-permute-start.37 = (bf16[2,88,1024]{2,1,0:T(8,128)(2,1)}, bf16[2,88,1024]{2,1,0:T(8,128)(2,1)}, u32[]{:S(2)}, u32[]{:S(2)}) collective-permute-start(bf16[2,88,1024]{2,1,0:T(8,128)(2,1)} %get-tuple-element.187), channel_id=1, source_target_pairs={{0,2},{1,3},{2,0},{3,1},{4,6},{5,7},{6,4},{7,5},{8,10},{9,11},{10,... | collective-permute-start | bytes 1081352 | tf_op jit(solution)/shard_map/ppermute | solution.py:108
  279.3 31.1 %collective-permute-start.39 = (bf16[2,256,2048]{2,1,0:T(8,128)(2,1)}, bf16[2,256,2048]{2,1,0:T(8,128)(2,1)S(1)}, u32[]{:S(2)}, u32[]{:S(2)}) collective-permute-start(bf16[2,256,2048]{2,1,0:T(8,128)(2,1)} %get-tuple-element.189), channel_id=1, source_target_pairs={{0,8},{1,9},{2,10},{3,11},{4,12},{5,13},{6,14},{7,15},{8,0},{9,1},... | collective-permute-start | bytes 6291464 | tf_op jit(solution)/shard_map/ppermute | solution.py:108
  284.6 25.8 %collective-permute-start.38 = (bf16[2,2,2,32,2048]{4,3,2,1,0:T(8,128)(2,1)}, bf16[2,2,2,32,2048]{4,3,2,1,0:T(8,128)(2,1)S(1)}, u32[]{:S(2)}, u32[]{:S(2)}) collective-permute-start(bf16[2,2,2,32,2048]{4,3,2,1,0:T(8,128)(2,1)} %get-tuple-element.185.refs_4_), channel_id=1, source_target_pairs={{0,16},{1,17},{2,18},{3,19},{4,20},{5,21},{6,22},{7,23},{8,24},{9,... | collective-permute-start | bytes 3145736 | tf_op jit(solution)/shard_map/ppermute | solution.py:108
  308.2 25.0 %collective-permute-start.41 = (bf16[2,2,32,1024]{3,2,1,0:T(8,128)(2,1)S(1)}, bf16[2,2,32,1024]{3,2,1,0:T(8,128)(2,1)S(1)}, u32[]{:S(2)}, u32[]{:S(2)}) collective-permute-start(bf16[2,2,32,1024]{3,2,1,0:T(8,128)(2,1)S(1)} %copy-done.44), channel_id=1, source_target_pairs={{0,1},{1,0},{2,3},{3,2},{4,5},{5,4},{6,7},{7,6},{8,9},{9,8},{10,11... | collective-permute-start | bytes 786440 | tf_op jit(solution)/shard_map/ppermute | solution.py:108
  317.6 16.7 %collective-permute-start.42 = (bf16[2,2,32,2048]{3,2,1,0:T(8,128)(2,1)}, bf16[2,2,32,2048]{3,2,1,0:T(8,128)(2,1)S(1)}, u32[]{:S(2)}, u32[]{:S(2)}) collective-permute-start(bf16[2,2,32,2048]{3,2,1,0:T(8,128)(2,1)} %get-tuple-element.196), channel_id=1, source_target_pairs={{0,1},{1,0},{2,3},{3,2},{4,5},{5,4},{6,7},{7,6},{8,9},{9,8},{10,11... | collective-permute-start | bytes 1572872 | tf_op jit(solution)/shard_map/ppermute | solution.py:108
  318.4 25.6 %collective-permute-start.43 = (bf16[2,2,2,32,2048]{4,3,2,1,0:T(8,128)(2,1)}, bf16[2,2,2,32,2048]{4,3,2,1,0:T(8,128)(2,1)S(1)}, u32[]{:S(2)}, u32[]{:S(2)}) collective-permute-start(bf16[2,2,2,32,2048]{4,3,2,1,0:T(8,128)(2,1)} %get-tuple-element.197), channel_id=1, source_target_pairs={{0,16},{1,17},{2,18},{3,19},{4,20},{5,21},{6,22},{7,23},{8,24},{9,... | collective-permute-start | bytes 3145736 | tf_op jit(solution)/shard_map/ppermute | solution.py:108
  319.2 24.8 %collective-permute-start.44 = (bf16[2,2,2,32,1152]{4,3,2,1,0:T(8,128)(2,1)}, bf16[2,2,2,32,1152]{4,3,2,1,0:T(8,128)(2,1)S(1)}, u32[]{:S(2)}, u32[]{:S(2)}) collective-permute-start(bf16[2,2,2,32,1152]{4,3,2,1,0:T(8,128)(2,1)} %get-tuple-element.198), channel_id=1, source_target_pairs={{0,1},{1,0},{2,3},{3,2},{4,5},{5,4},{6,7},{7,6},{8,9},{9,8},{10,11... | collective-permute-start | bytes 1769480 | tf_op jit(solution)/shard_map/ppermute | solution.py:108
  320.4 32.2 %collective-permute-start.48 = (bf16[2,2,32,1408]{3,2,1,0:T(8,128)(2,1)}, bf16[2,2,32,1408]{3,2,1,0:T(8,128)(2,1)S(1)}, u32[]{:S(2)}, u32[]{:S(2)}) collective-permute-start(bf16[2,2,32,1408]{3,2,1,0:T(8,128)(2,1)} %get-tuple-element.191.refs_5_), channel_id=1, source_target_pairs={{0,4},{1,5},{2,6},{3,7},{4,0},{5,1},{6,2},{7,3},{8,12},{9,13},{10,... | collective-permute-start | bytes 1081352 | tf_op jit(solution)/shard_map/ppermute | solution.py:108
  333.2 19.4 %collective-permute-start.49 = (bf16[88,1024]{1,0:T(8,128)(2,1)S(1)}, bf16[88,1024]{1,0:T(8,128)(2,1)S(1)}, u32[]{:S(2)}, u32[]{:S(2)}) collective-permute-start(bf16[88,1024]{1,0:T(8,128)(2,1)S(1)} %copy-done.47), channel_id=1, source_target_pairs={{0,4},{1,5},{2,6},{3,7},{4,0},{5,1},{6,2},{7,3},{8,12},{9,13},{10,... | collective-permute-start | bytes 540680 | tf_op jit(solution)/shard_map/ppermute | solution.py:108
  369.1 16.7 %collective-permute-start.55 = (bf16[32,1408]{1,0:T(8,128)(2,1)S(1)}, bf16[32,1408]{1,0:T(8,128)(2,1)S(1)}, u32[]{:S(2)}, u32[]{:S(2)}) collective-permute-start(bf16[32,1408]{1,0:T(8,128)(2,1)S(1)} %get-tuple-element.232), channel_id=1, source_target_pairs={{0,24},{1,25},{2,26},{3,27},{4,28},{5,29},{6,30},{7,31},{8,16},{9,... | collective-permute-start | bytes 270344 | tf_op jit(solution)/shard_map/ppermute | solution.py:108
  371.0 17.1 %collective-permute-start.50 = (bf16[32,3072]{1,0:T(8,128)(2,1)}, bf16[32,3072]{1,0:T(8,128)(2,1)S(1)}, u32[]{:S(2)}, u32[]{:S(2)}) collective-permute-start(bf16[32,3072]{1,0:T(8,128)(2,1)} %get-tuple-element.204.refs_11_), channel_id=1, source_target_pairs={{0,4},{1,5},{2,6},{3,7},{4,0},{5,1},{6,2},{7,3},{8,12},{9,13},{10,... | collective-permute-start | bytes 589832 | tf_op jit(solution)/shard_map/ppermute | solution.py:108
  (74 other events, 516.2 us)

commit v5 on v4

--- a/solution.py
+++ b/solution.py
@@ -1219,7 +1219,8 @@
     keep, away = keyval_weight_grad(links, memory, grad_keyval, small_rows, done)
     late_sums = halves(keep, away, lo_hi, (0, KVH * PAIR + EXTRA))
     memory_grad = memory_gradient(links, grad_keyval, first_blocks, 0, None, (keep,))
-    done = advance(links, feed_sums + o1q2_sums + middle_sums + late_sums, (memory_grad,))
+    o2_got = early_sums[0].leaves[-1].array
+    done = advance(links, feed_sums + o1q2_sums + middle_sums + late_sums, (memory_grad, o2_got))
     early_sums += o1q2_sums
     for b in range(1, seqs):
         memory_grad = memory_gradient(links, grad_keyval, first_blocks, b, memory_grad, done)

time: 406 us -> 406 us (level)
  transfers between devices with their start and end apart: 56 -> 56, of which waited for: 21 -> 21; matrix products, arithmetic and copies ran while one was open for 5% -> 5% of each run, Pallas kernels for 46% -> 45%
where the time goes in v5:
time: 406 us; the launch traced here: 399 us
  Pallas kernels  203 us (50%)
  waiting for transfers between devices  91.2 us (22%)
  starting transfers between devices  57.9 us (14%)
  local copies, waits for them, and re-layouts  34.6 us (9%)
  other arithmetic  8.74 us (2%)
    pallas_call x23, Pallas kernels, call(): pl.pallas_call(body, grid_spec=spec, out_shape=out_shape, input_output_al...  203 us
    ppermute x56, waiting for transfers between devices, send(): return lax.ppermute(tie(a, *after), AXES, self.pairs[way])  91.2 us
    ppermute x56, starting transfers between devices, send(): return lax.ppermute(tie(a, *after), AXES, self.pairs[way])  57.9 us
    unnamed x110, local copies, waits for them, and re-layouts  17.4 us
  transfers between devices with their start and end apart: 56, of which 21 were waited for; matrix products, arithmetic and copies ran while one was open for 5% of the time, Pallas kernels for 45%

profile of v5, /device:TPU:0, one launch (start us, length us, event | category | flops | bytes accessed | tf_op | source)
XLA Modules:
  0.0 399.2 jit_solution(16577061139313581553)
XLA Ops:
  5.7 4.1 %collective-permute-start = (bf16[1,32,1152]{2,1,0:T(8,128)(2,1)S(1)}, bf16[1,32,1152]{2,1,0:T(8,128)(2,1)S(1)}, u32[]{:S(2)}, u32[]{:S(2)}) collective-permute-start(bf16[1,32,1152]{2,1,0:T(8,128)(2,1)S(1)} %bitcast.118), channel_id=1, source_target_pairs={{0,4},{1,5},{2,6},{3,7},{4,0},{5,1},{6,2},{7,3},{8,12},{9,13},{10,... | collective-permute-start | bytes 221192 | tf_op jit(solution)/shard_map/ppermute | solution.py:108
  15.6 3.7 collective-permute-done.1
  23.3 3.6 collective-permute-done.3
  30.2 6.9 %collective-permute-done.2 = bf16[1,32,5120]{2,1,0:T(8,128)(2,1)S(1)} collective-permute-done((bf16[1,32,5120]{2,1,0:T(8,128)(2,1)S(1)}, bf16[1,32,5120]{2,1,0:T(8,128)(2,1)S(1)}, u32[]{:S(2)}, u32[]{:S(2)}) %collective-permute-start.2) | collective-permute-done | bytes 327712 | tf_op jit(solution)/shard_map/ppermute | solution.py:108
  37.2 6.1 %collective-permute-done.4 = bf16[8,32,1152]{2,1,0:T(8,128)(2,1)S(1)} collective-permute-done((bf16[8,32,1152]{2,1,0:T(8,128)(2,1)S(1)}, bf16[8,32,1152]{2,1,0:T(8,128)(2,1)S(1)}, u32[]{:S(2)}, u32[]{:S(2)}) %collective-permute-start.4) | collective-permute-done | bytes 589856 | tf_op jit(solution)/shard_map/ppermute | solution.py:108
  46.0 5.4 %collective-permute-done.8.refs_3_.refs_7_ = bf16[256,1024]{1,0:T(8,128)(2,1)} collective-permute-done((bf16[256,1024]{1,0:T(8,128)(2,1)S(1)}, bf16[256,1024]{1,0:T(8,128)(2,1)}, u32[]{:S(2)}, u32[]{:S(2)}) %collective-permute-start.8) | collective-permute-done | bytes 524320 | tf_op jit(solution)/shard_map/ppermute | solution.py:108
  58.6 3.6 collective-permute-start.13
  64.7 14.1 %project_memory.1 = (bf16[2,1024,2048]{2,1,0:T(8,128)(2,1)}, f32[8,1024]{1,0:T(8,128)}) custom-call(s32[6]{0:T(128)} %stack.66.refs_0_, bf16[2,2048,1024]{2,1,0:T(8,128)(2,1)} %refs_1_.6, bf16[16,32,1152]{2,1,0:T(8,128)(2,1)} %constant_dynamic-update-slice_fusion.4.refs_2_, bf16[16,32,1152]{2,1,0:T(8,128)(2,1)} %copy-done.30), custom_call_target="tpu_custom_call" | custom-call | flops 30000001024 | bytes 1000 | tf_op jit(solution)/shard_map/project_memory/pallas_call | solution.py:59
  82.1 3.7 collective-permute-start.17
  85.8 6.5 %collective-permute-done.18 = bf16[1,88,1024]{2,1,0:T(8,128)(2,1)S(1)} collective-permute-done((bf16[1,88,1024]{2,1,0:T(8,128)(2,1)S(1)}, bf16[1,88,1024]{2,1,0:T(8,128)(2,1)S(1)}, u32[]{:S(2)}, u32[]{:S(2)}) %collective-permute-start.18) | collective-permute-done | bytes 180256 | tf_op jit(solution)/shard_map/ppermute | solution.py:108
  92.5 16.7 %collective-permute-done.16 = bf16[8,32,2560]{2,1,0:T(8,128)(2,1)S(1)} collective-permute-done((bf16[8,32,2560]{2,1,0:T(8,128)(2,1)S(1)}, bf16[8,32,2560]{2,1,0:T(8,128)(2,1)S(1)}, u32[]{:S(2)}, u32[]{:S(2)}) %collective-permute-start.16) | collective-permute-done | bytes 1310752 | tf_op jit(solution)/shard_map/ppermute | solution.py:108
  117.8 4.9 %collective-permute-done.20.refs_6_.refs_8_.refs_9_.refs_10_ = bf16[16,32,5120]{2,1,0:T(8,128)(2,1)} collective-permute-done((bf16[16,32,5120]{2,1,0:T(8,128)(2,1)}, bf16[16,32,5120]{2,1,0:T(8,128)(2,1)}, u32[]{:S(2)}, u32[]{:S(2)}) %collective-permute-start.20) | collective-permute-done | bytes 5242912 | tf_op jit(solution)/shard_map/ppermute | solution.py:108
  122.7 8.2 %causal_forward.1 = (f32[256,1024]{1,0:T(8,128)}, bf16[256,1024]{1,0:T(8,128)(2,1)}, bf16[256,2048]{1,0:T(8,128)(2,1)}, bf16[256,1024]{1,0:T(8,128)(2,1)}) custom-call(s32[6]{0:T(128)} %stack.66.refs_0_, s32[2]{0:T(128)} %refs_1_.5, bf16[256,1024]{1,0:T(8,128)(2,1)} %bitcast.160, f32[1,1024]{1,0:T(1,128)} %get-tuple-element.256.refs_3_.refs_7_, ...), custom_call_target="tpu_custom_call" | custom-call | flops 17999998976 | bytes 1000 | tf_op jit(solution)/shard_map/causal_forward/pallas_call | solution.py:59
  131.0 33.6 %cross_forward.1 = (bf16[256,1024]{1,0:T(8,128)(2,1)}, bf16[256,1024]{1,0:T(8,128)(2,1)}, bf16[256,1024]{1,0:T(8,128)(2,1)}, f32[256,1024]{1,0:T(8,128)}, bf16[2...) custom-call(s32[6]{0:T(128)} %stack.66.refs_0_, f32[256,1024]{1,0:T(8,128)} %get-tuple-element.137.refs_1_.refs_2_, ...), custom_call_target="tpu_custom_call" | custom-call | flops 67999997952 | bytes 1000 | tf_op jit(solution)/shard_map/cross_forward/pallas_call | solution.py:59
  171.5 7.4 %feed_prepare.1 = (bf16[1024,704]{1,0:T(8,128)(2,1)}, bf16[1024,704]{1,0:T(8,128)(2,1)}, f32[1024,704]{1,0:T(8,128)}) custom-call(s32[6]{0:T(128)} %stack.66.refs_0_, bf16[256,1024]{1,0:T(8,128)(2,1)} %bitcast.155, bf16[256,1024]{1,0:T(8,128)(2,1)} %collective-permute-done.7.refs_2_.refs_6_, bf16[256,1024]{1,0:T(8,128)(2,1)} %collective-permute-done.8.refs_3_.refs_7_, ...), custom_call_target="tpu_custom_call" | custom-call | flops 12000000000 | bytes 1000 | tf_op jit(solution)/shard_map/feed_prepare/pallas_call | solution.py:59
  181.8 12.9 %feed_through.1 = (bf16[1024,704]{1,0:T(8,128)(2,1)}, bf16[1024,704]{1,0:T(8,128)(2,1)}, bf16[1024,704]{1,0:T(8,128)(2,1)}, f32[256,1024]{1,0:T(8,128)}, f32[256,1024]{1,0:T(8,128)}, /*index=5*/bf16[512,1024]{1,0:T(8,128)(2,1)}) custom-call(bf16[256,1024]{1,0:T(8,128)(2,1)} %get-tuple-element.139.refs_3_.refs_8_.refs_0_.refs_1_, ...), custom_call_target="tpu_custom_call" | custom-call | flops 28000000000 | bytes 1000 | tf_op jit(solution)/shard_map/feed_through/pallas_call | solution.py:59
  200.7 12.5 %feed_weight_grads.1 = (f32[256,1024]{1,0:T(8,128)}, f32[256,1024]{1,0:T(8,128)}, bf16[512,1024]{1,0:T(8,128)(2,1)}, bf16[4,4,32,1408]{3,2,1,0:T(8,128)(2,1)}, b...) custom-call(s32[6]{0:T(128)} %stack.66.refs_0_, ...), custom_call_target="tpu_custom_call" | custom-call | flops 24000000000 | bytes 1000 | tf_op jit(solution)/shard_map/feed_weight_grads/pallas_call | solution.py:59
  217.0 6.2 %cross_enter.1 = (f32[256,1024]{1,0:T(8,128)}, bf16[256,1024]{1,0:T(8,128)(2,1)}, bf16[2,256,1024]{2,1,0:T(8,128)(2,1)}, bf16[2,256,1024]{2,1,0:T(8,128)(2,1)}, f32[1,1024]{1,0:T(1,128)}) custom-call(s32[6]{0:T(128)} %stack.66.refs_0_, f32[256,1024]{1,0:T(8,128)} %get-tuple-element.138.refs_1_, f32[1,1024]{1,0:T(1,128)} %get-tuple-element.254.refs_4_.refs_2_, ...), custom_call_target="tpu_custom_call" | custom-call | flops 12000000000 | bytes 1000 | tf_op jit(solution)/shard_map/cross_enter/pallas_call | solution.py:59
  223.6 19.7 %cross_backward.1 = (bf16[256,1024]{1,0:T(8,128)(2,1)}, bf16[2,1024,2048]{2,1,0:T(8,128)(2,1)}) custom-call(bf16[256,1024]{1,0:T(8,128)(2,1)} %get-tuple-element.153.refs_0_, bf16[256,1024]{1,0:T(8,128)(2,1)} %get-tuple-element.156.refs_1_, bf16[256,1024]{1,0:T(8,128)(2,1)} %get-tuple-element.155.refs_7_.refs_2_, ...), custom_call_target="tpu_custom_call" | custom-call | flops 49999998976 | bytes 1000 | tf_op jit(solution)/shard_map/cross_backward/pallas_call | solution.py:59
  243.4 8.5 %causal_enter.1 = (f32[256,1024]{1,0:T(8,128)}, bf16[256,1024]{1,0:T(8,128)(2,1)}, bf16[2,256,2048]{2,1,0:T(8,128)(2,1)}, bf16[2,256,2048]{2,1,0:T(8,128)(2,1)}, f32[1,1024]{1,0:T(1,128)}) custom-call(s32[6]{0:T(128)} %stack.66.refs_0_, f32[256,1024]{1,0:T(8,128)} %get-tuple-element.158.refs_5_.refs_1_, f32[256,1024]{1,0:T(8,128)} %get-tuple-element.137.refs_1_.refs_2_, ...), custom_call_target="tpu_custom_call" | custom-call | flops 16000000000 | bytes 1000 | tf_op jit(solution)/shard_map/causal_enter/pallas_call | solution.py:59
  258.9 13.3 %causal_backward.1 = (bf16[2,256,2048]{2,1,0:T(8,128)(2,1)}, bf16[2,256,2048]{2,1,0:T(8,128)(2,1)}, f32[1,1024]{1,0:T(1,128)}, f32[16,128]{1,0:T(8,128)}, bf16[256,1024]{1,0:T(8,128)(2,1)}) custom-call(s32[6]{0:T(128)} %stack.66.refs_0_, s32[2]{0:T(128)} %refs_1_.5, f32[256,1024]{1,0:T(8,128)} %get-tuple-element.163.refs_3_.refs_2_, ...), custom_call_target="tpu_custom_call" | custom-call | flops 30000001024 | bytes 1000 | tf_op jit(solution)/shard_map/causal_backward/pallas_call | solution.py:59
  280.9 3.9 combine.9
  285.6 14.1 %keyval_weight_grad.1 = (bf16[2,256,1152]{2,1,0:T(8,128)(2,1)}, bf16[2,256,1152]{2,1,0:T(8,128)(2,1)}) custom-call(s32[6]{0:T(128)} %stack.66.refs_0_, bf16[2,2048,1024]{2,1,0:T(8,128)(2,1)} %refs_1_.6, bf16[2,1024,2048]{2,1,0:T(8,128)(2,1)} %get-tuple-element.159.refs_2_.refs_1_, f32[8,1024]{1,0:T(8,128)} %concatenate.110.refs_3_, ...), custom_call_target="tpu_custom_call" | custom-call | flops 30000001024 | bytes 1000 | tf_op jit(solution)/shard_map/keyval_weight_grad/pallas_call | solution.py:59
  303.5 8.4 %memory_gradient.2.refs_14_.refs_4_ = bf16[2,2048,1024]{2,1,0:T(8,128)(2,1)} custom-call(s32[6]{0:T(128)} %stack.66.refs_0_, bf16[2,1024,2048]{2,1,0:T(8,128)(2,1)} %get-tuple-element.159.refs_2_.refs_1_, bf16[16,32,1152]{2,1,0:T(8,128)(2,1)} %constant_dynamic-update-slice_fusion.4.refs_2_, bf16[16,32,1152]{2,1,0:T(8,128)(2,1)} %copy-done.30, ...), custom_call_target="tpu_custom_call" | custom-call | flops 16000000000 | bytes 1000 | tf_op jit(solution)/shard_map/memory_gradient/pallas_call | solution.py:59
  314.0 5.3 %combine.10 = (bf16[2,2,32,1408]{3,2,1,0:T(8,128)(2,1)}, bf16[88,1024]{1,0:T(8,128)(2,1)}, bf16[2,2,32,2048]{3,2,1,0:T(8,128)(2,1)}, bf16[2,2,2,32,2048]{4,3,2,1,0:T(8,128)(2,1)}, bf16[2,2,2,32,1152]{4,3,2,1,0:T(8,128)(2,1)}) custom-call(s32[6]{0:T(128)} %stack.66.refs_0_, bf16[2,2,2,2,32,1408]{5,4,3,2,1,0:T(8,128)(2,1)} %bitcast.126, ...), custom_call_target="tpu_custom_call" | custom-call | flops 6000000000 | bytes 1000 | tf_op jit(solution)/shard_map/combine/pallas_call | solution.py:59
  324.0 8.6 %memory_gradient.3.refs_15_ = bf16[2,2048,1024]{2,1,0:T(8,128)(2,1)} custom-call(s32[6]{0:T(128)} %stack.66.refs_0_, bf16[2,1024,2048]{2,1,0:T(8,128)(2,1)} %get-tuple-element.159.refs_2_.refs_1_, bf16[16,32,1152]{2,1,0:T(8,128)(2,1)} %constant_dynamic-update-slice_fusion.4.refs_2_, ...), custom_call_target="tpu_custom_call", output_to_operand_aliasing={{}: (4, {})} | custom-call | flops 16000000000 | bytes 1000 | tf_op jit(solution)/shard_map/memory_gradient/pallas_call | solution.py:59
  336.0 8.8 %collective-permute-done.44.refs_14_.refs_17_.refs_8_.refs_21_ = bf16[2,2,2,32,1152]{4,3,2,1,0:T(8,128)(2,1)S(1)} collective-permute-done((bf16[2,2,2,32,1152]{4,3,2,1,0:T(8,128)(2,1)}, bf16[2,2,2,32,1152]{4,3,2,1,0:T(8,128)(2,1)S(1)}, u32[]{:S(2)}, u32[]{:S(2)}) %collective-permute-start.44) | collective-permute-done | bytes 589856 | tf_op jit(solution)/shard_map/ppermute | solution.py:108
  346.5 4.1 %combine.11 = (bf16[2,32,3072]{2,1,0:T(8,128)(2,1)}, bf16[2,2,32,2048]{3,2,1,0:T(8,128)(2,1)}, bf16[2,2,32,1152]{3,2,1,0:T(8,128)(2,1)}) custom-call(s32[6]{0:T(128)} %stack.66.refs_0_, bf16[2,2,2,2,32,1024]{5,4,3,2,1,0:T(8,128)(2,1)} %bitcast.130, bf16[2,2,2,2,32,1024]{5,4,3,2,1,0:T(8,128)(2,1)} %bitcast.135, ...), custom_call_target="tpu_custom_call" | custom-call | flops 6000000000 | bytes 1000 | tf_op jit(solution)/shard_map/combine/pallas_call | solution.py:59
  359.7 3.6 collective-permute-done.46.refs_14_.refs_4_.refs_16_
  364.1 3.7 combine.12
  373.3 4.9 %collective-permute-done.51.refs_5_.refs_10_.refs_17_.refs_23_ = bf16[2,32,3200]{2,1,0:T(8,128)(2,1)S(1)} collective-permute-done((bf16[2,32,3200]{2,1,0:T(8,128)(2,1)}, bf16[2,32,3200]{2,1,0:T(8,128)(2,1)S(1)}, u32[]{:S(2)}, u32[]{:S(2)}) %collective-permute-start.51) | collective-permute-done | bytes 409632 | tf_op jit(solution)/shard_map/ppermute | solution.py:108
  386.6 5.2 %collective-permute-done.52.refs_18_.refs_24_ = bf16[32,3200]{1,0:T(8,128)(2,1)S(1)} collective-permute-done((bf16[32,3200]{1,0:T(8,128)(2,1)}, bf16[32,3200]{1,0:T(8,128)(2,1)S(1)}, u32[]{:S(2)}, u32[]{:S(2)}) %collective-permute-start.52) | collective-permute-done | bytes 204832 | tf_op jit(solution)/shard_map/ppermute | solution.py:108
  (282 shorter events, 125.0 us)
Async XLA Ops:
  20.9 16.3 %collective-permute-start.2 = (bf16[1,32,5120]{2,1,0:T(8,128)(2,1)S(1)}, bf16[1,32,5120]{2,1,0:T(8,128)(2,1)S(1)}, u32[]{:S(2)}, u32[]{:S(2)}) collective-permute-start(bf16[1,32,5120]{2,1,0:T(8,128)(2,1)S(1)} %bitcast.122), channel_id=1, source_target_pairs={{0,4},{1,5},{2,6},{3,7},{4,0},{5,1},{6,2},{7,3},{8,12},{9,13},{10,... | collective-permute-start | bytes 983048 | tf_op jit(solution)/shard_map/ppermute | solution.py:108
  27.0 16.3 %collective-permute-start.4 = (bf16[8,32,1152]{2,1,0:T(8,128)(2,1)S(1)}, bf16[8,32,1152]{2,1,0:T(8,128)(2,1)S(1)}, u32[]{:S(2)}, u32[]{:S(2)}) collective-permute-start(bf16[8,32,1152]{2,1,0:T(8,128)(2,1)S(1)} %pad_maximum_fusion.5), channel_id=1, source_target_pairs={{0,16},{1,17},{2,18},{3,19},{4,20},{5,21},{6,22},{7,23},{8,24},{9,... | collective-permute-start | bytes 1769480 | tf_op jit(solution)/shard_map/ppermute | solution.py:108
  28.5 17.4 %collective-permute-start.7 = (bf16[256,1024]{1,0:T(8,128)(2,1)S(1)}, bf16[256,1024]{1,0:T(8,128)(2,1)}, u32[]{:S(2)}, u32[]{:S(2)}) collective-permute-start(bf16[256,1024]{1,0:T(8,128)(2,1)S(1)} %bitcast.158), channel_id=1, source_target_pairs={{0,8},{1,9},{2,10},{3,11},{4,12},{5,13},{6,14},{7,15},{8,0},{9,1},... | collective-permute-start | bytes 1572872 | tf_op jit(solution)/shard_map/ppermute | solution.py:108
  28.5 22.8 %collective-permute-start.8 = (bf16[256,1024]{1,0:T(8,128)(2,1)S(1)}, bf16[256,1024]{1,0:T(8,128)(2,1)}, u32[]{:S(2)}, u32[]{:S(2)}) collective-permute-start(bf16[256,1024]{1,0:T(8,128)(2,1)S(1)} %bitcast.159), channel_id=1, source_target_pairs={{0,16},{1,17},{2,18},{3,19},{4,20},{5,21},{6,22},{7,23},{8,24},{9,... | collective-permute-start | bytes 1572872 | tf_op jit(solution)/shard_map/ppermute | solution.py:108
  58.4 20.5 %collective-permute-start.15 = (bf16[4,32,2560]{2,1,0:T(8,128)(2,1)S(1)}, bf16[4,32,2560]{2,1,0:T(8,128)(2,1)S(1)}, u32[]{:S(2)}, u32[]{:S(2)}) collective-permute-start(bf16[4,32,2560]{2,1,0:T(8,128)(2,1)S(1)} %get-tuple-element.224), channel_id=1, source_target_pairs={{0,16},{1,17},{2,18},{3,19},{4,20},{5,21},{6,22},{7,23},{8,24},{9,... | collective-permute-start | bytes 1966088 | tf_op jit(solution)/shard_map/ppermute | solution.py:108
  58.6 20.3 %collective-permute-start.13 = (bf16[1,128,1408]{2,1,0:T(8,128)(2,1)S(1)}, bf16[1,128,1408]{2,1,0:T(8,128)(2,1)S(1)}, u32[]{:S(2)}, u32[]{:S(2)}) collective-permute-start(bf16[1,128,1408]{2,1,0:T(8,128)(2,1)S(1)} %fusion.4), channel_id=1, source_target_pairs={{0,4},{1,5},{2,6},{3,7},{4,0},{5,1},{6,2},{7,3},{8,12},{9,13},{10,... | collective-permute-start | bytes 1081352 | tf_op jit(solution)/shard_map/ppermute | solution.py:108
  62.2 18.0 %collective-permute-start.12 = (bf16[4,32,2560]{2,1,0:T(8,128)(2,1)S(1)}, bf16[4,32,2560]{2,1,0:T(8,128)(2,1)S(1)}, u32[]{:S(2)}, u32[]{:S(2)}) collective-permute-start(bf16[4,32,2560]{2,1,0:T(8,128)(2,1)S(1)} %get-tuple-element.223), channel_id=1, source_target_pairs={{0,1},{1,0},{2,3},{3,2},{4,5},{5,4},{6,7},{7,6},{8,9},{9,8},{10,11... | collective-permute-start | bytes 1966088 | tf_op jit(solution)/shard_map/ppermute | solution.py:108
  79.0 30.2 %collective-permute-start.16 = (bf16[8,32,2560]{2,1,0:T(8,128)(2,1)S(1)}, bf16[8,32,2560]{2,1,0:T(8,128)(2,1)S(1)}, u32[]{:S(2)}, u32[]{:S(2)}) collective-permute-start(bf16[8,32,2560]{2,1,0:T(8,128)(2,1)S(1)} %pad_maximum_fusion.2), channel_id=1, source_target_pairs={{0,1},{1,0},{2,3},{3,2},{4,5},{5,4},{6,7},{7,6},{8,9},{9,8},{10,11... | collective-permute-start | bytes 3932168 | tf_op jit(solution)/shard_map/ppermute | solution.py:108
  80.4 30.0 %collective-permute-start.14 = (bf16[8,32,2560]{2,1,0:T(8,128)(2,1)S(1)}, bf16[8,32,2560]{2,1,0:T(8,128)(2,1)S(1)}, u32[]{:S(2)}, u32[]{:S(2)}) collective-permute-start(bf16[8,32,2560]{2,1,0:T(8,128)(2,1)S(1)} %pad_maximum_fusion.1), channel_id=1, source_target_pairs={{0,16},{1,17},{2,18},{3,19},{4,20},{5,21},{6,22},{7,23},{8,24},{9,... | collective-permute-start | bytes 3932168 | tf_op jit(solution)/shard_map/ppermute | solution.py:108
  82.1 31.4 %collective-permute-start.17 = (bf16[2,128,1408]{2,1,0:T(8,128)(2,1)S(1)}, bf16[2,128,1408]{2,1,0:T(8,128)(2,1)S(1)}, u32[]{:S(2)}, u32[]{:S(2)}) collective-permute-start(bf16[2,128,1408]{2,1,0:T(8,128)(2,1)S(1)} %constant_dynamic-update-slice_fusion.9), channel_id=1, source_target_pairs={{0,2},{1,3},{2,0},{3,1},{4,6},{5,7},{6,4},{7,5},{8,10},{9,11},{10,... | collective-permute-start | bytes 2162696 | tf_op jit(solution)/shard_map/ppermute | solution.py:108
  92.4 21.2 %collective-permute-start.19 = (bf16[2,88,1024]{2,1,0:T(8,128)(2,1)S(1)}, bf16[2,88,1024]{2,1,0:T(8,128)(2,1)S(1)}, u32[]{:S(2)}, u32[]{:S(2)}) collective-permute-start(bf16[2,88,1024]{2,1,0:T(8,128)(2,1)S(1)} %pad_maximum_fusion.8), channel_id=1, source_target_pairs={{0,2},{1,3},{2,0},{3,1},{4,6},{5,7},{6,4},{7,5},{8,10},{9,11},{10,... | collective-permute-start | bytes 1081352 | tf_op jit(solution)/shard_map/ppermute | solution.py:108
  115.8 54.5 %collective-permute-start.23 = (bf16[256,1024]{1,0:T(8,128)(2,1)}, bf16[256,1024]{1,0:T(8,128)(2,1)S(1)}, u32[]{:S(2)}, u32[]{:S(2)}) collective-permute-start(bf16[256,1024]{1,0:T(8,128)(2,1)} %collective-permute-done.8.refs_3_.refs_7_), channel_id=1, source_target_pairs={{0,8},{1,9},{2,10},{3,11},{4,12},{5,13},{6,14},{7,15},{8,0},{9,1},... | collective-permute-start | bytes 1572872 | tf_op jit(solution)/shard_map/ppermute | solution.py:108
  115.8 50.6 %collective-permute-start.24 = (bf16[4,88,1024]{2,1,0:T(8,128)(2,1)S(1)}, bf16[4,88,1024]{2,1,0:T(8,128)(2,1)S(1)}, u32[]{:S(2)}, u32[]{:S(2)}) collective-permute-start(bf16[4,88,1024]{2,1,0:T(8,128)(2,1)S(1)} %constant_dynamic-update-slice_fusion.13.refs_1_), channel_id=1, source_target_pairs={{0,1},{1,0},{2,3},{3,2},{4,5},{5,4},{6,7},{7,6},{8,9},{9,8},{10,11... | collective-permute-start | bytes 2162696 | tf_op jit(solution)/shard_map/ppermute | solution.py:108
  116.6 53.7 %collective-permute-start.25 = (bf16[4,128,1408]{2,1,0:T(8,128)(2,1)S(1)}, bf16[4,128,1408]{2,1,0:T(8,128)(2,1)S(1)}, u32[]{:S(2)}, u32[]{:S(2)}) collective-permute-start(bf16[4,128,1408]{2,1,0:T(8,128)(2,1)S(1)} %constant_dynamic-update-slice_fusion.11.refs_6_), channel_id=1, source_target_pairs={{0,1},{1,0},{2,3},{3,2},{4,5},{5,4},{6,7},{7,6},{8,9},{9,8},{10,11... | collective-permute-start | bytes 4325384 | tf_op jit(solution)/shard_map/ppermute | solution.py:108
  199.0 17.2 %collective-permute-start.28 = (bf16[256,1024]{1,0:T(8,128)(2,1)S(1)}, bf16[256,1024]{1,0:T(8,128)(2,1)S(1)}, u32[]{:S(2)}, u32[]{:S(2)}) collective-permute-start(bf16[256,1024]{1,0:T(8,128)(2,1)S(1)} %add_convert_fusion.2.refs_13_), channel_id=1, source_target_pairs={{0,16},{1,17},{2,18},{3,19},{4,20},{5,21},{6,22},{7,23},{8,24},{9,... | collective-permute-start | bytes 1572872 | tf_op jit(solution)/shard_map/ppermute | solution.py:108
  213.2 60.0 %collective-permute-start.32 = (bf16[4,4,32,1408]{3,2,1,0:T(8,128)(2,1)}, bf16[4,4,32,1408]{3,2,1,0:T(8,128)(2,1)}, u32[]{:S(2)}, u32[]{:S(2)}) collective-permute-start(bf16[4,4,32,1408]{3,2,1,0:T(8,128)(2,1)} %get-tuple-element.176), channel_id=1, source_target_pairs={{0,1},{1,0},{2,3},{3,2},{4,5},{5,4},{6,7},{7,6},{8,9},{9,8},{10,11... | collective-permute-start | bytes 4325384 | tf_op jit(solution)/shard_map/ppermute | solution.py:108
  214.1 59.1 %collective-permute-start.33 = (bf16[4,88,1024]{2,1,0:T(8,128)(2,1)}, bf16[4,88,1024]{2,1,0:T(8,128)(2,1)}, u32[]{:S(2)}, u32[]{:S(2)}) collective-permute-start(bf16[4,88,1024]{2,1,0:T(8,128)(2,1)} %get-tuple-element.178), channel_id=1, source_target_pairs={{0,1},{1,0},{2,3},{3,2},{4,5},{5,4},{6,7},{7,6},{8,9},{9,8},{10,11... | collective-permute-start | bytes 2162696 | tf_op jit(solution)/shard_map/ppermute | solution.py:108
  223.1 28.8 %collective-permute-start.34 = (bf16[512,1024]{1,0:T(8,128)(2,1)S(1)}, bf16[512,1024]{1,0:T(8,128)(2,1)S(1)}, u32[]{:S(2)}, u32[]{:S(2)}) collective-permute-start(bf16[512,1024]{1,0:T(8,128)(2,1)S(1)} %copy-done.31), channel_id=1, source_target_pairs={{0,8},{1,9},{2,10},{3,11},{4,12},{5,13},{6,14},{7,15},{8,0},{9,1},... | collective-permute-start | bytes 3145736 | tf_op jit(solution)/shard_map/ppermute | solution.py:108
  223.1 30.6 %collective-permute-start.29 = (bf16[2,256,1024]{2,1,0:T(8,128)(2,1)}, bf16[2,256,1024]{2,1,0:T(8,128)(2,1)S(1)}, u32[]{:S(2)}, u32[]{:S(2)}) collective-permute-start(bf16[2,256,1024]{2,1,0:T(8,128)(2,1)} %get-tuple-element.168), channel_id=1, source_target_pairs={{0,8},{1,9},{2,10},{3,11},{4,12},{5,13},{6,14},{7,15},{8,0},{9,1},... | collective-permute-start | bytes 3145736 | tf_op jit(solution)/shard_map/ppermute | solution.py:108
  251.8 27.7 %collective-permute-start.30 = (bf16[2,256,2048]{2,1,0:T(8,128)(2,1)}, bf16[2,256,2048]{2,1,0:T(8,128)(2,1)S(1)}, u32[]{:S(2)}, u32[]{:S(2)}) collective-permute-start(bf16[2,256,2048]{2,1,0:T(8,128)(2,1)} %get-tuple-element.174), channel_id=1, source_target_pairs={{0,8},{1,9},{2,10},{3,11},{4,12},{5,13},{6,14},{7,15},{8,0},{9,1},... | collective-permute-start | bytes 6291464 | tf_op jit(solution)/shard_map/ppermute | solution.py:108
  253.0 26.5 %collective-permute-start.35 = (bf16[256,1024]{1,0:T(8,128)(2,1)}, bf16[256,1024]{1,0:T(8,128)(2,1)}, u32[]{:S(2)}, u32[]{:S(2)}) collective-permute-start(bf16[256,1024]{1,0:T(8,128)(2,1)} %add_convert_fusion.1), channel_id=1, source_target_pairs={{0,16},{1,17},{2,18},{3,19},{4,20},{5,21},{6,22},{7,23},{8,24},{9,... | collective-permute-start | bytes 1572872 | tf_op jit(solution)/shard_map/ppermute | solution.py:108
  257.6 21.8 %collective-permute-start.31 = (bf16[2,2,2,32,1024]{4,3,2,1,0:T(8,128)(2,1)}, bf16[2,2,2,32,1024]{4,3,2,1,0:T(8,128)(2,1)}, u32[]{:S(2)}, u32[]{:S(2)}) collective-permute-start(bf16[2,2,2,32,1024]{4,3,2,1,0:T(8,128)(2,1)} %combine.7.refs_11_), channel_id=1, source_target_pairs={{0,16},{1,17},{2,18},{3,19},{4,20},{5,21},{6,22},{7,23},{8,24},{9,... | collective-permute-start | bytes 1572872 | tf_op jit(solution)/shard_map/ppermute | solution.py:108
  276.8 35.2 %collective-permute-start.36 = (bf16[2,2,2,32,1408]{4,3,2,1,0:T(8,128)(2,1)}, bf16[2,2,2,32,1408]{4,3,2,1,0:T(8,128)(2,1)}, u32[]{:S(2)}, u32[]{:S(2)}) collective-permute-start(bf16[2,2,2,32,1408]{4,3,2,1,0:T(8,128)(2,1)} %get-tuple-element.180.refs_6_), channel_id=1, source_target_pairs={{0,2},{1,3},{2,0},{3,1},{4,6},{5,7},{6,4},{7,5},{8,10},{9,11},{10,... | collective-permute-start | bytes 2162696 | tf_op jit(solution)/shard_map/ppermute | solution.py:108
  277.3 25.5 %collective-permute-start.37 = (bf16[2,88,1024]{2,1,0:T(8,128)(2,1)}, bf16[2,88,1024]{2,1,0:T(8,128)(2,1)}, u32[]{:S(2)}, u32[]{:S(2)}) collective-permute-start(bf16[2,88,1024]{2,1,0:T(8,128)(2,1)} %get-tuple-element.187), channel_id=1, source_target_pairs={{0,2},{1,3},{2,0},{3,1},{4,6},{5,7},{6,4},{7,5},{8,10},{9,11},{10,... | collective-permute-start | bytes 1081352 | tf_op jit(solution)/shard_map/ppermute | solution.py:108
  279.5 32.6 %collective-permute-start.39 = (bf16[2,256,2048]{2,1,0:T(8,128)(2,1)}, bf16[2,256,2048]{2,1,0:T(8,128)(2,1)S(1)}, u32[]{:S(2)}, u32[]{:S(2)}) collective-permute-start(bf16[2,256,2048]{2,1,0:T(8,128)(2,1)} %get-tuple-element.189), channel_id=1, source_target_pairs={{0,8},{1,9},{2,10},{3,11},{4,12},{5,13},{6,14},{7,15},{8,0},{9,1},... | collective-permute-start | bytes 6291464 | tf_op jit(solution)/shard_map/ppermute | solution.py:108
  284.7 27.3 %collective-permute-start.38 = (bf16[2,2,2,32,2048]{4,3,2,1,0:T(8,128)(2,1)}, bf16[2,2,2,32,2048]{4,3,2,1,0:T(8,128)(2,1)S(1)}, u32[]{:S(2)}, u32[]{:S(2)}) collective-permute-start(bf16[2,2,2,32,2048]{4,3,2,1,0:T(8,128)(2,1)} %get-tuple-element.185.refs_4_), channel_id=1, source_target_pairs={{0,16},{1,17},{2,18},{3,19},{4,20},{5,21},{6,22},{7,23},{8,24},{9,... | collective-permute-start | bytes 3145736 | tf_op jit(solution)/shard_map/ppermute | solution.py:108
  319.3 16.7 %collective-permute-start.42 = (bf16[2,2,32,2048]{3,2,1,0:T(8,128)(2,1)}, bf16[2,2,32,2048]{3,2,1,0:T(8,128)(2,1)S(1)}, u32[]{:S(2)}, u32[]{:S(2)}) collective-permute-start(bf16[2,2,32,2048]{3,2,1,0:T(8,128)(2,1)} %get-tuple-element.196), channel_id=1, source_target_pairs={{0,1},{1,0},{2,3},{3,2},{4,5},{5,4},{6,7},{7,6},{8,9},{9,8},{10,11... | collective-permute-start | bytes 1572872 | tf_op jit(solution)/shard_map/ppermute | solution.py:108
  320.5 24.2 %collective-permute-start.43 = (bf16[2,2,2,32,2048]{4,3,2,1,0:T(8,128)(2,1)}, bf16[2,2,2,32,2048]{4,3,2,1,0:T(8,128)(2,1)S(1)}, u32[]{:S(2)}, u32[]{:S(2)}) collective-permute-start(bf16[2,2,2,32,2048]{4,3,2,1,0:T(8,128)(2,1)} %get-tuple-element.197), channel_id=1, source_target_pairs={{0,16},{1,17},{2,18},{3,19},{4,20},{5,21},{6,22},{7,23},{8,24},{9,... | collective-permute-start | bytes 3145736 | tf_op jit(solution)/shard_map/ppermute | solution.py:108
  321.3 23.4 %collective-permute-start.44 = (bf16[2,2,2,32,1152]{4,3,2,1,0:T(8,128)(2,1)}, bf16[2,2,2,32,1152]{4,3,2,1,0:T(8,128)(2,1)S(1)}, u32[]{:S(2)}, u32[]{:S(2)}) collective-permute-start(bf16[2,2,2,32,1152]{4,3,2,1,0:T(8,128)(2,1)} %get-tuple-element.198), channel_id=1, source_target_pairs={{0,1},{1,0},{2,3},{3,2},{4,5},{5,4},{6,7},{7,6},{8,9},{9,8},{10,11... | collective-permute-start | bytes 1769480 | tf_op jit(solution)/shard_map/ppermute | solution.py:108
  322.1 31.0 %collective-permute-start.48 = (bf16[2,2,32,1408]{3,2,1,0:T(8,128)(2,1)}, bf16[2,2,32,1408]{3,2,1,0:T(8,128)(2,1)S(1)}, u32[]{:S(2)}, u32[]{:S(2)}) collective-permute-start(bf16[2,2,32,1408]{3,2,1,0:T(8,128)(2,1)} %get-tuple-element.192.refs_5_), channel_id=1, source_target_pairs={{0,4},{1,5},{2,6},{3,7},{4,0},{5,1},{6,2},{7,3},{8,12},{9,13},{10,... | collective-permute-start | bytes 1081352 | tf_op jit(solution)/shard_map/ppermute | solution.py:108
  332.7 20.5 %collective-permute-start.49 = (bf16[88,1024]{1,0:T(8,128)(2,1)S(1)}, bf16[88,1024]{1,0:T(8,128)(2,1)S(1)}, u32[]{:S(2)}, u32[]{:S(2)}) collective-permute-start(bf16[88,1024]{1,0:T(8,128)(2,1)S(1)} %copy-done.47), channel_id=1, source_target_pairs={{0,4},{1,5},{2,6},{3,7},{4,0},{5,1},{6,2},{7,3},{8,12},{9,13},{10,... | collective-permute-start | bytes 540680 | tf_op jit(solution)/shard_map/ppermute | solution.py:108
  370.8 15.8 %collective-permute-start.50 = (bf16[32,3072]{1,0:T(8,128)(2,1)}, bf16[32,3072]{1,0:T(8,128)(2,1)S(1)}, u32[]{:S(2)}, u32[]{:S(2)}) collective-permute-start(bf16[32,3072]{1,0:T(8,128)(2,1)} %get-tuple-element.204.refs_11_), channel_id=1, source_target_pairs={{0,4},{1,5},{2,6},{3,7},{4,0},{5,1},{6,2},{7,3},{8,12},{9,13},{10,... | collective-permute-start | bytes 589832 | tf_op jit(solution)/shard_map/ppermute | solution.py:108
  (74 other events, 514.7 us)
